TPU v7x, 32 devices: a whole 2x2x4 slice. The times are simulated.
32 devices in a mesh: dp: 4 (over y, x), fsdp: 8 (over z, core).
Axes of the slice: x: 2, y: 2, z: 4, core: 2. Of those that a mesh axis runs over, the one named last changes fastest.
Arguments:
- tokens: bfloat16 [32, 512, 768], P(('dp', 'fsdp')), may hold values from -6 to 6
- segments: int32 [32, 512], P(('dp', 'fsdp')), may hold values from 0 to 3, never falling along the last dimension, each value on 1 to 256 neighbouring positions
- cotangent: bfloat16 [32, 512, 768], P(('dp', 'fsdp')), may hold values from -6 to 6
- joint_weight: float32 [2, 768, 2304], P(None, 'fsdp'), may hold values from -0.21875 to 0.21875
- output_weight: float32 [2, 768, 768], P(None, 'fsdp'), may hold values from -0.875 to 0.875
- expand_weight: float32 [2, 768, 3072], P(None, 'fsdp'), may hold values from -0.21875 to 0.21875
- shrink_weight: float32 [2, 3072, 768], P(None, 'fsdp'), may hold values from -0.109375 to 0.109375
- norm_gains: float32 [2, 2, 768], P(None, None, 'fsdp'), may hold values from 0.5 to 1.5
- biases: float32 [2, 6, 768], P(None, None, 'fsdp'), may hold values from -1.25 to 1.25
- hidden_bias: float32 [2, 3072], P(None, 'fsdp'), may hold values from -1.25 to 1.25
- joint_rows: float32 [2, 768], P(None, 'fsdp'), may hold values from 0.14 to 2.9
- joint_columns: float32 [2, 2304], replicated, may hold values from 0.2 to 0.8
- output_rows: float32 [2, 768], P(None, 'fsdp'), may hold values from 0.014 to 0.29
- output_columns: float32 [2, 768], replicated, may hold values from 0.02 to 0.08
- expand_rows: float32 [2, 768], P(None, 'fsdp'), may hold values from 0.07 to 1.42
- expand_columns: float32 [2, 3072], replicated, may hold values from 0.1 to 0.4
- shrink_rows: float32 [2, 3072], P(None, 'fsdp'), may hold values from 0.21 to 4.3
- shrink_columns: float32 [2, 768], replicated, may hold values from 0.3 to 1.2
- gain_moments: float32 [2, 2, 768], P(None, None, 'fsdp'), may hold values from 0.7 to 14.2
- bias_moments: float32 [2, 6, 768], P(None, None, 'fsdp'), may hold values from 0.14 to 2.9
- hidden_moments: float32 [2, 3072], P(None, 'fsdp'), may hold values from 0.07 to 1.42
Outputs:
- activations: bfloat16 [32, 512, 768], P(('dp', 'fsdp'))
- input_gradient: bfloat16 [32, 512, 768], P(('dp', 'fsdp'))
- joint_gradient: float32 [2, 768, 2304], P(None, 'fsdp')
- output_gradient: float32 [2, 768, 768], P(None, 'fsdp')
- expand_gradient: float32 [2, 768, 3072], P(None, 'fsdp')
- shrink_gradient: float32 [2, 3072, 768], P(None, 'fsdp')
- gain_gradient: float32 [2, 2, 768], P(None, None, 'fsdp')
- bias_gradient: float32 [2, 6, 768], P(None, None, 'fsdp')
- hidden_gradient: float32 [2, 3072], P(None, 'fsdp')
- joint_next: float32 [2, 768, 2304], P(None, 'fsdp')
- output_next: float32 [2, 768, 768], P(None, 'fsdp')
- expand_next: float32 [2, 768, 3072], P(None, 'fsdp')
- shrink_next: float32 [2, 3072, 768], P(None, 'fsdp')
- gains_next: float32 [2, 2, 768], P(None, None, 'fsdp')
- biases_next: float32 [2, 6, 768], P(None, None, 'fsdp')
- hidden_bias_next: float32 [2, 3072], P(None, 'fsdp')
- joint_copy: bfloat16 [2, 768, 2304], P(None, 'fsdp')
- output_copy: bfloat16 [2, 768, 768], P(None, 'fsdp')
- expand_copy: bfloat16 [2, 768, 3072], P(None, 'fsdp')
- shrink_copy: bfloat16 [2, 3072, 768], P(None, 'fsdp')
- joint_rows_next: float32 [2, 768], P(None, 'fsdp')
- joint_columns_next: float32 [2, 2304], replicated
- output_rows_next: float32 [2, 768], P(None, 'fsdp')
- output_columns_next: float32 [2, 768], replicated
- expand_rows_next: float32 [2, 768], P(None, 'fsdp')
- expand_columns_next: float32 [2, 3072], replicated
- shrink_rows_next: float32 [2, 3072], P(None, 'fsdp')
- shrink_columns_next: float32 [2, 768], replicated
- gain_moments_next: float32 [2, 2, 768], P(None, None, 'fsdp')
- bias_moments_next: float32 [2, 6, 768], P(None, None, 'fsdp')
- hidden_moments_next: float32 [2, 3072], P(None, 'fsdp')
Inputs may be any that keep to these rules, and one draw needn't show every extreme that they name: `segments`: within each row of 512 slots the page numbers never fall, and each page takes 1 to 256 consecutive slots.
All inputs are finite; a program needn't handle non-finite values.
Results may differ from a plain program's by a relative error of at most 0.022.
Values may be sent and summed in bfloat16 or wider, within the bound.
A program may use at most 256 MiB of HBM per device.

v0:
```python
from functools import partial
import math

import jax
import jax.numpy as jnp
from jax import lax
from jax.sharding import PartitionSpec as P

HEADS = 12
HEAD_SIZE = 64


NORM_EPSILON = 1e-12
SCORE_SCALE = 0.125
MASK_VALUE = -1e30
FLOOR_SQUARE = 1e-30
FLOOR_SCALE = 0.001
DECAY_RATE = 0.5
CLIP_LIMIT = 0.25
STEP_RATE = 4.0


def product(left, right):
    return jnp.dot(left, right, preferred_element_type=jnp.float32)


def product_left(left, right):
    return lax.dot_general(
        left, right, (((0,), (0,)), ((), ())), preferred_element_type=jnp.float32
    )


def product_right(left, right):
    return lax.dot_general(
        left, right, (((1,), (1,)), ((), ())), preferred_element_type=jnp.float32
    )


def normalize(values):
    average = jnp.mean(values, axis=-1, keepdims=True)
    centered = values - average
    variance = jnp.mean(centered * centered, axis=-1, keepdims=True)
    inverse = lax.rsqrt(variance + NORM_EPSILON)
    return (centered * inverse, inverse)


def normalize_back(grad_scaled, scaled, inverse):
    first_mean = jnp.mean(grad_scaled, axis=-1, keepdims=True)
    second_mean = jnp.mean(grad_scaled * scaled, axis=-1, keepdims=True)
    return inverse * (grad_scaled - first_mean - scaled * second_mean)


def split_heads(joint_row):
    slot_count = joint_row.shape[0]
    shaped = joint_row.reshape(slot_count, 3, HEADS, HEAD_SIZE)
    return (shaped[:, 0], shaped[:, 1], shaped[:, 2])


def masked_scores(query_rows, key_rows, segment_row):
    scores = (
        jnp.einsum("qhe,khe->hqk", query_rows, key_rows, preferred_element_type=jnp.float32)
        * SCORE_SCALE
    )
    allowed = segment_row[:, None] == segment_row[None, :]
    return jnp.where(allowed[None], scores, MASK_VALUE)


def attend_forward(packed):
    joint_row, segment_row = packed
    query_rows, key_rows, value_rows = split_heads(joint_row)
    scores = masked_scores(query_rows, key_rows, segment_row)
    highest = jnp.max(scores, axis=-1, keepdims=True)
    raised = jnp.exp(scores - highest)
    denominator = jnp.sum(raised, axis=-1, keepdims=True)
    weights = (raised / denominator).astype(jnp.bfloat16)
    context = jnp.einsum("hqk,khe->qhe", weights, value_rows, preferred_element_type=jnp.float32)
    logsum = (highest + jnp.log(denominator))[:, :, 0]
    return (context.astype(jnp.bfloat16).reshape(joint_row.shape[0], HEADS * HEAD_SIZE), logsum)


def attend_backward(packed):
    joint_row, segment_row, logsum, grad_row = packed
    slot_count = joint_row.shape[0]
    query_rows, key_rows, value_rows = split_heads(joint_row)
    scores = masked_scores(query_rows, key_rows, segment_row)
    probabilities = jnp.exp(scores - logsum[:, :, None])
    upstream = grad_row.reshape(slot_count, HEADS, HEAD_SIZE)
    grad_probs = jnp.einsum(
        "qhe,khe->hqk", upstream, value_rows, preferred_element_type=jnp.float32
    )
    row_delta = jnp.sum(probabilities * grad_probs, axis=-1, keepdims=True)
    grad_scores = (probabilities * (grad_probs - row_delta)).astype(jnp.bfloat16)
    grad_query = (
        jnp.einsum("hqk,khe->qhe", grad_scores, key_rows, preferred_element_type=jnp.float32)
        * SCORE_SCALE
    )
    grad_key = (
        jnp.einsum("hqk,qhe->khe", grad_scores, query_rows, preferred_element_type=jnp.float32)
        * SCORE_SCALE
    )
    grad_value = jnp.einsum(
        "hqk,qhe->khe",
        probabilities.astype(jnp.bfloat16),
        upstream,
        preferred_element_type=jnp.float32,
    )
    stacked = jnp.stack([grad_query, grad_key, grad_value], axis=1)
    return stacked.reshape(slot_count, 3 * HEADS * HEAD_SIZE).astype(jnp.bfloat16)


def block_forward(hidden_in, segments, weights):
    joint_matrix, output_matrix, expand_matrix, shrink_matrix, gain_rows, bias_rows, inner_bias = (
        weights
    )
    gain_values = gain_rows.astype(jnp.float32)
    bias_values = bias_rows.astype(jnp.float32)
    row_count, slot_count = segments.shape
    zero_block = jnp.zeros_like(bias_values[0])
    joint_bias = jnp.concatenate([bias_values[0], zero_block, bias_values[1]])
    joint_out = (product(hidden_in.astype(jnp.bfloat16), joint_matrix) + joint_bias).astype(
        jnp.bfloat16
    )
    context, logsum = lax.map(
        attend_forward, (joint_out.reshape(row_count, slot_count, -1), segments)
    )
    context = context.reshape(row_count * slot_count, -1)
    attended = product(context, output_matrix) + bias_values[2]
    first_scaled, first_inverse = normalize(hidden_in + attended)
    first_norm = first_scaled * gain_values[0] + bias_values[3]
    pre_active = product(first_norm.astype(jnp.bfloat16), expand_matrix) + inner_bias.astype(
        jnp.float32
    )
    active = jax.nn.gelu(pre_active, approximate=False).astype(jnp.bfloat16)
    branch = product(active, shrink_matrix) + bias_values[4]
    second_scaled, second_inverse = normalize(first_norm + branch)
    result = second_scaled * gain_values[1] + bias_values[5]
    stored = (
        hidden_in,
        joint_out,
        context,
        logsum,
        first_scaled,
        first_inverse,
        pre_active,
        second_scaled,
        second_inverse,
    )
    return (result, stored)


def block_backward(grad_out, segments, weights, stored):
    joint_matrix, output_matrix, expand_matrix, shrink_matrix, gain_rows, bias_rows, inner_bias = (
        weights
    )
    (
        hidden_in,
        joint_out,
        context,
        logsum,
        first_scaled,
        first_inverse,
        pre_active,
        second_scaled,
        second_inverse,
    ) = stored
    gain_values = gain_rows.astype(jnp.float32)
    bias_values = bias_rows.astype(jnp.float32)
    row_count, slot_count = segments.shape
    features = hidden_in.shape[1]
    grad_second_bias = jnp.sum(grad_out, axis=0)
    grad_second_gain = jnp.sum(grad_out * second_scaled, axis=0)
    grad_sum = normalize_back(grad_out * gain_values[1], second_scaled, second_inverse)
    grad_branch = grad_sum.astype(jnp.bfloat16)
    active, gelu_back = jax.vjp(partial(jax.nn.gelu, approximate=False), pre_active)
    grad_shrink = product_left(active.astype(jnp.bfloat16), grad_branch)
    grad_active = product_right(grad_branch, shrink_matrix)
    grad_pre = gelu_back(grad_active)[0].astype(jnp.bfloat16)
    first_norm = first_scaled * gain_values[0] + bias_values[3]
    grad_expand = product_left(first_norm.astype(jnp.bfloat16), grad_pre)
    grad_first = grad_sum + product_right(grad_pre, expand_matrix)
    grad_first_bias = jnp.sum(grad_first, axis=0)
    grad_first_gain = jnp.sum(grad_first * first_scaled, axis=0)
    grad_middle = normalize_back(grad_first * gain_values[0], first_scaled, first_inverse)
    grad_attended = grad_middle.astype(jnp.bfloat16)
    grad_output = product_left(context, grad_attended)
    grad_context = product_right(grad_attended, output_matrix).astype(jnp.bfloat16)
    grad_joint_out = lax.map(
        attend_backward,
        (
            joint_out.reshape(row_count, slot_count, -1),
            segments,
            logsum,
            grad_context.reshape(row_count, slot_count, -1),
        ),
    )
    grad_joint_out = grad_joint_out.reshape(row_count * slot_count, -1)
    grad_joint = product_left(hidden_in.astype(jnp.bfloat16), grad_joint_out)
    grad_input = grad_middle + product_right(grad_joint_out, joint_matrix)
    joint_sums = jnp.sum(grad_joint_out, axis=0, dtype=jnp.float32)
    bias_grads = jnp.stack(
        [
            joint_sums[:features],
            joint_sums[2 * features :],
            jnp.sum(grad_attended, axis=0, dtype=jnp.float32),
            grad_first_bias,
            jnp.sum(grad_branch, axis=0, dtype=jnp.float32),
            grad_second_bias,
        ]
    )
    gain_grads = jnp.stack([grad_first_gain, grad_second_gain])
    inner_grad = jnp.sum(grad_pre, axis=0, dtype=jnp.float32)
    return (
        grad_input,
        (grad_joint, grad_output, grad_expand, grad_shrink, gain_grads, bias_grads, inner_grad),
    )


def factored_partials(gradient, weight, rows_old):
    squared = gradient * gradient + FLOOR_SQUARE
    rows_next = DECAY_RATE * rows_old + (1.0 - DECAY_RATE) * jnp.mean(squared, axis=2)
    return (
        rows_next,
        jnp.sum(squared, axis=1),
        jnp.sum(rows_next, axis=1),
        jnp.sum(weight * weight, axis=(1, 2)),
    )


def vector_partials(gradient, moments_old):
    moments_next = DECAY_RATE * moments_old + (1.0 - DECAY_RATE) * (
        gradient * gradient + FLOOR_SQUARE
    )
    return (moments_next, gradient * lax.rsqrt(moments_next))


def local(
    tokens,
    segments,
    cotangent,
    joint_weight,
    output_weight,
    expand_weight,
    shrink_weight,
    norm_gains,
    biases,
    hidden_bias,
    joint_rows,
    joint_columns,
    output_rows,
    output_columns,
    expand_rows,
    expand_columns,
    shrink_rows,
    shrink_columns,
    gain_moments,
    bias_moments,
    hidden_moments,
):
    layers = joint_weight.shape[0]
    row_count, slot_count, features = tokens.shape
    hidden = tokens.astype(jnp.float32).reshape(row_count * slot_count, features)
    gathered_list = []
    stored_list = []
    for number in range(layers):
        weights = (
            lax.all_gather(joint_weight[number].astype(jnp.bfloat16), "fsdp", axis=0, tiled=True),
            lax.all_gather(output_weight[number].astype(jnp.bfloat16), "fsdp", axis=0, tiled=True),
            lax.all_gather(expand_weight[number].astype(jnp.bfloat16), "fsdp", axis=0, tiled=True),
            lax.all_gather(shrink_weight[number].astype(jnp.bfloat16), "fsdp", axis=0, tiled=True),
            lax.all_gather(norm_gains[number].astype(jnp.bfloat16), "fsdp", axis=1, tiled=True),
            lax.all_gather(biases[number].astype(jnp.bfloat16), "fsdp", axis=1, tiled=True),
            lax.all_gather(hidden_bias[number].astype(jnp.bfloat16), "fsdp", axis=0, tiled=True),
        )
        hidden, stored = block_forward(hidden, segments, weights)
        gathered_list.append(weights)
        stored_list.append(stored)
    activations = hidden.reshape(row_count, slot_count, features).astype(jnp.bfloat16)
    grad_hidden = cotangent.astype(jnp.float32).reshape(row_count * slot_count, features)
    collected = []
    for number in reversed(range(layers)):
        weights = (
            lax.all_gather(joint_weight[number].astype(jnp.bfloat16), "fsdp", axis=0, tiled=True),
            lax.all_gather(output_weight[number].astype(jnp.bfloat16), "fsdp", axis=0, tiled=True),
            lax.all_gather(expand_weight[number].astype(jnp.bfloat16), "fsdp", axis=0, tiled=True),
            lax.all_gather(shrink_weight[number].astype(jnp.bfloat16), "fsdp", axis=0, tiled=True),
            lax.all_gather(norm_gains[number].astype(jnp.bfloat16), "fsdp", axis=1, tiled=True),
            lax.all_gather(biases[number].astype(jnp.bfloat16), "fsdp", axis=1, tiled=True),
            lax.all_gather(hidden_bias[number].astype(jnp.bfloat16), "fsdp", axis=0, tiled=True),
        )
        grad_hidden, local_grads = block_backward(
            grad_hidden, segments, weights, stored_list[number]
        )
        grad_joint, grad_output, grad_expand, grad_shrink, gain_grads, bias_grads, inner_grad = (
            local_grads
        )
        shards = (
            lax.psum_scatter(grad_joint, "fsdp", scatter_dimension=0, tiled=True),
            lax.psum_scatter(grad_output, "fsdp", scatter_dimension=0, tiled=True),
            lax.psum_scatter(grad_expand, "fsdp", scatter_dimension=0, tiled=True),
            lax.psum_scatter(grad_shrink, "fsdp", scatter_dimension=0, tiled=True),
            lax.psum_scatter(gain_grads, "fsdp", scatter_dimension=1, tiled=True),
            lax.psum_scatter(bias_grads, "fsdp", scatter_dimension=1, tiled=True),
            lax.psum_scatter(inner_grad, "fsdp", scatter_dimension=0, tiled=True),
        )
        summed = (
            lax.psum(shards[0].astype(jnp.bfloat16), "dp").astype(jnp.float32),
            lax.psum(shards[1].astype(jnp.bfloat16), "dp").astype(jnp.float32),
            lax.psum(shards[2].astype(jnp.bfloat16), "dp").astype(jnp.float32),
            lax.psum(shards[3].astype(jnp.bfloat16), "dp").astype(jnp.float32),
            lax.psum(shards[4].astype(jnp.bfloat16), "dp").astype(jnp.float32),
            lax.psum(shards[5].astype(jnp.bfloat16), "dp").astype(jnp.float32),
            lax.psum(shards[6].astype(jnp.bfloat16), "dp").astype(jnp.float32),
        )
        collected.append(summed)
    collected = collected[::-1]
    input_gradient = grad_hidden.reshape(row_count, slot_count, features).astype(jnp.bfloat16)
    fsdp_count = lax.axis_size("fsdp")
    token_total = row_count * slot_count * lax.axis_size("dp") * fsdp_count
    root_scale = 1.0 / math.sqrt(token_total)
    stacked_grads = [
        jnp.stack([entry[index] for entry in collected]) * root_scale for index in range(7)
    ]
    matrices = (
        (stacked_grads[0], joint_weight, joint_rows, joint_columns),
        (stacked_grads[1], output_weight, output_rows, output_columns),
        (stacked_grads[2], expand_weight, expand_rows, expand_columns),
        (stacked_grads[3], shrink_weight, shrink_rows, shrink_columns),
    )
    partial_list = [factored_partials(item[0], item[1], item[2]) for item in matrices]
    vectors = (
        (stacked_grads[4], norm_gains, gain_moments),
        (stacked_grads[5], biases, bias_moments),
        (stacked_grads[6][:, None, :], hidden_bias[:, None, :], hidden_moments[:, None, :]),
    )
    vector_list = [vector_partials(item[0], item[2]) for item in vectors]
    vector_squares = jnp.concatenate(
        [jnp.sum(item[1] * item[1], axis=2) for item in vectors], axis=1
    )
    statistics = lax.psum(
        (
            partial_list[0][1],
            partial_list[1][1],
            partial_list[2][1],
            partial_list[3][1],
            jnp.stack([item[2] for item in partial_list], axis=1),
            jnp.stack([item[3] for item in partial_list], axis=1),
            vector_squares,
        ),
        "fsdp",
    )
    updates = []
    columns_list = []
    for index in range(4):
        gradient = matrices[index][0]
        total_rows = gradient.shape[1] * fsdp_count
        rows_next = partial_list[index][0]
        columns_next = DECAY_RATE * matrices[index][3] + (1.0 - DECAY_RATE) * (
            statistics[index] / total_rows
        )
        row_average = statistics[4][:, index] / total_rows
        estimate = rows_next[:, :, None] * columns_next[:, None, :] / row_average[:, None, None]
        updates.append(gradient * lax.rsqrt(estimate))
        columns_list.append(columns_next)
    matrix_squares = jnp.stack([jnp.sum(item * item, axis=(1, 2)) for item in updates], axis=1)
    vector_updates = jnp.concatenate(
        [jnp.sum(item[1] * item[1], axis=2) for item in vector_list], axis=1
    )
    norms = lax.psum((matrix_squares, vector_updates), "fsdp")
    matrix_next = []
    for index in range(4):
        gradient = matrices[index][0]
        entry_count = gradient.shape[1] * fsdp_count * gradient.shape[2]
        clip_ratio = jnp.sqrt(norms[0][:, index] / entry_count) / CLIP_LIMIT
        update = updates[index] / jnp.maximum(clip_ratio, 1.0)[:, None, None]
        stride = STEP_RATE * jnp.maximum(
            FLOOR_SCALE, jnp.sqrt(statistics[5][:, index] / entry_count)
        )
        matrix_next.append(matrices[index][1] - stride[:, None, None] * update)
    vector_next = []
    offset = 0
    for index in range(3):
        gradient = vectors[index][0]
        kinds = gradient.shape[1]
        entry_count = gradient.shape[2] * fsdp_count
        clip_ratio = jnp.sqrt(norms[1][:, offset : offset + kinds] / entry_count) / CLIP_LIMIT
        update = vector_list[index][1] / jnp.maximum(clip_ratio, 1.0)[:, :, None]
        stride = STEP_RATE * jnp.maximum(
            FLOOR_SCALE, jnp.sqrt(statistics[6][:, offset : offset + kinds] / entry_count)
        )
        vector_next.append(vectors[index][1] - stride[:, :, None] * update)
        offset = offset + kinds
    return (
        activations,
        input_gradient,
        stacked_grads[0],
        stacked_grads[1],
        stacked_grads[2],
        stacked_grads[3],
        stacked_grads[4],
        stacked_grads[5],
        stacked_grads[6],
        matrix_next[0],
        matrix_next[1],
        matrix_next[2],
        matrix_next[3],
        vector_next[0],
        vector_next[1],
        vector_next[2][:, 0, :],
        matrix_next[0].astype(jnp.bfloat16),
        matrix_next[1].astype(jnp.bfloat16),
        matrix_next[2].astype(jnp.bfloat16),
        matrix_next[3].astype(jnp.bfloat16),
        partial_list[0][0],
        columns_list[0],
        partial_list[1][0],
        columns_list[1],
        partial_list[2][0],
        columns_list[2],
        partial_list[3][0],
        columns_list[3],
        vector_list[0][0],
        vector_list[1][0],
        vector_list[2][0][:, 0, :],
    )


def solution(mesh):
    placed = (
        P(("dp", "fsdp"), None, None),
        P(("dp", "fsdp"), None),
        P(("dp", "fsdp"), None, None),
        P(None, "fsdp", None),
        P(None, "fsdp", None),
        P(None, "fsdp", None),
        P(None, "fsdp", None),
        P(None, None, "fsdp"),
        P(None, None, "fsdp"),
        P(None, "fsdp"),
        P(None, "fsdp"),
        P(),
        P(None, "fsdp"),
        P(),
        P(None, "fsdp"),
        P(),
        P(None, "fsdp"),
        P(),
        P(None, None, "fsdp"),
        P(None, None, "fsdp"),
        P(None, "fsdp"),
    )
    return jax.shard_map(
        local,
        mesh=mesh,
        in_specs=placed,
        out_specs=(
            P(("dp", "fsdp"), None, None),
            P(("dp", "fsdp"), None, None),
            P(None, "fsdp", None),
            P(None, "fsdp", None),
            P(None, "fsdp", None),
            P(None, "fsdp", None),
            P(None, None, "fsdp"),
            P(None, None, "fsdp"),
            P(None, "fsdp"),
            P(None, "fsdp", None),
            P(None, "fsdp", None),
            P(None, "fsdp", None),
            P(None, "fsdp", None),
            P(None, None, "fsdp"),
            P(None, None, "fsdp"),
            P(None, "fsdp"),
            P(None, "fsdp", None),
            P(None, "fsdp", None),
            P(None, "fsdp", None),
            P(None, "fsdp", None),
            P(None, "fsdp"),
            P(),
            P(None, "fsdp"),
            P(),
            P(None, "fsdp"),
            P(),
            P(None, "fsdp"),
            P(),
            P(None, None, "fsdp"),
            P(None, None, "fsdp"),
            P(None, "fsdp"),
        ),
        check_vma=False,
    )
```

profile of v0, /device:TPU:0, one launch (start us, length us, event | category | flops | bytes accessed | tf_op | source)
XLA Modules:
  0.0 1436.1 jit_solution(8705835819073505729)
XLA Ops:
  20.8 17.6 %all-gather.8 = bf16[1,6,768]{1,0,2:T(2,128)(2,1)S(1)} all-gather(bf16[1,6,96]{1,0,2:T(2,128)(2,1)S(1)} %get-tuple-element.409), channel_id=10, replica_groups=mesh['dp'=4,'fsdp'=8] {'fsdp'}, dimensions={2}, use_global_device_ids=true | all-gather | bytes 10368 | tf_op jit(solution)/shard_map/all_gather | solution.py:271
  38.8 13.4 slice_reduce_fusion
  52.2 15.2 %all-gather.1 = bf16[1,6,768]{1,0,2:T(2,128)(2,1)S(1)} all-gather(bf16[1,6,96]{1,0,2:T(2,128)(2,1)S(1)} %get-tuple-element.408), channel_id=3, replica_groups=mesh['dp'=4,'fsdp'=8] {'fsdp'}, dimensions={2}, use_global_device_ids=true | all-gather | bytes 10368 | tf_op jit(solution)/shard_map/all_gather | solution.py:271
  67.9 12.8 slice_reduce_fusion.8
  81.1 14.5 %all-gather.3 = bf16[1,2,768]{1,0,2:T(2,128)(2,1)S(1)} all-gather(bf16[1,2,96]{1,0,2:T(2,128)(2,1)S(1)} %get-tuple-element.407), channel_id=5, replica_groups=mesh['dp'=4,'fsdp'=8] {'fsdp'}, dimensions={2}, use_global_device_ids=true | all-gather | bytes 3456 | tf_op jit(solution)/shard_map/all_gather | solution.py:270
  101.3 13.3 all-gather.5
  114.7 28.3 %all-gather.10 = bf16[1,2,768]{1,0,2:T(2,128)(2,1)S(1)} all-gather(bf16[1,2,96]{1,0,2:T(2,128)(2,1)S(1)} %get-tuple-element.406), channel_id=12, replica_groups=mesh['dp'=4,'fsdp'=8] {'fsdp'}, dimensions={2}, use_global_device_ids=true | all-gather | bytes 3456 | tf_op jit(solution)/shard_map/all_gather | solution.py:270
  148.0 12.9 all-gather.12
  160.9 5.5 fusion.40
  183.0 20.2 %multiply_convert_fusion.3 = (bf16[512,3072]{1,0:T(8,128)(2,1)}, f32[512,3072]{1,0:T(8,128)}, f32[512,3072]{1,0:T(8,128)}) fusion(f32[3072]{0:T(1024)S(1)} %bitcast.331, bf16[1,768,3072]{2,1,0:T(8,128)(2,1)} %all-gather.27.cloned.1.call-done, f32[512,768]{1,0:T(8,128)S(1)} %get-tuple-element.438, f32[768]{0:T(1024)S(1)} %get-tuple-element.318, ...), kind=kOutput, calls=%fused_computation.41 | convolution fusion | flops 2521694208 | bytes 22042624 | tf_op jit(solution)/shard_map/dot_general | solution.py:24
  203.2 6.1 fusion.184
  209.7 22.7 %all-gather.31.cloned.1.call-done = bf16[1,768,2304]{2,1,0:T(8,128)(2,1)} async-done(((bf16[1,96,2304]{2,1,0:T(8,128)(2,1)}), bf16[1,768,2304]{2,1,0:T(8,128)(2,1)}) %all-gather.31.cloned.1.call-update) | async-done | bytes 3538960 | tf_op jit(solution)/shard_map/all_gather | solution.py:266
  232.3 5.5 fusion.41
  251.1 4.9 all-gather.33.cloned.1.call-done
  260.3 49.3 %all-gather.35.cloned.1.call-done = bf16[1,768,3072]{2,1,0:T(8,128)(2,1)} async-done(((bf16[1,96,3072]{2,1,0:T(8,128)(2,1)}), bf16[1,768,3072]{2,1,0:T(8,128)(2,1)}) %all-gather.35.cloned.1.call-update) | async-done | bytes 4718608 | tf_op jit(solution)/shard_map/all_gather | solution.py:268
  309.5 20.8 %multiply_convert_fusion.2 = (bf16[512,3072]{1,0:T(8,128)(2,1)}, f32[512,3072]{1,0:T(8,128)}, f32[512,3072]{1,0:T(8,128)}) fusion(f32[3072]{0:T(1024)S(1)} %bitcast.333, bf16[1,768,3072]{2,1,0:T(8,128)(2,1)} %all-gather.35.cloned.1.call-done, f32[512,768]{1,0:T(8,128)} %copy-done.20, f32[768]{0:T(1024)S(1)} %get-tuple-element.310, ...), kind=kOutput, calls=%fused_computation.28 | convolution fusion | flops 2521694208 | bytes 22042624 | tf_op jit(solution)/shard_map/dot_general | solution.py:24
  330.3 32.0 %all-gather.37.cloned.1.call-done = bf16[1,3072,768]{2,1,0:T(8,128)(2,1)} async-done(((bf16[1,384,768]{2,1,0:T(8,128)(2,1)}), bf16[1,3072,768]{2,1,0:T(8,128)(2,1)}) %all-gather.37.cloned.1.call-update) | async-done | bytes 4718608 | tf_op jit(solution)/shard_map/all_gather | solution.py:269
  362.3 6.5 fusion.186
  371.6 9.9 convert_reduce_fusion
  390.3 11.4 multiply_reduce_fusion.1
  403.2 7.0 multiply_convert_fusion.1
  424.3 6.2 multiply_reduce_fusion.9
  431.3 9.6 convert_reduce_fusion.1
  453.3 11.0 multiply_reduce_fusion
  464.3 7.0 multiply_convert_fusion
  479.6 5.0 convolution_bitcast_fusion
  484.5 8.1 copy.240
  494.1 6.8 fusion.157
  502.6 7.2 fusion.160
  511.2 7.2 fusion.154
  519.8 8.4 fusion.143
  529.6 8.3 fusion.137
  546.7 26.2 %reduce-scatter.37.cloned.1.call-done = f32[96,2304]{1,0:T(8,128)} async-done(((f32[768,2304]{1,0:T(8,128)}), f32[96,2304]{1,0:T(8,128)}) %reduce-scatter.37.cloned.1.call-update) | async-done | bytes 884752
  575.1 75.6 %reduce-scatter.39.cloned.1.call-done = f32[96,2304]{1,0:T(8,128)} async-done(((f32[768,2304]{1,0:T(8,128)}), f32[96,2304]{1,0:T(8,128)}) %reduce-scatter.39.cloned.1.call-update) | async-done | bytes 884752
  652.9 98.0 %reduce-scatter.29.cloned.1.call-done = f32[96,3072]{1,0:T(8,128)} async-done(((f32[768,3072]{1,0:T(8,128)}), f32[96,3072]{1,0:T(8,128)}) %reduce-scatter.29.cloned.1.call-update) | async-done | bytes 1179664 | tf_op jit(solution)/shard_map/reduce_scatter | solution.py:299
  753.0 97.9 %reduce-scatter.31.cloned.1.call-done = f32[96,3072]{1,0:T(8,128)} async-done(((f32[768,3072]{1,0:T(8,128)}), f32[96,3072]{1,0:T(8,128)}) %reduce-scatter.31.cloned.1.call-update) | async-done | bytes 1179664 | tf_op jit(solution)/shard_map/reduce_scatter | solution.py:299
  853.1 97.9 %reduce-scatter.35.cloned.1.call-done = f32[384,768]{1,0:T(8,128)} async-done(((f32[3072,768]{1,0:T(8,128)}), f32[384,768]{1,0:T(8,128)}) %reduce-scatter.35.cloned.1.call-update) | async-done | bytes 1179664 | tf_op jit(solution)/shard_map/reduce_scatter | solution.py:300
  953.1 97.9 %reduce-scatter.33.cloned.1.call-done = f32[384,768]{1,0:T(8,128)} async-done(((f32[3072,768]{1,0:T(8,128)}), f32[384,768]{1,0:T(8,128)}) %reduce-scatter.33.cloned.1.call-update) | async-done | bytes 1179664 | tf_op jit(solution)/shard_map/reduce_scatter | solution.py:300
  1059.3 23.5 %reduce-scatter.41.cloned.1.call-done = f32[96,2]{1,0:T(8,128)} async-done(((f32[768,2]{1,0:T(8,128)}), f32[96,2]{1,0:T(8,128)}) %reduce-scatter.41.cloned.1.call-update) | async-done | bytes 784
  1084.2 30.2 %reduce-scatter.43.cloned.1.call-done = f32[96,2]{1,0:T(8,128)} async-done(((f32[768,2]{1,0:T(8,128)}), f32[96,2]{1,0:T(8,128)}) %reduce-scatter.43.cloned.1.call-update) | async-done | bytes 784
  1115.7 29.7 %reduce-scatter.45.cloned.1.call-done = f32[96,6]{1,0:T(8,128)} async-done(((f32[768,6]{1,0:T(8,128)}), f32[96,6]{1,0:T(8,128)}) %reduce-scatter.45.cloned.1.call-update) | async-done | bytes 2320
  1146.8 30.1 %reduce-scatter.47.cloned.1.call-done = f32[96,6]{1,0:T(8,128)} async-done(((f32[768,6]{1,0:T(8,128)}), f32[96,6]{1,0:T(8,128)}) %reduce-scatter.47.cloned.1.call-update) | async-done | bytes 2320
  1178.4 102.5 %all-reduce.9.cloned.1.call-done = (bf16[1,96,2304]{1,2,0:T(8,128)(2,1)}, bf16[1,96,2304]{1,2,0:T(8,128)(2,1)}, bf16[1,96,768]{2,1,0:T(8,128)(2,1)}, bf16[1,96,7...) async-done(((bf16[1,96,2304]{1,2,0:T(8,128)(2,1)}, ...) | async-done | bytes 3538960 | tf_op jit(solution)/shard_map/psum | solution.py:306
  1292.5 30.6 %all-reduce.10 = (bf16[3072]{0:T(1024)(128)(2,1)}, bf16[3072]{0:T(1024)(128)(2,1)}, f32[2,4]{0,1:T(4,128)}, f32[2,768]{1,0:T(2,128)}, f32[2,3072]{1,0:T(2,128)}, /*index=5*/f32[2,768]{1,0:T(2,128)}, f32[2,2304]{1,0:T(2,128)}) all-reduce(f32[3072]{0:T(1024)} %get-tuple-element.456, ...), channel_id=29, replica_groups=mesh['dp'=4,'fsdp'=8] {'fsdp'}, use_global_device_ids=true, to_apply=%region_64.65.clone | all-reduce | flops 19976 | bytes 147520
  1325.7 9.7 all-reduce.4
  1354.6 4.9 fusion.95
  1359.5 27.4 %all-reduce.2 = (f32[2,4]{0,1:T(4,128)}, f32[2,4]{0,1:T(4,128)}, f32[2,9]{0,1:T(8,128)}, f32[2,9]{0,1:T(8,128)}) all-reduce(f32[2,4]{0,1:T(4,128)} %pad_maximum_fusion.9, f32[2,4]{0,1:T(4,128)} %pad_maximum_fusion.7, f32[2,9]{0,1:T(8,128)} %pad_maximum_fusion.4, f32[2,9]{0,1:T(8,128)} %pad_maximum_fusion.3), channel_id=1, replica_groups=mesh['dp'=4,'fsdp'=8] {'fsdp'}, use_global_device_ids=true, to_apply=%region_92.93 | all-reduce | flops 52 | bytes 416 | tf_op jit(solution)/shard_map/psum | solution.py:368
  1418.4 5.0 fusion.163
  (490 shorter events, 217.7 us)
Async XLA Ops:
  7.2 153.7 %all-gather.23.cloned.1.call-start = ((), (), s32[]{:S(2)}) async-start(), calls=%async_computation.18 | async-start | bytes 3981312 | tf_op jit(solution)/shard_map/all_gather | solution.py:266
  11.1 169.0 %all-gather.25.cloned.1.call-start = ((), (), s32[]{:S(2)}) async-start(), calls=%async_computation.19 | async-start | bytes 1327104 | tf_op jit(solution)/shard_map/all_gather | solution.py:267
  12.7 170.3 %all-gather.27.cloned.1.call-start = ((), (), s32[]{:S(2)}) async-start(), calls=%async_computation.20 | async-start | bytes 5308416 | tf_op jit(solution)/shard_map/all_gather | solution.py:268
  14.8 188.4 %all-gather.29.cloned.1.call-start = ((), (), s32[]{:S(2)}) async-start(), calls=%async_computation.21 | async-start | bytes 5308416 | tf_op jit(solution)/shard_map/all_gather | solution.py:269
  17.8 214.5 %all-gather.31.cloned.1.call-start = ((), (), s32[]{:S(2)}) async-start(), calls=%async_computation.22 | async-start | bytes 3981312 | tf_op jit(solution)/shard_map/all_gather | solution.py:266
  18.4 237.5 %all-gather.33.cloned.1.call-start = ((), (), s32[]{:S(2)}) async-start(), calls=%async_computation.23 | async-start | bytes 1327104 | tf_op jit(solution)/shard_map/all_gather | solution.py:267
  19.0 290.5 %all-gather.35.cloned.1.call-start = ((), (), s32[]{:S(2)}) async-start(), calls=%async_computation.24 | async-start | bytes 5308416 | tf_op jit(solution)/shard_map/all_gather | solution.py:268
  19.8 342.5 %all-gather.37.cloned.1.call-start = ((), (), s32[]{:S(2)}) async-start(), calls=%async_computation.25 | async-start | bytes 5308416 | tf_op jit(solution)/shard_map/all_gather | solution.py:269
  20.5 522.9 %reduce-scatter.27.cloned.1.call-start = ((), (), s32[]{:S(2)}) async-start(), calls=%async_computation.13 | async-start | bytes 2654208 | tf_op jit(solution)/shard_map/reduce_scatter | solution.py:298
  52.2 28.5 %copy-start.79 = (s32[1,512]{1,0:T(1,128)S(1)}, s32[1,512]{1,0:T(1,128)}, u32[]{:S(2)}) copy-start(s32[1,512]{1,0:T(1,128)} %param.22) | copy-start | bytes 6148
  52.2 28.7 %copy-start.65 = (f32[2,2,96]{2,1,0:T(2,128)S(1)}, f32[2,2,96]{2,1,0:T(2,128)}, u32[]{:S(2)}) copy-start(f32[2,2,96]{2,1,0:T(2,128)} %param.28) | copy-start | bytes 4612
  67.8 32.8 %copy-start.73 = (f32[2,384]{1,0:T(2,128)S(1)}, f32[2,384]{1,0:T(2,128)}, u32[]{:S(2)}) copy-start(f32[2,384]{1,0:T(2,128)} %param.30) | copy-start | bytes 9220
  80.6 122.5 %copy-start.92 = (f32[768]{0:T(1024)}, f32[768]{0:T(1024)S(1)}, u32[]{:S(2)}) copy-start(f32[768]{0:T(1024)S(1)} %get-tuple-element.318) | copy-start | bytes 9220
  80.7 175.3 %copy-start.94 = (f32[768]{0:T(1024)}, f32[768]{0:T(1024)S(1)}, u32[]{:S(2)}) copy-start(f32[768]{0:T(1024)S(1)} %get-tuple-element.316) | copy-start | bytes 9220
  80.7 80.2 %copy-start.46 = (bf16[1,512,768]{2,1,0:T(8,128)(2,1)S(1)}, bf16[1,512,768]{2,1,0:T(8,128)(2,1)}, u32[]{:S(2)}) copy-start(bf16[1,512,768]{2,1,0:T(8,128)(2,1)} %param.21) | copy-start | bytes 2359300
  100.7 102.5 %copy-start.68 = (f32[768]{0:T(1024)}, f32[768]{0:T(1024)S(1)}, u32[]{:S(2)}) copy-start(f32[768]{0:T(1024)S(1)} %get-tuple-element.315) | copy-start | bytes 9220
  114.7 68.3 %copy-start.71 = (f32[1,3072]{1,0:T(1,128)}, f32[1,3072]{1,0:T(1,128)S(1)}, u32[]{:S(2)}) copy-start(f32[1,3072]{1,0:T(1,128)S(1)} %convert_element_type.396) | copy-start | bytes 36868
  182.6 20.6 %copy-start.17 = (f32[512,768]{1,0:T(8,128)}, f32[512,768]{1,0:T(8,128)S(1)}, u32[]{:S(2)}) copy-start(f32[512,768]{1,0:T(8,128)S(1)} %get-tuple-element.438) | copy-start | bytes 4718596
  182.6 20.6 %copy-start.63 = (f32[512]{0:T(512)}, f32[512]{0:T(512)S(1)}, u32[]{:S(2)}) copy-start(f32[512]{0:T(512)S(1)} %broadcast_multiply_fusion.11) | copy-start | bytes 6148
  182.9 20.3 %copy-start.80 = (f32[512]{0:T(512)}, f32[512]{0:T(512)S(1)}, u32[]{:S(2)}) copy-start(f32[512]{0:T(512)S(1)} %add_rsqrt_fusion.3) | copy-start | bytes 6148
  209.3 23.0 %copy-start.23 = (f32[512,768]{1,0:T(8,128)}, f32[512,768]{1,0:T(8,128)S(1)}, u32[]{:S(2)}) copy-start(f32[512,768]{1,0:T(8,128)S(1)} %get-tuple-element.441) | copy-start | bytes 4718596
  309.5 52.8 %copy-start.96 = (f32[768]{0:T(1024)S(1)}, f32[768]{0:T(1024)}, u32[]{:S(2)}) copy-start(f32[768]{0:T(1024)} %get-tuple-element.309) | copy-start | bytes 9220
  370.0 11.5 slice-start.8
  390.3 11.4 slice-start.3
  390.3 11.4 slice-start.4
  390.3 12.8 slice-start.5
  421.2 123.8 %reduce-scatter.25.cloned.1.call-start = ((), (), s32[]{:S(2)}) async-start(), calls=%async_computation.12 | async-start | bytes 2654208 | tf_op jit(solution)/shard_map/reduce_scatter | solution.py:298
  424.3 16.6 %slice-start.6 = ((s8[4718592]{0:T(1024)(128)(4,1)}), s8[4194304]{0:T(1024)(128)(4,1)S(1)}, s32[]{:S(2)}) async-start(s8[4718592]{0:T(1024)(128)(4,1)} %bitcast.354), calls=%async_computation.39 | async-start | bytes 8388608
  451.6 121.2 %reduce-scatter.37.cloned.1.call-start = ((), (), s32[]{:S(2)}) async-start(), calls=%async_computation.26 | async-start | bytes 7962624
  451.9 12.5 slice-start
  492.6 158.0 %reduce-scatter.39.cloned.1.call-start = ((), (), s32[]{:S(2)}) async-start(), calls=%async_computation.27 | async-start | bytes 7962624
  500.9 250.0 %reduce-scatter.29.cloned.1.call-start = ((), (), s32[]{:S(2)}) async-start(), calls=%async_computation.14 | async-start | bytes 10616832 | tf_op jit(solution)/shard_map/reduce_scatter | solution.py:299
  509.9 341.1 %reduce-scatter.31.cloned.1.call-start = ((), (), s32[]{:S(2)}) async-start(), calls=%async_computation.15 | async-start | bytes 10616832 | tf_op jit(solution)/shard_map/reduce_scatter | solution.py:299
  518.4 432.6 %reduce-scatter.35.cloned.1.call-start = ((), (), s32[]{:S(2)}) async-start(), calls=%async_computation.17 | async-start | bytes 10616832 | tf_op jit(solution)/shard_map/reduce_scatter | solution.py:300
  528.2 522.9 %reduce-scatter.33.cloned.1.call-start = ((), (), s32[]{:S(2)}) async-start(), calls=%async_computation.16 | async-start | bytes 10616832 | tf_op jit(solution)/shard_map/reduce_scatter | solution.py:300
  537.9 544.9 %reduce-scatter.41.cloned.1.call-start = ((), (), s32[]{:S(2)}) async-start(), calls=%async_computation.28 | async-start | bytes 442368
  539.5 574.8 %reduce-scatter.43.cloned.1.call-start = ((), (), s32[]{:S(2)}) async-start(), calls=%async_computation.29 | async-start | bytes 442368
  540.5 604.8 %reduce-scatter.45.cloned.1.call-start = ((), (), s32[]{:S(2)}) async-start(), calls=%async_computation.30 | async-start | bytes 442368
  541.8 635.1 %reduce-scatter.47.cloned.1.call-start = ((), (), s32[]{:S(2)}) async-start(), calls=%async_computation.31 | async-start | bytes 442368
  543.1 737.8 %all-reduce.9.cloned.1.call-start = ((), (), s32[]{:S(2)}) async-start(), calls=%async_computation.32 | async-start | bytes 7667712 | tf_op jit(solution)/shard_map/psum | solution.py:306
  1287.2 136.2 %copy-start.2 = (f32[2,96,3072]{2,1,0:T(8,128)}, f32[2,96,3072]{2,1,0:T(8,128)S(1)}, u32[]{:S(2)}) copy-start(f32[2,96,3072]{2,1,0:T(8,128)S(1)} %get-tuple-element.368) | copy-start | bytes 7077892
  1287.2 61.3 %copy-start.32 = (bf16[1,96,2304]{1,2,0:T(8,128)(2,1)S(1)}, bf16[1,96,2304]{1,2,0:T(8,128)(2,1)}, u32[]{:S(2)}) copy-start(bf16[1,96,2304]{1,2,0:T(8,128)(2,1)} %get-tuple-element.339) | copy-start | bytes 1327108
  1287.2 61.3 %copy-start.33 = (bf16[1,96,2304]{1,2,0:T(8,128)(2,1)S(1)}, bf16[1,96,2304]{1,2,0:T(8,128)(2,1)}, u32[]{:S(2)}) copy-start(bf16[1,96,2304]{1,2,0:T(8,128)(2,1)} %get-tuple-element.340) | copy-start | bytes 1327108
  1341.8 11.4 copy-start.3
  1341.8 11.4 copy-start.62
  1342.7 11.3 copy-start.89
  1342.7 11.3 copy-start.91
  1344.2 81.9 %copy-start.56 = (f32[2,768]{1,0:T(2,128)}, f32[2,768]{1,0:T(2,128)S(1)}, u32[]{:S(2)}) copy-start(f32[2,768]{1,0:T(2,128)S(1)} %multiply_add_fusion.10) | copy-start | bytes 18436
  (104 other events, 472.8 us)
Sparse Core Ops, SparseCore 0:
  11.3 47.3 all-gather.22
  60.9 21.5 all-gather.24
  84.7 52.8 all-gather.26
  139.6 50.3 all-gather.28
  192.1 40.2 all-gather.30
  234.4 21.5 all-gather.32
  258.2 51.3 all-gather.34
  311.7 50.5 all-gather.36
  421.4 35.0 reduce-scatter.26
  458.6 35.4 reduce-scatter.24
  496.4 76.3 reduce-scatter.36
  575.0 75.6 reduce-scatter.38
  653.0 97.8 reduce-scatter.28
  753.0 97.8 reduce-scatter.30
  853.1 97.8 reduce-scatter.34
  953.2 97.8 reduce-scatter.32
  1053.7 29.0 reduce-scatter.40
  1085.6 28.7 reduce-scatter.42
  1116.6 28.7 reduce-scatter.44
  1148.2 28.7 reduce-scatter.46
  1182.6 98.2 all-reduce.8
where the time goes:
time: 1450 us; the launch traced here: 1440 us
  waiting for transfers between devices  821 us (57%)
  matrix products  206 us (14%)
  blocking collectives  170 us (12%)
  local copies, waits for them, and re-layouts  118 us (8%)
  other arithmetic  102 us (7%)
  between operations  17.1 us (1%)
    unnamed x27, waiting for transfers between devices  218 us
    reduce_scatter x2, waiting for transfers between devices, local(): lax.psum_scatter(grad_expand, 'fsdp', scatter_dimension=0, tiled=True)  196 us
    reduce_scatter x2, waiting for transfers between devices, local(): lax.psum_scatter(grad_shrink, 'fsdp', scatter_dimension=0, tiled=True)  196 us
    psum x1, waiting for transfers between devices, local(): lax.psum(shards[0].astype(jnp.bfloat16), 'dp').astype(jnp.float32)  102 us
    dot_general x8, matrix products, product(): return jnp.dot(left, right, preferred_element_type=jnp.float32)  69.8 us
    unnamed x285, local copies, waits for them, and re-layouts  58.8 us
    all_gather x2, waiting for transfers between devices, local(): lax.all_gather(expand_weight[number].astype(jnp.bfloat16), 'fsdp', axis=0...  49.3 us
    all_gather x2, blocking collectives, local(): lax.all_gather(norm_gains[number].astype(jnp.bfloat16), 'fsdp', axis=1, t...  42.8 us
  transfers between devices with their start and end apart: 21, of which 15 were waited for; matrix products, arithmetic and copies ran while one was open for 18% of the time, Pallas kernels for 0%

commit v1 on v0

--- a/solution.py
+++ b/solution.py
@@ -5,6 +5,8 @@
 import jax.numpy as jnp
 from jax import lax
 from jax.sharding import PartitionSpec as P
+from jax.experimental import pallas as pl
+from jax.experimental.pallas import tpu as pltpu
 
 HEADS = 12
 HEAD_SIZE = 64
@@ -233,7 +235,7 @@
     return (moments_next, gradient * lax.rsqrt(moments_next))
 
 
-def local(
+def local_plain(
     tokens,
     segments,
     cotangent,
@@ -424,6 +426,898 @@
     )
 
 
+F32 = jnp.float32
+BF = jnp.bfloat16
+T = 512
+D = 768
+
+
+def nn(a, b):
+    return lax.dot_general(a, b, (((1,), (0,)), ((), ())), preferred_element_type=F32)
+
+
+def nt(a, b):
+    return lax.dot_general(a, b, (((1,), (1,)), ((), ())), preferred_element_type=F32)
+
+
+def rows_at(i, n):
+    return pl.ds(pl.multiple_of(i * n, n), n)
+
+
+def build_mask(seg_ref, bias_ref):
+    row = seg_ref[...]
+    wide = jnp.broadcast_to(row, (128, T)).T
+    for j in range(T // 128):
+        bias_ref[:, j * 128 : (j + 1) * 128] = jnp.where(
+            wide == row[:, j * 128 : (j + 1) * 128], 0.0, MASK_VALUE
+        ).astype(F32)
+
+
+def joint_forward(xb, wa, vec, joint, tile=256):
+    for b in range(3):
+        @pl.loop(0, T // tile)
+        def _(i, b=b):
+            r = rows_at(i, tile)
+            out = nn(xb[r, :], wa[b])
+            if b == 0:
+                out = out + vec[2:3, :]
+            if b == 2:
+                out = out + vec[3:4, :]
+            joint[b, r, :] = out.astype(BF)
+
+
+def head_masks():
+    lane = lax.broadcasted_iota(jnp.int32, (1, 128), 1)
+    return [
+        jnp.where(lane < 64, 1.0, 0.0).astype(F32),
+        jnp.where(lane >= 64, 1.0, 0.0).astype(F32),
+    ]
+
+
+def attend_forward_pair(p, joint, bias, ctx, logsum):
+    lanes = pl.ds(pl.multiple_of(p * 128, 128), 128)
+    masks = head_masks()
+    q2 = joint[0, :, lanes]
+    k2 = joint[1, :, lanes]
+    vt = joint[2, :, lanes].T
+    outs, sums = [], []
+    for h in range(2):
+        qm = q2 * (masks[h] * 0.125).astype(BF)
+        st = nt(k2, qm) + bias[...]
+        top = jnp.max(st, axis=0, keepdims=True)
+        e = jnp.exp(st - top)
+        total = jnp.sum(e, axis=0, keepdims=True)
+        ct = nn(vt[64 * h : 64 * h + 64, :], e.astype(BF))
+        outs.append(ct * (1.0 / total))
+        sums.append(top + jnp.log(total))
+    ctx[:, lanes] = jnp.concatenate(outs, axis=0).T.astype(BF)
+    logsum[p] = jnp.concatenate(sums, axis=0)
+
+
+def norm_parts(u):
+    avg = jnp.mean(u, axis=-1, keepdims=True)
+    c = u - avg
+    var = jnp.mean(c * c, axis=-1, keepdims=True)
+    inv = lax.rsqrt(var + NORM_EPSILON)
+    return c * inv, inv
+
+
+def out_forward(ctx, x, wo, vec, n1, r1, h, hb, tile=128):
+    @pl.loop(0, T // tile)
+    def _(i):
+        r = rows_at(i, tile)
+        u = nn(ctx[r, :], wo[...]) + vec[4:5, :] + x[r, :].astype(F32)
+        n, inv = norm_parts(u)
+        y = n * vec[0:1, :] + vec[5:6, :]
+        n1[r, :] = n.astype(n1.dtype)
+        r1[r, :] = jnp.broadcast_to(inv, (tile, 128))
+        h[r, :] = y
+        hb[r, :] = y.astype(BF)
+
+
+def gelu_parts(z):
+    a = jnp.abs(z)
+    e = jnp.exp(z * z * -0.5)
+    t = 1.0 / (1.0 + 0.23164189 * a)
+    poly = t * (
+        0.127414796 + t * (-0.142248368 + t * (0.7107068705 + t * (-0.7265760135 + t * 0.5307027145)))
+    )
+    tail = poly * e
+    cdf = jnp.where(z >= 0.0, 1.0 - tail, tail)
+    return z * cdf, cdf + z * (e * 0.3989422804014327)
+
+
+def ffn_up(hb, we, vec, g, gp, b, tile=128):
+    @pl.loop(0, T // tile)
+    def _(i):
+        r = rows_at(i, tile)
+        z = nn(hb[r, :], we[b]) + vec[8 + b : 9 + b, :]
+        act, der = gelu_parts(z)
+        g[b, r, :] = act.astype(BF)
+        gp[b, r, :] = der.astype(BF)
+
+
+def ffn_down(g, ws, vec, h, n2, r2, x_out, xb_out, tile=128):
+    @pl.loop(0, T // tile)
+    def _(i):
+        r = rows_at(i, tile)
+        u = h[r, :] + vec[6:7, :]
+        for b in range(4):
+            u = u + nn(g[b, r, :], ws[b])
+        n, inv = norm_parts(u)
+        y = n * vec[1:2, :] + vec[7:8, :]
+        n2[r, :] = n.astype(n2.dtype)
+        r2[r, :] = jnp.broadcast_to(inv, (tile, 128))
+        if x_out is not None:
+            x_out[r, :] = y
+        xb_out[r, :] = y.astype(BF)
+
+
+def sum8(v):
+    return jnp.sum(v.reshape(v.shape[0] // 8, 8, v.shape[1]), axis=0)
+
+
+def norm_backward(dy, n, r, gain_row, du, dub, sums, rows, tile=128):
+    def step(i, carry):
+        s = rows_at(i, tile)
+        g = dy[s, :].astype(F32)
+        nv = n[s, :].astype(F32)
+        inv = r[s, 0:1]
+        e = g * gain_row
+        m1 = jnp.mean(e, axis=-1, keepdims=True)
+        m2 = jnp.mean(e * nv, axis=-1, keepdims=True)
+        d = inv * (e - m1 - nv * m2)
+        db = d.astype(BF)
+        du[s, :] = d
+        dub[s, :] = db
+        return (
+            carry[0] + sum8(g * nv),
+            carry[1] + sum8(g),
+            carry[2] + sum8(db.astype(F32)),
+        )
+
+    zero = jnp.zeros((8, D), F32)
+    out = lax.fori_loop(0, T // tile, step, (zero, zero, zero))
+    for k in range(3):
+        sums[rows[k] : rows[k] + 1, :] = jnp.sum(out[k], axis=0, keepdims=True)
+
+
+def transpose_into(src, dst, tile=128):
+    @pl.loop(0, T // tile)
+    def _(i):
+        dst[:, rows_at(i, tile)] = src[rows_at(i, tile), :].T
+
+
+def weight_grad(at, bmat, out, tile=256):
+    @pl.loop(0, D // tile)
+    def _(i):
+        r = rows_at(i, tile)
+        out[r, :] = nn(at[r, :], bmat[...]).astype(BF)
+
+
+def ffn_back_block(dob, ws, g, gp, dz, sums, b, tile=128):
+    def step(i, acc):
+        r = rows_at(i, tile)
+        v = (nt(dob[r, :], ws[b]) * gp[b, r, :].astype(F32)).astype(BF)
+        dz[b, r, :] = v
+        return acc + sum8(v.astype(F32))
+
+    acc = lax.fori_loop(0, T // tile, step, jnp.zeros((8, D), F32))
+    sums[8 + b : 9 + b, :] = jnp.sum(acc, axis=0, keepdims=True)
+
+
+def ffn_back_input(dz, we, du, tile=128):
+    @pl.loop(0, T // tile)
+    def _(i):
+        r = rows_at(i, tile)
+        u = du[r, :]
+        for b in range(4):
+            u = u + nt(dz[b, r, :], we[b])
+        du[r, :] = u
+
+
+def context_back(dab, wo, dc, tile=256):
+    @pl.loop(0, T // tile)
+    def _(i):
+        r = rows_at(i, tile)
+        dc[r, :] = nt(dab[r, :], wo[...]).astype(BF)
+
+
+def attend_backward_pair(p, joint, bias, logsum, dc, dj):
+    lanes = pl.ds(pl.multiple_of(p * 128, 128), 128)
+    masks = head_masks()
+    q2 = joint[0, :, lanes]
+    k2 = joint[1, :, lanes]
+    v2 = joint[2, :, lanes]
+    d2 = dc[:, lanes]
+    kt = k2.T
+    ls = logsum[p]
+    dk = jnp.zeros((T, 128), F32)
+    dv = jnp.zeros((T, 128), F32)
+    dqt = []
+    for h in range(2):
+        qm = q2 * (masks[h] * 0.125).astype(BF)
+        dm = d2 * masks[h].astype(BF)
+        prob = jnp.exp(nt(k2, qm) + bias[...] - ls[h : h + 1, :])
+        dp = nt(v2, dm)
+        delta = jnp.sum(prob * dp, axis=0, keepdims=True)
+        ds = (prob * (dp - delta)).astype(BF)
+        dv = dv + nn(prob.astype(BF), dm)
+        dk = dk + nn(ds, qm)
+        dqt.append(nn(kt[64 * h : 64 * h + 64, :], ds))
+    dj[0, :, lanes] = (jnp.concatenate(dqt, axis=0) * 0.125).T.astype(BF)
+    dj[1, :, lanes] = dk.astype(BF)
+    dj[2, :, lanes] = dv.astype(BF)
+
+
+def input_back(dj, wa, du, dx, sums, tile=128):
+    def step(i, carry):
+        r = rows_at(i, tile)
+        u = du[r, :]
+        for b in range(3):
+            u = u + nt(dj[b, r, :], wa[b])
+        dx[r, :] = u.astype(dx.dtype)
+        return (carry[0] + sum8(dj[0, r, :].astype(F32)), carry[1] + sum8(dj[2, r, :].astype(F32)))
+
+    zero = jnp.zeros((8, D), F32)
+    out = lax.fori_loop(0, T // tile, step, (zero, zero))
+    sums[2:3, :] = jnp.sum(out[0], axis=0, keepdims=True)
+    sums[3:4, :] = jnp.sum(out[1], axis=0, keepdims=True)
+
+
+MESH = pl.DeviceIdType.MESH
+PAIRS = 6
+PIECE = 96
+GROUPS = 6
+
+
+def place():
+    q = lax.axis_index("dp")
+    f = lax.axis_index("fsdp")
+    z = f // 2
+    c = f % 2
+    x_side = (q + 1 - 2 * (q % 2), f)
+    y_side = ((q + 2) % 4, f)
+    sibling = (q, f + 1 - 2 * c)
+    planes = [(q, (f + 2 * k) % 8) for k in range(1, 4)]
+    return q, z, c, x_side, y_side, sibling, planes
+
+
+def greet(peers):
+    barrier = pltpu.get_barrier_semaphore()
+    for peer in peers:
+        pl.semaphore_signal(barrier, inc=1, device_id=peer, device_id_type=MESH)
+    pl.semaphore_wait(barrier, len(peers))
+
+
+def hidden_piece(kind, b, zz, c, first, count):
+    if kind < 2:
+        start = 192 * zz + 96 * c + first
+        return b, pl.ds(pl.multiple_of(start, 16), count)
+    start = 384 * c + 96 * b + first
+    return zz, pl.ds(pl.multiple_of(start, 16), count)
+
+
+PARTS = [(g, first, 32) for g in range(6) for first in (0, 32, 64)]
+
+
+class Gather:
+    def __init__(self, whole, sbuf, sems):
+        self.whole, self.sbuf, self.sems = whole, sbuf, sems
+        q, z, c, self.x_side, self.y_side, self.sibling, self.planes = place()
+        self.q, self.z, self.c = q, z, c
+        self.qx = q + 1 - 2 * (q % 2)
+        self.qy = (q + 2) % 4
+        self.qd = (self.qx + 2) % 4
+        self.others = [(z + k) % 4 for k in range(1, 4)]
+
+    def spot(self, k, b, zz, cols=None):
+        g, first, count = PARTS[k]
+        lead, rows = hidden_piece(g % 3, b, zz, self.c, first, count)
+        if cols is None:
+            return self.whole.at[g, lead, rows, :]
+        return self.whole.at[g, lead, rows, pl.ds(384 * cols, 384)]
+
+    def send(self, k, src, dst, slot, peer):
+        pltpu.make_async_remote_copy(
+            src_ref=src, dst_ref=dst, send_sem=self.sems.at[k, slot], recv_sem=self.sems.at[k, slot + 1],
+            device_id=peer, device_id_type=MESH,
+        ).start()
+
+    def total(self, k, slot, rows, cols=768):
+        lead = self.whole.at[0, 0, pl.ds(0, rows), pl.ds(0, cols)] if rows <= 768 else self.whole.at[0, pl.ds(0, rows // 768)]
+        pltpu.make_async_copy(lead, lead, self.sems.at[k, slot]).wait()
+
+    def z_send(self, k):
+        g, first, count = PARTS[k]
+        src = self.sbuf.at[g, self.q, pl.ds(first, count), :]
+        for peer in self.planes:
+            self.send(k, src, self.spot(k, self.q, self.z), 0, peer)
+        for b in range(4):
+            mine = self.sbuf.at[g, b, pl.ds(first, count), :]
+            self.send(k, mine, self.spot(k, b, self.z), 10, self.sibling)
+            pltpu.make_async_copy(mine, self.spot(k, b, self.z), self.sems.at[k, 12]).start()
+
+    def xy_send(self, k):
+        count = PARTS[k][2]
+        self.total(k, 1, 3 * count)
+        for zz in self.others:
+            spot = self.spot(k, self.q, zz)
+            self.send(k, spot, spot, 2, self.x_side)
+            self.send(k, spot, spot, 4, self.y_side)
+        for zz in self.others:
+            spot = self.spot(k, self.q, zz)
+            self.send(k, spot, spot, 10, self.sibling)
+
+    def diagonal_send(self, k):
+        count = PARTS[k][2]
+        self.total(k, 3, 3 * count)
+        self.total(k, 5, 3 * count)
+        for zz in self.others:
+            spot = self.spot(k, self.qy, zz, 0)
+            self.send(k, spot, spot, 6, self.x_side)
+            spot = self.spot(k, self.qx, zz, 1)
+            self.send(k, spot, spot, 8, self.y_side)
+        for zz in self.others:
+            for b in (self.qx, self.qy):
+                spot = self.spot(k, b, zz)
+                self.send(k, spot, spot, 10, self.sibling)
+
+    def last_send(self, k):
+        count = PARTS[k][2]
+        self.total(k, 7, 3 * count, 384)
+        self.total(k, 9, 3 * count, 384)
+        for zz in self.others:
+            spot = self.spot(k, self.qd, zz)
+            self.send(k, spot, spot, 10, self.sibling)
+
+    def finish(self, k):
+        count = PARTS[k][2]
+        self.total(k, 11, 16 * count)
+        self.total(k, 12, 4 * count)
+
+    def drain(self, k):
+        count = PARTS[k][2]
+        self.total(k, 0, 3 * count)
+        self.total(k, 2, 3 * count)
+        self.total(k, 4, 3 * count)
+        self.total(k, 6, 3 * count, 384)
+        self.total(k, 8, 3 * count, 384)
+        self.total(k, 10, 16 * count)
+
+
+UNIT_TIMES = (("joint", 3.0),) + tuple((f"att{p}", 1.4) for p in range(6)) + (("out", 2.0),) + tuple(
+    (f"up{b}", 1.7) for b in range(4)
+) + (("down", 3.0),)
+
+
+def forward_plan():
+    events = []
+    z_free = 5.0
+    xy_free = 0.0
+    ready = {}
+    jobs = []
+    for k, (g, first, count) in enumerate(PARTS):
+        share = count / 96.0
+        z_start = z_free
+        z_free = z_start + 12.6 * share
+        jobs.append([z_free + 1.5, k, "xy", 9.9 * share])
+        events.append((z_start if k else 0.0, 0, "z", k))
+    done = []
+    jobs.sort()
+    while jobs:
+        jobs.sort(key=lambda j: (max(j[0], xy_free), 0 if j[2] == "dg" else 1, j[1]))
+        at, k, kind, cost = jobs.pop(0)
+        start = max(at, xy_free)
+        xy_free = start + cost
+        share = PARTS[k][2] / 96.0
+        if kind == "xy":
+            events.append((at, 1, "xy", k))
+            jobs.append([xy_free + 1.5, k, "dg", 5.1 * share])
+        else:
+            events.append((at, 2, "dg", k))
+            events.append((xy_free + 1.5, 3, "last", k))
+            events.append((xy_free + 1.5 + 2.0, 4, "fin", k))
+            ready[PARTS[k][0]] = xy_free + 3.5 + 2.0
+    events.sort()
+    order, now, pos = [], 0.0, 0
+    for layer in range(2):
+        for name, cost in UNIT_TIMES:
+            need = {"joint": 0, "up0": 1, "down": 2}.get(name)
+            start = now
+            if need is not None:
+                start = max(now, ready[3 * layer + need])
+            while pos < len(events) and events[pos][0] <= start + 0.3:
+                order.append(events[pos][2:])
+                pos += 1
+            order.append(("run", layer, name))
+            now = start + cost
+    assert pos == len(events)
+    return order
+
+
+def forward_kernel(
+    tokens, seg, vecs, joint_w, output_w, expand_w, shrink_w,
+    whole, vec_out, x_saved, j_saved, c_saved, l_saved, n1_saved, r1_saved, g_saved, gp_saved, n2_saved, r2_saved, final, squares,
+    stage, sbuf, wv, bias, x1, h, hb, xb, joint, ctx, logsum, n1, r1, g, gp, n2, r2, vg, vec,
+    sems, stage_sems, wv_sems, vec_sems, out_sems,
+):
+    masters = (joint_w, output_w, expand_w, shrink_w)
+    gather = Gather(whole, sbuf, sems)
+    q, z, c = gather.q, gather.z, gather.c
+
+    def stage_copies(grp):
+        layer, kind = divmod(grp, 3)
+        slot = grp % 2
+        out = []
+        for b in range(4):
+            if kind == 0:
+                src = output_w.at[layer] if b == 3 else joint_w.at[layer, :, pl.ds(768 * b, 768)]
+            elif kind == 1:
+                src = expand_w.at[layer, :, pl.ds(768 * b, 768)]
+            else:
+                src = shrink_w.at[layer, pl.ds(96 * b, 96), :]
+            out.append(pltpu.make_async_copy(src, stage.at[slot, b], stage_sems.at[slot, b]))
+        return out
+
+    def take(grp):
+        layer, kind = divmod(grp, 3)
+        slot = grp % 2
+        for cp in stage_copies(grp):
+            cp.wait()
+        sums = []
+        for b in range(4):
+            value = stage[slot, b]
+            sbuf[grp, b] = value.astype(BF)
+            sums.append(jnp.sum(value * value, axis=0, keepdims=True))
+        if kind == 0:
+            squares[4 * layer : 4 * layer + 1, :] = sums[0] + sums[1] + sums[2]
+            squares[4 * layer + 1 : 4 * layer + 2, :] = sums[3]
+        else:
+            row = 4 * layer + 1 + kind
+            squares[row : row + 1, :] = sums[0] + sums[1] + sums[2] + sums[3]
+        if grp + 2 < GROUPS:
+            for cp in stage_copies(grp + 2):
+                cp.start()
+
+    for grp in range(2):
+        for cp in stage_copies(grp):
+            cp.start()
+    take(0)
+    greet([gather.x_side, gather.y_side, gather.sibling] + gather.planes)
+    gather.z_send(0)
+
+    vg[z, c] = vecs[...]
+
+    def vec_copy(zz, peer, slot):
+        return pltpu.make_async_remote_copy(
+            src_ref=vg.at[zz, c], dst_ref=vg.at[zz, c], send_sem=vec_sems.at[2 * slot], recv_sem=vec_sems.at[2 * slot + 1],
+            device_id=peer, device_id_type=MESH,
+        )
+
+    def vec_total(slot, count):
+        ref = vg.at[0, pl.ds(0, 1)] if count == 1 else (vg.at[0, pl.ds(0, 2)] if count == 2 else vg.at[pl.ds(0, 2)])
+        pltpu.make_async_copy(ref, ref, vec_sems.at[slot]).wait()
+
+    for k, peer in enumerate(gather.planes):
+        vec_copy(z, peer, k).start()
+    take(1)
+    take(2)
+    take(3)
+    for k in range(3):
+        vec_copy((z + 3 - k) % 4, gather.planes[0], k).wait_recv()
+    for zz in range(4):
+        vec_copy(zz, gather.sibling, 3 + zz).start()
+    gather.z_send(1)
+    take(4)
+    take(5)
+    build_mask(seg, bias)
+    for zz in range(4):
+        vec_copy(zz, gather.sibling, 3 + zz).wait_recv()
+    lane = lax.broadcasted_iota(jnp.int32, (128, 768), 1)
+    spot = lax.broadcasted_iota(jnp.int32, (128, 768), 0)
+    for layer in range(2):
+        acc = jnp.zeros((16, 768), F32)
+        for m in range(8):
+            pick = jnp.where((lane == spot + 96 * m) & (spot < 96), 1.0, 0.0).astype(BF)
+            first = vg[m // 2, m % 2, 16 * layer : 16 * layer + 8, :]
+            rest = [vg[b, m // 4, 16 * layer + 8 + m % 4 : 16 * layer + 9 + m % 4, :] for b in range(4)]
+            left = jnp.concatenate([first] + rest + [jnp.zeros((4, 128), F32)], axis=0)
+            acc = acc + nn(left.astype(BF), pick)
+        vec[layer] = acc
+
+    state = {"sent": 2}
+    started = []
+
+    def save(src, dst):
+        n = len(started)
+        cp = pltpu.make_async_copy(src, dst, out_sems.at[n])
+        cp.start()
+        started.append(cp)
+
+    def load(grp):
+        return pltpu.make_async_copy(whole.at[grp], wv.at[grp % 3], wv_sems.at[grp % 3])
+
+    def event(kind, k):
+        if kind == "z":
+            return
+        if kind == "xy":
+            gather.xy_send(k)
+            if k + 2 < len(PARTS):
+                gather.z_send(k + 2)
+        elif kind == "dg":
+            gather.diagonal_send(k)
+        elif kind == "last":
+            gather.last_send(k)
+        elif kind == "fin":
+            gather.finish(k)
+            grp, first, count = PARTS[k]
+            if first + count == 96:
+                load(grp).start()
+
+    order = forward_plan()
+    pos = 0
+    while pos < len(order):
+        item = order[pos]
+        if item[0] != "run":
+            event(*item)
+            pos += 1
+            continue
+        _, layer, name = item
+        vl = vec.at[layer]
+        x_in = tokens if layer == 0 else x1
+        xb_in = tokens if layer == 0 else xb
+        if name == "joint":
+            load(3 * layer).wait()
+            joint_forward(xb_in, wv.at[0], vl, joint.at[layer])
+            save(joint.at[layer], j_saved.at[layer])
+        elif name.startswith("att"):
+            hooks, first = {}, int(name[3:])
+            p, look = first, pos
+            while True:
+                it = order[look]
+                if it[0] == "run":
+                    if not it[2].startswith("att"):
+                        break
+                    p = int(it[2][3:]) + 1
+                else:
+                    hooks.setdefault(p, []).append(it)
+                look += 1
+            tail = hooks.pop(6, [])
+
+            @pl.loop(0, PAIRS)
+            def _(p):
+                for at, items in hooks.items():
+                    @pl.when(p == at)
+                    def _():
+                        for it in items:
+                            event(*it)
+                attend_forward_pair(p, joint.at[layer], bias, ctx.at[layer], logsum.at[layer])
+
+            for it in tail:
+                event(*it)
+            save(ctx.at[layer], c_saved.at[layer])
+            save(logsum.at[layer], l_saved.at[layer])
+            pos = look
+            continue
+        elif name == "out":
+            out_forward(ctx.at[layer], x_in, wv.at[0, 3], vl, n1.at[layer], r1.at[layer], h, hb)
+            save(n1.at[layer], n1_saved.at[layer])
+            save(r1.at[layer], r1_saved.at[layer])
+        elif name.startswith("up"):
+            b = int(name[2:])
+            if b == 0:
+                load(3 * layer + 1).wait()
+            ffn_up(hb, wv.at[1], vl, g.at[layer], gp.at[layer], b)
+            if b == 3:
+                save(g.at[layer], g_saved.at[layer])
+                save(gp.at[layer], gp_saved.at[layer])
+        else:
+            load(3 * layer + 2).wait()
+            ffn_down(g.at[layer], wv.at[2], vl, h, n2.at[layer], r2.at[layer], x1 if layer == 0 else None, xb if layer == 0 else hb)
+            save(n2.at[layer], n2_saved.at[layer])
+            save(r2.at[layer], r2_saved.at[layer])
+            if layer == 0:
+                save(xb, x_saved)
+            else:
+                save(hb, final)
+        pos += 1
+    save(vec, vec_out)
+    for k in range(len(PARTS)):
+        gather.drain(k)
+    for k in range(3):
+        vec_copy(z, gather.planes[k], k).wait_send()
+    for zz in range(4):
+        vec_copy(zz, gather.sibling, 3 + zz).wait_send()
+    for cp in started:
+        cp.wait()
+
+
+def forward_call(tokens, seg, vecs, joint_w, output_w, expand_w, shrink_w):
+    sd = jax.ShapeDtypeStruct
+    any_spec = pl.BlockSpec(memory_space=pl.ANY)
+    vm = pl.BlockSpec(memory_space=pltpu.VMEM)
+    V = pltpu.VMEM
+    saved = [
+        sd((6, 4, 768, 768), BF),
+        sd((2, 16, 768), F32),
+        sd((T, D), BF),
+        sd((2, 3, T, D), BF),
+        sd((2, T, D), BF),
+        sd((2, 6, 2, T), F32),
+        sd((2, T, D), BF),
+        sd((2, T, 128), F32),
+        sd((2, 4, T, D), BF),
+        sd((2, 4, T, D), BF),
+        sd((2, T, D), BF),
+        sd((2, T, 128), F32),
+        sd((T, D), BF),
+        sd((8, 768), F32),
+    ]
+    scratch = [
+        V((2, 4, 96, 768), F32),
+        V((6, 4, 96, 768), BF),
+        V((3, 4, 768, 768), BF),
+        V((T, T), F32),
+        V((T, D), F32),
+        V((T, D), F32),
+        V((T, D), BF),
+        V((T, D), BF),
+        V((2, 3, T, D), BF),
+        V((2, T, D), BF),
+        V((2, 6, 2, T), F32),
+        V((2, T, D), BF),
+        V((2, T, 128), F32),
+        V((2, 4, T, D), BF),
+        V((2, 4, T, D), BF),
+        V((2, T, D), BF),
+        V((2, T, 128), F32),
+        V((4, 2, 32, 128), F32),
+        V((2, 16, 768), F32),
+        pltpu.SemaphoreType.DMA((len(PARTS), 13)),
+        pltpu.SemaphoreType.DMA((2, 4)),
+        pltpu.SemaphoreType.DMA((3,)),
+        pltpu.SemaphoreType.DMA((14,)),
+        pltpu.SemaphoreType.DMA((24,)),
+    ]
+    return pl.pallas_call(
+        forward_kernel,
+        out_shape=saved,
+        in_specs=[vm, vm, vm] + [any_spec] * 4,
+        out_specs=[any_spec] * 13 + [vm],
+        scratch_shapes=scratch,
+        compiler_params=pltpu.CompilerParams(
+            collective_id=0, has_side_effects=True, vmem_limit_bytes=62 << 20
+        ),
+        name="forward",
+    )(tokens, seg, vecs, joint_w, output_w, expand_w, shrink_w)
+
+
+def pack_vectors(norm_gains, biases, hidden_bias):
+    parts = []
+    for layer in range(2):
+        parts.append(norm_gains[layer])
+        parts.append(biases[layer])
+        parts.append(hidden_bias[layer].reshape(4, 96))
+        parts.append(jnp.zeros((4, 96), F32))
+    rows = jnp.concatenate(parts, axis=0)
+    return jnp.pad(rows, ((0, 0), (0, 32)))
+
+
+def backward_call(dy, xb, seg, whole, layer, vec, saved):
+    joint, ctx, logsum, n1, r1, g, gp, n2, r2 = saved
+
+    def kernel(dy, xb, seg, whole, vec, joint, ctx, logsum, n1, r1, g, gp, n2, r2, dx, ga, ge, gs, sums, bias, du, dob, at, hb, dz, dc, dj):
+        wa, we, ws = whole.at[0], whole.at[1], whole.at[2]
+        build_mask(seg, bias)
+        sums[...] = jnp.zeros_like(sums)
+        norm_backward(dy, n2, r2, vec[1:2, :], du, dob, sums, (1, 7, 6))
+        for b in range(4):
+            ffn_back_block(dob, ws, g, gp, dz, sums, b)
+            transpose_into(g.at[b], at)
+            weight_grad(at, dob, gs.at[b])
+        hb[...] = (n1[...].astype(F32) * vec[0:1, :] + vec[5:6, :]).astype(BF)
+        transpose_into(hb, at)
+        for b in range(4):
+            weight_grad(at, dz.at[b], ge.at[b])
+        ffn_back_input(dz, we, du)
+        norm_backward(du, n1, r1, vec[0:1, :], du, dob, sums, (0, 5, 4))
+        transpose_into(ctx, at)
+        weight_grad(at, dob, ga.at[3])
+        context_back(dob, wa.at[3], dc)
+
+        @pl.loop(0, PAIRS)
+        def _(p):
+            attend_backward_pair(p, joint, bias, logsum, dc, dj)
+
+        transpose_into(xb, at)
+        for b in range(3):
+            weight_grad(at, dj.at[b], ga.at[b])
+        input_back(dj, wa, du, dx, sums)
+
+    sd = jax.ShapeDtypeStruct
+    V = pltpu.VMEM
+    VM = pl.BlockSpec(memory_space=pltpu.VMEM)
+    return pl.pallas_call(
+        kernel,
+        out_shape=[sd((512, 768), F32), sd((4, 768, 768), BF), sd((4, 768, 768), BF), sd((4, 768, 768), BF), sd((16, 768), F32)],
+        in_specs=[VM] * 14,
+        out_specs=[VM] * 5,
+        scratch_shapes=[V((512, 512), F32), V((512, 768), F32), V((512, 768), BF), V((768, 512), BF), V((512, 768), BF), V((4, 512, 768), BF), V((512, 768), BF), V((3, 512, 768), BF)],
+        compiler_params=pltpu.CompilerParams(vmem_limit_bytes=63 << 20),
+        name="backward",
+    )(dy, xb, seg, whole, vec, joint, ctx, logsum, n1, r1, g, gp, n2, r2)
+
+
+def local_kernels(
+    tokens,
+    segments,
+    cotangent,
+    joint_weight,
+    output_weight,
+    expand_weight,
+    shrink_weight,
+    norm_gains,
+    biases,
+    hidden_bias,
+    joint_rows,
+    joint_columns,
+    output_rows,
+    output_columns,
+    expand_rows,
+    expand_columns,
+    shrink_rows,
+    shrink_columns,
+    gain_moments,
+    bias_moments,
+    hidden_moments,
+):
+    row_count, slot_count, features = tokens.shape
+    vecs = pack_vectors(norm_gains, biases, hidden_bias)
+    (whole, vec, x_saved, j_s, c_s, l_s, n1_s, r1_s, g_s, gp_s, n2_s, r2_s, final, squares) = forward_call(
+        tokens[0], segments, vecs, joint_weight, output_weight, expand_weight, shrink_weight
+    )
+    activations = final[None]
+    grad = cotangent[0]
+    blocks, sums_list = [], []
+    for number in (1, 0):
+        saved = (j_s[number], c_s[number], l_s[number], n1_s[number], r1_s[number], g_s[number], gp_s[number], n2_s[number], r2_s[number])
+        grad, ga, ge, gs, sums = backward_call(
+            grad, tokens[0] if number == 0 else x_saved, segments, whole[3 * number : 3 * number + 3], number, vec[number], saved
+        )
+        blocks.append((
+            lax.psum(lax.psum_scatter(ga, "fsdp", scatter_dimension=1, tiled=True), "dp"),
+            lax.psum(lax.psum_scatter(ge, "fsdp", scatter_dimension=1, tiled=True), "dp"),
+            lax.psum(lax.psum_scatter(gs.reshape(3072, 768), "fsdp", scatter_dimension=0, tiled=True), "dp"),
+        ))
+        sums_list.append(sums)
+    sums = lax.psum(jnp.stack(sums_list[::-1]), ("dp", "fsdp"))
+    f = lax.axis_index("fsdp")
+    mine = lax.dynamic_slice_in_dim(sums[:, :8], f * 96, 96, axis=2)
+    hidden_mine = lax.dynamic_slice_in_dim(sums[:, 8:12].reshape(2, 3072), f * 384, 384, axis=1)
+    collected = []
+    for number in range(2):
+        ga, ge, gs = blocks[1 - number]
+        collected.append((
+            ga[:3].transpose(1, 0, 2).reshape(96, 2304).astype(jnp.float32),
+            ga[3].astype(jnp.float32),
+            ge.transpose(1, 0, 2).reshape(96, 3072).astype(jnp.float32),
+            gs.astype(jnp.float32),
+            mine[number, :2],
+            mine[number, 2:8],
+            hidden_mine[number],
+        ))
+    input_gradient = grad.astype(jnp.bfloat16)[None]
+    fsdp_count = lax.axis_size("fsdp")
+    token_total = row_count * slot_count * lax.axis_size("dp") * fsdp_count
+    root_scale = 1.0 / math.sqrt(token_total)
+    stacked_grads = [
+        jnp.stack([entry[index] for entry in collected]) * root_scale for index in range(7)
+    ]
+    matrices = (
+        (stacked_grads[0], joint_weight, joint_rows, joint_columns),
+        (stacked_grads[1], output_weight, output_rows, output_columns),
+        (stacked_grads[2], expand_weight, expand_rows, expand_columns),
+        (stacked_grads[3], shrink_weight, shrink_rows, shrink_columns),
+    )
+    partial_list = [factored_partials(item[0], item[1], item[2]) for item in matrices]
+    vectors = (
+        (stacked_grads[4], norm_gains, gain_moments),
+        (stacked_grads[5], biases, bias_moments),
+        (stacked_grads[6][:, None, :], hidden_bias[:, None, :], hidden_moments[:, None, :]),
+    )
+    vector_list = [vector_partials(item[0], item[2]) for item in vectors]
+    vector_squares = jnp.concatenate(
+        [jnp.sum(item[1] * item[1], axis=2) for item in vectors], axis=1
+    )
+    statistics = lax.psum(
+        (
+            partial_list[0][1],
+            partial_list[1][1],
+            partial_list[2][1],
+            partial_list[3][1],
+            jnp.stack([item[2] for item in partial_list], axis=1),
+            jnp.stack([item[3] for item in partial_list], axis=1),
+            vector_squares,
+        ),
+        "fsdp",
+    )
+    updates = []
+    columns_list = []
+    for index in range(4):
+        gradient = matrices[index][0]
+        total_rows = gradient.shape[1] * fsdp_count
+        rows_next = partial_list[index][0]
+        columns_next = DECAY_RATE * matrices[index][3] + (1.0 - DECAY_RATE) * (
+            statistics[index] / total_rows
+        )
+        row_average = statistics[4][:, index] / total_rows
+        estimate = rows_next[:, :, None] * columns_next[:, None, :] / row_average[:, None, None]
+        updates.append(gradient * lax.rsqrt(estimate))
+        columns_list.append(columns_next)
+    matrix_squares = jnp.stack([jnp.sum(item * item, axis=(1, 2)) for item in updates], axis=1)
+    vector_updates = jnp.concatenate(
+        [jnp.sum(item[1] * item[1], axis=2) for item in vector_list], axis=1
+    )
+    norms = lax.psum((matrix_squares, vector_updates), "fsdp")
+    matrix_next = []
+    for index in range(4):
+        gradient = matrices[index][0]
+        entry_count = gradient.shape[1] * fsdp_count * gradient.shape[2]
+        clip_ratio = jnp.sqrt(norms[0][:, index] / entry_count) / CLIP_LIMIT
+        update = updates[index] / jnp.maximum(clip_ratio, 1.0)[:, None, None]
+        stride = STEP_RATE * jnp.maximum(
+            FLOOR_SCALE, jnp.sqrt(statistics[5][:, index] / entry_count)
+        )
+        matrix_next.append(matrices[index][1] - stride[:, None, None] * update)
+    vector_next = []
+    offset = 0
+    for index in range(3):
+        gradient = vectors[index][0]
+        kinds = gradient.shape[1]
+        entry_count = gradient.shape[2] * fsdp_count
+        clip_ratio = jnp.sqrt(norms[1][:, offset : offset + kinds] / entry_count) / CLIP_LIMIT
+        update = vector_list[index][1] / jnp.maximum(clip_ratio, 1.0)[:, :, None]
+        stride = STEP_RATE * jnp.maximum(
+            FLOOR_SCALE, jnp.sqrt(statistics[6][:, offset : offset + kinds] / entry_count)
+        )
+        vector_next.append(vectors[index][1] - stride[:, :, None] * update)
+        offset = offset + kinds
+    return (
+        activations,
+        input_gradient,
+        stacked_grads[0],
+        stacked_grads[1],
+        stacked_grads[2],
+        stacked_grads[3],
+        stacked_grads[4],
+        stacked_grads[5],
+        stacked_grads[6],
+        matrix_next[0],
+        matrix_next[1],
+        matrix_next[2],
+        matrix_next[3],
+        vector_next[0],
+        vector_next[1],
+        vector_next[2][:, 0, :],
+        matrix_next[0].astype(jnp.bfloat16),
+        matrix_next[1].astype(jnp.bfloat16),
+        matrix_next[2].astype(jnp.bfloat16),
+        matrix_next[3].astype(jnp.bfloat16),
+        partial_list[0][0],
+        columns_list[0],
+        partial_list[1][0],
+        columns_list[1],
+        partial_list[2][0],
+        columns_list[2],
+        partial_list[3][0],
+        columns_list[3],
+        vector_list[0][0],
+        vector_list[1][0],
+        vector_list[2][0][:, 0, :],
+    )
+
+
 def solution(mesh):
     placed = (
         P(("dp", "fsdp"), None, None),
@@ -448,8 +1342,9 @@
         P(None, None, "fsdp"),
         P(None, "fsdp"),
     )
+    known = dict(mesh.shape) == {"dp": 4, "fsdp": 8}
     return jax.shard_map(
-        local,
+        local_kernels if known else local_plain,
         mesh=mesh,
         in_specs=placed,
         out_specs=(

time: 1450 us -> 886 us (0.61)
  waiting for transfers between devices: 821 us -> 414 us
  Pallas kernels: 0 us -> 281 us
  matrix products: 206 us -> 0 us
  blocking collectives: 170 us -> 57.4 us
  other arithmetic: 102 us -> 46.9 us
  local copies, waits for them, and re-layouts: 118 us -> 65.6 us
    pallas_call x0 -> x3, Pallas kernels: none -> 281 us  [the longest x1 149 us: forward_call(): pl.pallas_call(forward_kernel, out_shape=saved, in_specs=[vm, vm, vm] + [...]
    unnamed x27 -> x8, waiting for transfers between devices: 218 us -> 2.98 us
    dot_general x35 -> x0, matrix products: 199 us -> none  [the longest x8 69.8 us: product(): return jnp.dot(left, right, preferred_element_type=jnp.float32)]
    all_gather x8 -> x0, waiting for transfers between devices: 109 us -> none  [the longest x2 49.3 us: local(): lax.all_gather(expand_weight[number].astype(jnp.bfloat16), 'fsdp', axis=0...]
    all_gather x6 -> x0, blocking collectives: 102 us -> none  [the longest x2 42.8 us: local(): lax.all_gather(norm_gains[number].astype(jnp.bfloat16), 'fsdp', axis=1, t...]
    reduce_scatter x6, waiting for transfers between devices: 392 us -> 328 us  [the longest x2 111 us: local_kernels(): lax.psum_scatter(ga, 'fsdp', scatter_dimension=1, tiled=True)]
    unnamed x285 -> x141, local copies, waits for them, and re-layouts: 58.8 us -> 8.3 us
    unnamed x1 -> x0, blocking collectives: 30.6 us -> none
  transfers between devices with their start and end apart: 21 -> 8, of which waited for: 15 -> 7; matrix products, arithmetic and copies ran while one was open for 18% -> 2% of each run, Pallas kernels for 0% -> 0%
where the time goes in v1:
time: 886 us; the launch traced here: 882 us
  waiting for transfers between devices  414 us (47%)
  Pallas kernels  281 us (32%)
  local copies, waits for them, and re-layouts  65.6 us (7%)
  blocking collectives  57.4 us (6%)
  other arithmetic  46.9 us (5%)
  between operations  16.4 us (2%)
    pallas_call x1, Pallas kernels, forward_call(): pl.pallas_call(forward_kernel, out_shape=saved, in_specs=[vm, vm, vm] + [...  149 us
    pallas_call x2, Pallas kernels, backward_call(): pl.pallas_call(kernel, out_shape=[sd((512, 768), F32), sd((4, 768, 768),...  132 us
    reduce_scatter x2, waiting for transfers between devices, local_kernels(): lax.psum_scatter(ga, 'fsdp', scatter_dimension=1, tiled=True)  111 us
    reduce_scatter x2, waiting for transfers between devices, local_kernels(): lax.psum_scatter(gs.reshape(3072, 768), 'fsdp', scatter_dimension=0, tile...  109 us
    reduce_scatter x2, waiting for transfers between devices, local_kernels(): lax.psum_scatter(ge, 'fsdp', scatter_dimension=1, tiled=True)  108 us
    psum x1, waiting for transfers between devices, local_kernels(): lax.psum(lax.psum_scatter(ga, 'fsdp', scatter_dimension=1, tiled=True), '...  82.5 us
    psum x1, blocking collectives, local_kernels(): lax.psum((partial_list[0][1], partial_list[1][1], partial_list[2][1], par...  30.1 us
    psum x1, blocking collectives, local_kernels(): norms = lax.psum((matrix_squares, vector_updates), 'fsdp')  27.3 us
  transfers between devices with their start and end apart: 8, of which 7 were waited for; matrix products, arithmetic and copies ran while one was open for 2% of the time, Pallas kernels for 0%

profile of v1, /device:TPU:0, one launch (start us, length us, event | category | flops | bytes accessed | tf_op | source)
XLA Modules:
  0.0 881.7 jit_solution(17873666059746846202)
XLA Ops:
  11.1 148.9 %forward.1 = (bf16[6,4,768,768]{3,2,1,0:T(8,128)(2,1)}, f32[2,16,768]{2,1,0:T(8,128)}, bf16[512,768]{1,0:T(8,128)(2,1)}, bf16[2,3,512,768]{3,2,1,0:T(8,128)(2,1)...) custom-call(bf16[512,768]{1,0:T(8,128)(2,1)} %bitcast.114, ...), custom_call_target="tpu_custom_call" | custom-call | tf_op jit(solution)/shard_map/forward/pallas_call | solution.py:1083
  160.0 21.1 %fusion.37 = (bf16[3,4,768,768]{3,2,1,0:T(8,128)(2,1)}, bf16[3,4,768,768]{3,2,1,0:T(8,128)(2,1)}) fusion(bf16[6,4,768,768]{3,2,1,0:T(8,128)(2,1)} %get-tuple-element.56), kind=kLoop, calls=%fused_computation.141 | loop fusion | bytes 56623104 | tf_op jit(solution)/shard_map/slice | solution.py:1186
  181.1 3.6 slice_bitcast_fusion
  184.8 1.4 copy-done.8
  186.2 3.5 slice_bitcast_fusion.1
  190.5 2.5 slice_bitcast_fusion.4
  193.0 1.2 slice_bitcast_fusion.6
  194.9 1.2 slice_bitcast_fusion.7
  196.2 1.2 slice_bitcast_fusion.8
  200.4 66.0 %backward.2 = (f32[512,768]{1,0:T(8,128)}, bf16[4,768,768]{2,1,0:T(8,128)(2,1)}, bf16[4,768,768]{2,1,0:T(8,128)(2,1)}, bf16[4,768,768]{2,1,0:T(8,128)(2,1)}, f32[16,768]{1,0:T(8,128)}) custom-call(bf16[512,768]{1,0:T(8,128)(2,1)} %bitcast.116, bf16[512,768]{1,0:T(8,128)(2,1)} %get-tuple-element.55.xb, s32[1,512]{1,0:T(1,128)} %seg.5, ...), custom_call_target="tpu_custom_call" | custom-call | tf_op jit(solution)/shard_map/backward/pallas_call | solution.py:1141
  266.4 66.4 %backward.3 = (f32[512,768]{1,0:T(8,128)}, bf16[4,768,768]{2,1,0:T(8,128)(2,1)}, bf16[4,768,768]{2,1,0:T(8,128)(2,1)}, bf16[4,768,768]{2,1,0:T(8,128)(2,1)}, f32[16,768]{1,0:T(8,128)}) custom-call(f32[512,768]{1,0:T(8,128)} %get-tuple-element.67.dy, bf16[512,768]{1,0:T(8,128)(2,1)} %bitcast.115, s32[1,512]{1,0:T(1,128)} %seg.5, ...), custom_call_target="tpu_custom_call" | custom-call | tf_op jit(solution)/shard_map/backward/pallas_call | solution.py:1141
  337.1 54.6 %reduce-scatter.11.cloned.1.call-done = bf16[4,96,768]{2,1,0:T(8,128)(2,1)} async-done(((bf16[4,768,768]{2,1,0:T(8,128)(2,1)}), bf16[4,96,768]{2,1,0:T(8,128)(2,1)}) %reduce-scatter.11.cloned.1.call-update) | async-done | bytes 589840 | tf_op jit(solution)/shard_map/reduce_scatter | solution.py:1190
  391.6 1.5 copy.121
  393.2 1.2 convert_element_type.85
  394.4 53.7 %reduce-scatter.13.cloned.1.call-done = bf16[4,96,768]{2,1,0:T(8,128)(2,1)} async-done(((bf16[4,768,768]{2,1,0:T(8,128)(2,1)}), bf16[4,96,768]{2,1,0:T(8,128)(2,1)}) %reduce-scatter.13.cloned.1.call-update) | async-done | bytes 589840 | tf_op jit(solution)/shard_map/reduce_scatter | solution.py:1190
  448.1 1.5 copy.122
  449.6 1.2 convert_element_type.87
  450.9 53.5 %reduce-scatter.15.cloned.1.call-done = bf16[384,768]{1,0:T(8,128)(2,1)} async-done(((bf16[3072,768]{1,0:T(8,128)(2,1)}), bf16[384,768]{1,0:T(8,128)(2,1)}) %reduce-scatter.15.cloned.1.call-update) | async-done | bytes 589840 | tf_op jit(solution)/shard_map/reduce_scatter | solution.py:1191
  504.3 55.5 %reduce-scatter.7.cloned.1.call-done = bf16[4,96,768]{2,1,0:T(8,128)(2,1)} async-done(((bf16[4,768,768]{2,1,0:T(8,128)(2,1)}), bf16[4,96,768]{2,1,0:T(8,128)(2,1)}) %reduce-scatter.7.cloned.1.call-update) | async-done | bytes 589840 | tf_op jit(solution)/shard_map/reduce_scatter | solution.py:1189
  559.9 55.4 %reduce-scatter.17.cloned.1.call-done = bf16[384,768]{1,0:T(8,128)(2,1)} async-done(((bf16[3072,768]{1,0:T(8,128)(2,1)}), bf16[384,768]{1,0:T(8,128)(2,1)}) %reduce-scatter.17.cloned.1.call-update) | async-done | bytes 589840 | tf_op jit(solution)/shard_map/reduce_scatter | solution.py:1191
  615.3 55.5 %reduce-scatter.9.cloned.1.call-done = bf16[4,96,768]{2,1,0:T(8,128)(2,1)} async-done(((bf16[4,768,768]{2,1,0:T(8,128)(2,1)}), bf16[4,96,768]{2,1,0:T(8,128)(2,1)}) %reduce-scatter.9.cloned.1.call-update) | async-done | bytes 589840 | tf_op jit(solution)/shard_map/reduce_scatter | solution.py:1189
  671.2 2.0 multiply_reduce_fusion.5
  674.9 1.0 convert_bitcast_fusion
  681.1 82.5 %all-reduce.9.cloned.1.call-done = (bf16[4,96,768]{2,1,0:T(8,128)(2,1)}, bf16[4,96,768]{2,1,0:T(8,128)(2,1)}, bf16[1,96,3072]{2,1,0:T(8,128)(2,1)}, bf16[1,96,30...) async-done(((bf16[4,96,768]{2,1,0:T(8,128)(2,1)}, bf16[4,96,768]{2,1,0:T(8,128)(2,1)}, bf16[1,96,3072]{2,1,0:T(8,128)(2,1)}, ...) | async-done | bytes 3538960 | tf_op jit(solution)/shard_map/psum | solution.py:1189
  764.5 1.0 slice_bitcast_fusion.13
  765.6 0.9 slice.222
  766.5 1.0 slice_bitcast_fusion.12
  769.6 2.2 fusion.4
  771.8 1.2 fusion.2
  773.7 2.6 fusion
  778.3 30.1 %all-reduce.2 = (f32[2,4]{0,1:T(4,128)}, f32[2,768]{1,0:T(2,128)}, f32[2,3072]{1,0:T(2,128)}, f32[2,768]{1,0:T(2,128)}, f32[2,2304]{1,0:T(2,128)}) all-reduce(f32[2,4]{0,1:T(4,128)} %pad_maximum_fusion.4, f32[2,768]{1,0:T(2,128)} %get-tuple-element.234, ...), channel_id=1, replica_groups=mesh['dp'=4,'fsdp'=8] {'fsdp'}, use_global_device_ids=true, to_apply=%region_28.29 | all-reduce | flops 13832 | bytes 110656 | tf_op jit(solution)/shard_map/psum | solution.py:1233
  812.4 2.0 multiply_reduce_fusion.4
  814.4 1.0 multiply_reduce_fusion.6
  817.5 27.3 %all-reduce.1 = (f32[2,4]{0,1:T(4,128)}, f32[2,4]{0,1:T(4,128)}, f32[2,9]{0,1:T(8,128)}, f32[2,9]{0,1:T(8,128)}) all-reduce(f32[2,4]{0,1:T(4,128)} %pad_maximum_fusion.5, f32[2,4]{0,1:T(4,128)} %pad_maximum_fusion.3, f32[2,9]{0,1:T(8,128)} %get-tuple-element.326, ...), channel_id=1, replica_groups=mesh['dp'=4,'fsdp'=8] {'fsdp'}, use_global_device_ids=true, to_apply=%region_39.40 | all-reduce | flops 52 | bytes 416 | tf_op jit(solution)/shard_map/psum | solution.py:1262
  844.9 1.2 fusion.28
  846.1 1.3 fusion.14
  847.4 1.2 fusion.24
  848.6 1.3 fusion.11
  849.9 1.3 fusion.20
  851.1 1.3 fusion.17
  852.4 1.3 copy.129
  853.7 1.3 copy.130
  856.5 1.3 copy.124
  857.8 1.3 copy.128
  860.9 4.3 fusion.29
  865.3 2.5 fusion.30
  867.9 1.2 fusion.31
  869.8 2.0 fusion.32
  (210 shorter events, 36.6 us)
Async XLA Ops:
  8.0 383.6 %reduce-scatter.11.cloned.1.call-start = ((), (), s32[]{:S(2)}) async-start(), calls=%async_computation.8 | async-start | bytes 5308416 | tf_op jit(solution)/shard_map/reduce_scatter | solution.py:1190
  160.0 21.1 %copy-start.9 = (bf16[2,4,512,768]{3,2,1,0:T(8,128)(2,1)S(1)}, bf16[2,4,512,768]{3,2,1,0:T(8,128)(2,1)}, u32[]{:S(2)}) copy-start(bf16[2,4,512,768]{3,2,1,0:T(8,128)(2,1)} %get-tuple-element.64) | copy-start | bytes 18874372
  181.1 5.1 copy-start.8
  181.1 8.6 slice-start
  186.2 4.3 slice-start.1
  196.2 2.9 copy-start.27
  196.2 3.5 copy-start.32
  332.8 115.3 %reduce-scatter.13.cloned.1.call-start = ((), (), s32[]{:S(2)}) async-start(), calls=%async_computation.9 | async-start | bytes 5308416 | tf_op jit(solution)/shard_map/reduce_scatter | solution.py:1190
  333.6 170.8 %reduce-scatter.15.cloned.1.call-start = ((), (), s32[]{:S(2)}) async-start(), calls=%async_computation.10 | async-start | bytes 5308416 | tf_op jit(solution)/shard_map/reduce_scatter | solution.py:1191
  334.3 225.6 %reduce-scatter.7.cloned.1.call-start = ((), (), s32[]{:S(2)}) async-start(), calls=%async_computation.6 | async-start | bytes 5308416 | tf_op jit(solution)/shard_map/reduce_scatter | solution.py:1189
  334.9 280.4 %reduce-scatter.17.cloned.1.call-start = ((), (), s32[]{:S(2)}) async-start(), calls=%async_computation.11 | async-start | bytes 5308416 | tf_op jit(solution)/shard_map/reduce_scatter | solution.py:1191
  335.5 335.3 %reduce-scatter.9.cloned.1.call-start = ((), (), s32[]{:S(2)}) async-start(), calls=%async_computation.7 | async-start | bytes 5308416 | tf_op jit(solution)/shard_map/reduce_scatter | solution.py:1189
  336.0 339.9 %all-reduce.7.cloned.1.call-start = ((), (), s32[]{:S(2)}) async-start(), calls=%async_computation.12 | async-start | bytes 196608 | tf_op jit(solution)/shard_map/psum | solution.py:1194
  337.0 426.6 %all-reduce.9.cloned.1.call-start = ((), (), s32[]{:S(2)}) async-start(), calls=%async_computation.13 | async-start | bytes 7077888 | tf_op jit(solution)/shard_map/psum | solution.py:1189
  449.6 221.2 %copy-start.38 = (f32[2,2,96]{2,1,0:T(2,128)S(1)}, f32[2,2,96]{2,1,0:T(2,128)}, u32[]{:S(2)}) copy-start(f32[2,2,96]{2,1,0:T(2,128)} %param.28) | copy-start | bytes 4612
  449.6 221.4 %copy-start.10 = (f32[2,96,768]{2,1,0:T(8,128)S(1)}, f32[2,96,768]{2,1,0:T(8,128)}, u32[]{:S(2)}) copy-start(f32[2,96,768]{2,1,0:T(8,128)} %output_w.1) | copy-start | bytes 1769476
  673.7 3.0 copy-start.30
  673.7 4.7 copy-start.59
  673.7 6.0 copy-start.58
  769.6 98.3 %copy-start.11 = (f32[2,96,768]{2,1,0:T(8,128)}, f32[2,96,768]{2,1,0:T(8,128)S(1)}, u32[]{:S(2)}) copy-start(f32[2,96,768]{2,1,0:T(8,128)S(1)} %get-tuple-element.361) | copy-start | bytes 1769476
  773.0 87.8 %copy-start = (f32[2,384,768]{2,1,0:T(8,128)}, f32[2,384,768]{2,1,0:T(8,128)S(1)}, u32[]{:S(2)}) copy-start(f32[2,384,768]{2,1,0:T(8,128)S(1)} %get-tuple-element.363) | copy-start | bytes 7077892
  773.0 3.3 copy-start.60
  773.0 4.0 copy-start.61
  773.0 4.0 copy-start.62
  808.4 7.0 copy-start.1
  808.4 7.0 copy-start.42
  809.3 5.1 copy-start.48
  809.3 5.1 copy-start.50
  809.3 6.8 copy-start.52
  809.3 6.8 copy-start.54
  810.8 57.1 %copy-start.28 = (f32[2,768]{1,0:T(2,128)}, f32[2,768]{1,0:T(2,128)S(1)}, u32[]{:S(2)}) copy-start(f32[2,768]{1,0:T(2,128)S(1)} %multiply_add_fusion.7) | copy-start | bytes 18436
  811.6 4.5 copy-start.23
  812.3 3.8 copy-start.31
  812.3 3.8 copy-start.37
  860.8 4.4 copy-start.2
  860.9 4.4 copy-start.5
  860.9 4.4 copy-start.24
  860.9 4.4 copy-start.43
  860.9 4.4 copy-start.53
  865.3 3.8 copy-start.7
  865.3 3.8 copy-start.26
  865.3 3.8 copy-start.45
  865.3 3.8 copy-start.49
  869.7 2.8 copy-start.39
  869.7 2.8 copy-start.46
  869.7 2.8 copy-start.47
  869.7 2.8 copy-start.55
  869.7 3.4 copy-start.16
  (27 other events, 54.1 us)
Sparse Core Ops, SparseCore 0:
  332.9 58.6 reduce-scatter.10
  393.9 54.0 reduce-scatter.12
  450.4 53.8 reduce-scatter.14
  506.5 53.3 reduce-scatter.6
  562.0 53.1 reduce-scatter.16
  617.4 53.3 reduce-scatter.8
Sparse Core Ops, SparseCore 1:
  342.7 174.5 all-reduce.6
  670.9 92.7 all-reduce.8

commit v2 on v1

--- a/solution.py
+++ b/solution.py
@@ -595,7 +595,7 @@
         out[r, :] = nn(at[r, :], bmat[...]).astype(BF)
 
 
-def ffn_back_block(dob, ws, g, gp, dz, sums, b, tile=128):
+def ffn_back_block(dob, ws, gp, dz, sums, b, tile=128):
     def step(i, acc):
         r = rows_at(i, tile)
         v = (nt(dob[r, :], ws[b]) * gp[b, r, :].astype(F32)).astype(BF)
@@ -1104,49 +1104,453 @@
     return jnp.pad(rows, ((0, 0), (0, 32)))
 
 
-def backward_call(dy, xb, seg, whole, layer, vec, saved):
-    joint, ctx, logsum, n1, r1, g, gp, n2, r2 = saved
-
-    def kernel(dy, xb, seg, whole, vec, joint, ctx, logsum, n1, r1, g, gp, n2, r2, dx, ga, ge, gs, sums, bias, du, dob, at, hb, dz, dc, dj):
-        wa, we, ws = whole.at[0], whole.at[1], whole.at[2]
-        build_mask(seg, bias)
-        sums[...] = jnp.zeros_like(sums)
-        norm_backward(dy, n2, r2, vec[1:2, :], du, dob, sums, (1, 7, 6))
-        for b in range(4):
-            ffn_back_block(dob, ws, g, gp, dz, sums, b)
-            transpose_into(g.at[b], at)
-            weight_grad(at, dob, gs.at[b])
-        hb[...] = (n1[...].astype(F32) * vec[0:1, :] + vec[5:6, :]).astype(BF)
-        transpose_into(hb, at)
-        for b in range(4):
-            weight_grad(at, dz.at[b], ge.at[b])
-        ffn_back_input(dz, we, du)
-        norm_backward(du, n1, r1, vec[0:1, :], du, dob, sums, (0, 5, 4))
-        transpose_into(ctx, at)
-        weight_grad(at, dob, ga.at[3])
-        context_back(dob, wa.at[3], dc)
+BACK_UNITS = (
+    (("ln2", 3.5),)
+    + tuple((f"s{i}", 2.0) for i in range(4))
+    + tuple((f"dz{i}", 2.0) for i in range(4))
+    + (("ht", 1.2), ("e0", 3.5), ("e1", 3.5), ("dh", 4.5), ("ln1", 3.5), ("o", 3.5))
+    + tuple((f"att{p}", 2.6) for p in range(6))
+    + (("xt", 0.8), ("q0", 2.8), ("q1", 2.8), ("dx", 3.5))
+)
+GROUP_OF = {"s": 0, "e": 1, "o": 2, "q": 2}
+PARTS_OF = {"s0": (0,), "s1": (1,), "s2": (2,), "s3": (3,), "e0": (0, 1), "e1": (2, 3), "q0": (0, 1), "q1": (2, 3)}
+
+
+def backward_plan():
+    now, xy_free, z_free, core_free = 0.0, 0.0, 0.0, 0.0
+    pending, order, summed = [], [], set()
+
+    def emit(entry):
+        nonlocal now, xy_free, z_free
+        ready, name, t, zz = entry
+        now = max(now, ready) + 0.4
+        order.append((name, t, zz))
+        if name == "xy1":
+            xy_free = max(xy_free, now) + 3.2
+            pending.append((xy_free + 1.5, "xy2", t, zz))
+        elif name == "xy2":
+            xy_free = max(xy_free, now) + 1.6
+            pending.append((xy_free + 1.5, "z", t, zz))
+        elif name == "z":
+            z_free = max(z_free, now) + 3.2
+            if sum(1 for o in order if o[0] == "z" and o[1] == t) == 4:
+                pending.append((z_free + 1.5, "sum", t, 0))
+        elif name == "sum":
+            summed.add(t)
+            xy_free = max(xy_free, now) + 3.2
+            pending.append((xy_free + 1.5, "ag", t, 0))
+        elif name == "ag":
+            xy_free = max(xy_free, now) + 1.6
+            pending.append((xy_free + 1.5, "fin", t, 0))
+
+    def step(limit):
+        pending.sort()
+        if pending and pending[0][0] <= limit:
+            emit(pending.pop(0))
+            return True
+        return False
+
+    for layer in (1, 0):
+        for name, cost in BACK_UNITS:
+            while step(now):
+                pass
+            if name[0] in GROUP_OF and name != "ln2":
+                t = 3 * (1 - layer) + GROUP_OF[name[0]]
+                while t >= 3 and t - 3 not in summed:
+                    step(1e9)
+            order.append(("run", layer, name))
+            now += cost
+            for zz in PARTS_OF.get(name, ()):
+                core_free = max(core_free, now) + 1.0
+                pending.append((core_free + 1.5, "xy1", 3 * (1 - layer) + GROUP_OF[name[0]], zz))
+    while step(1e9):
+        pass
+    return order
+
+
+class Reduce:
+    def __init__(self, gb, rc, rx1, ry1, rx2, ry2, rz, fin, sems, group_sems, credits):
+        self.gb, self.rc, self.rx1, self.ry1, self.rx2, self.ry2, self.rz, self.fin = gb, rc, rx1, ry1, rx2, ry2, rz, fin
+        self.sems, self.group_sems, self.credits = sems, group_sems, credits
+        q, z, c, self.x_side, self.y_side, self.sibling, self.planes = place()
+        self.q, self.z, self.c = q, z, c
+        self.ax, self.ay = q % 2, q // 2
+
+    def send(self, src, dst, sem, peer):
+        pltpu.make_async_remote_copy(
+            src_ref=src, dst_ref=dst, send_sem=sem[0], recv_sem=sem[1], device_id=peer, device_id_type=MESH
+        ).start()
+
+    def pair(self, t, zz, slot):
+        return self.sems.at[4 * t + zz, 2 * slot], self.sems.at[4 * t + zz, 2 * slot + 1]
+
+    def group_pair(self, t, slot):
+        return self.group_sems.at[t, 2 * slot], self.group_sems.at[t, 2 * slot + 1]
+
+    def wait(self, ref, sem):
+        pltpu.make_async_copy(ref, ref, sem).wait()
+
+    def credit_wait(self, t, phase, zz):
+        if t > 0:
+            pl.semaphore_wait(self.credits.at[phase, zz], 1)
+
+    def credit_give(self, t, phase, zz, peer):
+        if t < 5:
+            pl.semaphore_signal(self.credits.at[phase, zz], inc=1, device_id=peer, device_id_type=MESH)
+
+    def core_send(self, t, zz):
+        self.credit_wait(t, 0, zz)
+        self.send(self.gb.at[t % 3, :, :, zz, 1 - self.c], self.rc.at[zz], self.pair(t, zz, 0), self.sibling)
+
+    def add(self, ref, other):
+        ref[...] = (ref[...].astype(F32) + other[...].astype(F32)).astype(BF)
+
+    def xy1(self, t, zz):
+        gb, c = self.gb.at[t % 3], self.c
+        self.wait(self.rc.at[0], self.pair(t, zz, 0)[1])
+        for by in range(2):
+            for bx in range(2):
+                self.add(gb.at[by, bx, zz, c], self.rc.at[zz, by, bx])
+        self.credit_give(t, 0, zz, self.sibling)
+        self.credit_wait(t, 1, zz)
+        self.send(gb.at[:, 1 - self.ax, zz, c, pl.ds(0, 48)], self.rx1.at[zz], self.pair(t, zz, 1), self.x_side)
+        self.credit_wait(t, 2, zz)
+        self.send(gb.at[1 - self.ay, :, zz, c, pl.ds(48, 48)], self.ry1.at[zz], self.pair(t, zz, 2), self.y_side)
+
+    def xy2(self, t, zz):
+        gb, c = self.gb.at[t % 3], self.c
+        self.wait(self.rx1.at[0], self.pair(t, zz, 1)[1])
+        self.wait(self.ry1.at[0], self.pair(t, zz, 2)[1])
+        for k in range(2):
+            self.add(gb.at[k, self.ax, zz, c, pl.ds(0, 48)], self.rx1.at[zz, k])
+            self.add(gb.at[self.ay, k, zz, c, pl.ds(48, 48)], self.ry1.at[zz, k])
+        self.credit_give(t, 1, zz, self.x_side)
+        self.credit_give(t, 2, zz, self.y_side)
+        self.credit_wait(t, 3, zz)
+        self.send(gb.at[self.ay, 1 - self.ax, zz, c, pl.ds(48, 48)], self.rx2.at[zz], self.pair(t, zz, 3), self.x_side)
+        self.credit_wait(t, 4, zz)
+        self.send(gb.at[1 - self.ay, self.ax, zz, c, pl.ds(0, 48)], self.ry2.at[zz], self.pair(t, zz, 4), self.y_side)
+
+    def z_send(self, t, zz):
+        gb, c = self.gb.at[t % 3], self.c
+        self.wait(self.rx2.at[0], self.pair(t, zz, 3)[1])
+        self.wait(self.ry2.at[0], self.pair(t, zz, 4)[1])
+        self.add(gb.at[self.ay, self.ax, zz, c, pl.ds(48, 48)], self.rx2.at[zz])
+        self.add(gb.at[self.ay, self.ax, zz, c, pl.ds(0, 48)], self.ry2.at[zz])
+        self.credit_give(t, 3, zz, self.x_side)
+        self.credit_give(t, 4, zz, self.y_side)
+
+        @pl.when(self.z != zz)
+        def _():
+            self.send(
+                gb.at[self.ay, self.ax, zz, c], self.rz.at[t, (self.z + 3 - zz) % 4], self.group_pair(t, 0),
+                (self.q, 2 * zz + c),
+            )
+
+    def total(self, t):
+        gb, c = self.gb.at[t % 3], self.c
+        self.wait(self.rz.at[0], self.group_pair(t, 0)[1])
+        own = gb[self.ay, self.ax, self.z, c].astype(F32)
+        for k in range(3):
+            own = own + self.rz[t, k].astype(F32)
+        self.fin[t, self.q] = own.astype(BF)
+        spot = self.fin.at[t, self.q]
+        self.send(spot, spot, self.group_pair(t, 1), self.x_side)
+        self.send(spot, spot, self.group_pair(t, 2), self.y_side)
+
+    def share(self, t):
+        self.wait(self.fin.at[0, 0], self.group_pair(t, 1)[1])
+        self.wait(self.fin.at[0, 0], self.group_pair(t, 2)[1])
+        qx = self.q + 1 - 2 * self.ax
+        qy = (self.q + 2) % 4
+        spot = self.fin.at[t, qy, pl.ds(0, 48)]
+        self.send(spot, spot, self.group_pair(t, 3), self.x_side)
+        spot = self.fin.at[t, qx, pl.ds(48, 48)]
+        self.send(spot, spot, self.group_pair(t, 4), self.y_side)
+
+    def finish(self, t):
+        self.wait(self.fin.at[0, 0, pl.ds(0, 48)], self.group_pair(t, 3)[1])
+        self.wait(self.fin.at[0, 0, pl.ds(0, 48)], self.group_pair(t, 4)[1])
+
+    def drain(self, t):
+        for zz in range(4):
+            self.wait(self.rc.at[0], self.pair(t, zz, 0)[0])
+            self.wait(self.rx1.at[0], self.pair(t, zz, 1)[0])
+            self.wait(self.ry1.at[0], self.pair(t, zz, 2)[0])
+            self.wait(self.rx2.at[0], self.pair(t, zz, 3)[0])
+            self.wait(self.ry2.at[0], self.pair(t, zz, 4)[0])
+        self.wait(self.rz.at[0], self.group_pair(t, 0)[0])
+
+    def drain_share(self, t):
+        self.wait(self.fin.at[0, 0], self.group_pair(t, 1)[0])
+        self.wait(self.fin.at[0, 0], self.group_pair(t, 2)[0])
+        self.wait(self.fin.at[0, 0, pl.ds(0, 48)], self.group_pair(t, 3)[0])
+        self.wait(self.fin.at[0, 0, pl.ds(0, 48)], self.group_pair(t, 4)[0])
+
+
+def backward_kernel(
+    cot, seg, vec, tokens, x_saved, whole, j_saved, c_saved, l_saved, n1_saved, r1_saved, g_saved, gp_saved, n2_saved, r2_saved,
+    fin, total, grad_in,
+    gb, rc, rx1, ry1, rx2, ry2, rz, wv, g, dz, dj, ctx, n1, n2, r1, r2, logsum, xb, dob, at, hb, bias, du, sums, vr, va,
+    sems, group_sems, credits, load_sems, vec_sems,
+):
+    red = Reduce(gb, rc, rx1, ry1, rx2, ry2, rz, fin, sems, group_sems, credits)
+    q, z, c = red.q, red.z, red.c
+    sources = {
+        "n2": (n2_saved, n2), "r2": (r2_saved, r2), "g": (g_saved, g), "dz": (gp_saved, dz), "n1": (n1_saved, n1),
+        "r1": (r1_saved, r1), "ctx": (c_saved, ctx), "dj": (j_saved, dj), "logsum": (l_saved, logsum), "xb": (None, xb),
+    }
+    names = list(sources)
+
+    def load(name, layer):
+        src, dst = sources[name]
+        if name == "xb":
+            src = x_saved if layer == 1 else tokens
+        else:
+            src = src.at[layer]
+        return pltpu.make_async_copy(src, dst, load_sems.at[names.index(name)])
+
+    def weights(t):
+        layer, kind = 1 - t // 3, (2, 1, 0)[t % 3]
+        return pltpu.make_async_copy(whole.at[3 * layer + kind], wv.at[t % 2], load_sems.at[10 + t % 2])
+
+    def need(layer, *which):
+        for name in which:
+            load(name, layer).wait()
+
+    def release(layer, *which):
+        if layer == 1:
+            for name in which:
+                load(name, 0).start()
+
+    def next_weights(t):
+        if t + 2 < 6:
+            weights(t + 2).start()
+
+    for name in ("n2", "r2", "g"):
+        load(name, 1).start()
+    weights(0).start()
+    load("dz", 1).start()
+    weights(1).start()
+    for name in ("n1", "r1", "ctx", "dj", "logsum", "xb"):
+        load(name, 1).start()
+    build_mask(seg, bias)
+    sums[...] = jnp.zeros_like(sums)
+    greet([red.x_side, red.y_side, red.sibling] + red.planes)
+
+    def blocks_pair(slot, b, pair, left):
+        out = nn(at[pl.ds(384 * pair, 384), :], left).astype(BF)
+        gb[slot, b // 2, b % 2, pl.ds(2 * pair, 2)] = out.reshape(2, 2, 96, 768)
+
+    def unit(layer, name):
+        base = 3 * (1 - layer)
+        vl, sl = vec.at[layer], sums.at[layer]
+        if name == "ln2":
+            need(layer, "n2", "r2")
+            norm_backward(cot if layer == 1 else du, n2, r2, vl[1:2, :], du, dob, sl, (1, 7, 6))
+            release(layer, "n2", "r2")
+        elif name[0] == "s":
+            zz = int(name[1])
+            if zz == 0:
+                need(layer, "g")
+                if base >= 3:
+                    red.drain(base - 3)
+            transpose_into(g.at[zz], at)
+            for cc in range(2):
+                out = nn(at[pl.ds(384 * cc, 384), :], dob[...]).astype(BF)
+                gb[base % 3, :, :, zz, cc] = out.reshape(2, 2, 96, 768)
+            red.core_send(base, zz)
+            if zz == 3:
+                release(layer, "g")
+        elif name.startswith("dz"):
+            b = int(name[2])
+            if b == 0:
+                need(layer, "dz")
+                weights(base).wait()
+            ffn_back_block(dob, wv.at[base % 2], dz, dz, sl, b)
+            if b == 3:
+                next_weights(base)
+        elif name == "ht":
+            need(layer, "n1", "r1")
+            hb[...] = (n1[...].astype(F32) * vl[0:1, :] + vl[5:6, :]).astype(BF)
+            transpose_into(hb, at)
+        elif name[0] == "e":
+            pair = int(name[1])
+            if pair == 0 and base >= 3:
+                red.drain(base - 2)
+            for b in range(4):
+                blocks_pair((base + 1) % 3, b, pair, dz[b])
+            for zz in (2 * pair, 2 * pair + 1):
+                red.core_send(base + 1, zz)
+        elif name == "dh":
+            weights(base + 1).wait()
+            ffn_back_input(dz, wv.at[(base + 1) % 2], du)
+            release(layer, "dz")
+            next_weights(base + 1)
+        elif name == "ln1":
+            norm_backward(du, n1, r1, vl[0:1, :], du, dob, sl, (0, 5, 4))
+            release(layer, "n1", "r1")
+        elif name == "o":
+            need(layer, "ctx")
+            weights(base + 2).wait()
+            if base >= 3:
+                red.drain(base - 1)
+            transpose_into(ctx, at)
+            for pair in range(2):
+                blocks_pair((base + 2) % 3, 3, pair, dob[...])
+            context_back(dob, wv.at[(base + 2) % 2, 3], hb)
+            release(layer, "ctx")
+        elif name == "xt":
+            need(layer, "xb")
+            transpose_into(xb, at)
+            release(layer, "xb", "logsum")
+        elif name[0] == "q":
+            pair = int(name[1])
+            for b in range(3):
+                blocks_pair((base + 2) % 3, b, pair, dj[b])
+            for zz in (2 * pair, 2 * pair + 1):
+                red.core_send(base + 2, zz)
+        elif name == "dx":
+            input_back(dj, wv.at[(base + 2) % 2], du, du, sl)
+            release(layer, "dj")
+            next_weights(base + 2)
+
+    def event(name, t, zz):
+        if name == "xy1":
+            red.xy1(t, zz)
+        elif name == "xy2":
+            red.xy2(t, zz)
+        elif name == "z":
+            red.z_send(t, zz)
+        elif name == "sum":
+            red.total(t)
+        elif name == "ag":
+            red.share(t)
+        else:
+            red.finish(t)
+
+    def vec_copy(src, dst, k, peer):
+        return pltpu.make_async_remote_copy(
+            src_ref=src, dst_ref=dst, send_sem=vec_sems.at[2 * k], recv_sem=vec_sems.at[2 * k + 1],
+            device_id=peer, device_id_type=MESH,
+        )
+
+    def vec_hop(k, src, peer, out):
+        cp = vec_copy(src, vr.at[k], k, peer)
+        cp.start()
+        cp.wait()
+        out[...] = src[...] + vr[k]
+
+    order = backward_plan()
+    pos = 0
+    done_units = False
+    while pos < len(order):
+        item = order[pos]
+        if item[0] != "run":
+            event(*item)
+            pos += 1
+            continue
+        _, layer, name = item
+        if not name.startswith("att"):
+            unit(layer, name)
+            pos += 1
+            continue
+        hooks, look, p = {}, pos, 0
+        while True:
+            it = order[look]
+            if it[0] == "run":
+                if not it[2].startswith("att"):
+                    break
+                p = int(it[2][3:]) + 1
+            else:
+                hooks.setdefault(p, []).append(it)
+            look += 1
+        tail = hooks.pop(6, [])
+        need(layer, "dj", "logsum")
 
         @pl.loop(0, PAIRS)
         def _(p):
-            attend_backward_pair(p, joint, bias, logsum, dc, dj)
-
-        transpose_into(xb, at)
-        for b in range(3):
-            weight_grad(at, dj.at[b], ga.at[b])
-        input_back(dj, wa, du, dx, sums)
-
+            for at_pair, items in hooks.items():
+                @pl.when(p == at_pair)
+                def _():
+                    for it in items:
+                        event(*it)
+            attend_backward_pair(p, dj, bias, logsum, hb, dj)
+
+        for it in tail:
+            event(*it)
+        pos = look
+
+    grad_in[...] = du[...].astype(BF)
+    vec_hop(0, sums, red.sibling, va.at[0])
+    vec_hop(1, va.at[0], red.x_side, va.at[1])
+    vec_hop(2, va.at[1], red.y_side, va.at[2])
+    for k, peer in enumerate(red.planes):
+        vec_copy(va.at[2], vr.at[3 + k], 3 + k, peer).start()
+    for k, peer in enumerate(red.planes):
+        vec_copy(va.at[2], vr.at[3 + k], 3 + k, peer).wait()
+    acc = jnp.zeros((2, 16, 768), F32)
+    for plane in range(4):
+        part = jnp.where(z == plane, va[2], 0.0)
+        for k in range(3):
+            part = jnp.where((z + 3 - k) % 4 == plane, vr[3 + k], part)
+        acc = acc + part
+    total[...] = acc
+    for t in range(3, 6):
+        red.drain(t)
+    for t in range(6):
+        red.drain_share(t)
+
+
+def backward_call(cot, seg, vec, tokens, x_saved, whole, j_s, c_s, l_s, n1_s, r1_s, g_s, gp_s, n2_s, r2_s):
     sd = jax.ShapeDtypeStruct
+    any_spec = pl.BlockSpec(memory_space=pl.ANY)
+    vm = pl.BlockSpec(memory_space=pltpu.VMEM)
     V = pltpu.VMEM
-    VM = pl.BlockSpec(memory_space=pltpu.VMEM)
+    dma = pltpu.SemaphoreType.DMA
     return pl.pallas_call(
-        kernel,
-        out_shape=[sd((512, 768), F32), sd((4, 768, 768), BF), sd((4, 768, 768), BF), sd((4, 768, 768), BF), sd((16, 768), F32)],
-        in_specs=[VM] * 14,
-        out_specs=[VM] * 5,
-        scratch_shapes=[V((512, 512), F32), V((512, 768), F32), V((512, 768), BF), V((768, 512), BF), V((512, 768), BF), V((4, 512, 768), BF), V((512, 768), BF), V((3, 512, 768), BF)],
-        compiler_params=pltpu.CompilerParams(vmem_limit_bytes=63 << 20),
+        backward_kernel,
+        out_shape=[sd((6, 4, 96, 768), BF), sd((2, 16, 768), F32), sd((T, D), BF)],
+        in_specs=[vm, vm, vm] + [any_spec] * 12,
+        out_specs=[vm] * 3,
+        scratch_shapes=[
+            V((3, 2, 2, 4, 2, 96, 768), BF),
+            V((4, 2, 2, 96, 768), BF),
+            V((4, 2, 48, 768), BF),
+            V((4, 2, 48, 768), BF),
+            V((4, 48, 768), BF),
+            V((4, 48, 768), BF),
+            V((6, 3, 96, 768), BF),
+            V((2, 4, 768, 768), BF),
+            V((4, T, D), BF),
+            V((4, T, D), BF),
+            V((3, T, D), BF),
+            V((T, D), BF),
+            V((T, D), BF),
+            V((T, D), BF),
+            V((T, 128), F32),
+            V((T, 128), F32),
+            V((6, 2, T), F32),
+            V((T, D), BF),
+            V((T, D), BF),
+            V((D, T), BF),
+            V((T, D), BF),
+            V((T, T), F32),
+            V((T, D), F32),
+            V((2, 16, 768), F32),
+            V((6, 2, 16, 768), F32),
+            V((3, 2, 16, 768), F32),
+            dma((24, 10)),
+            dma((6, 10)),
+            pltpu.SemaphoreType.REGULAR((5, 4)),
+            dma((12,)),
+            dma((12,)),
+        ],
+        compiler_params=pltpu.CompilerParams(
+            collective_id=1, has_side_effects=True, vmem_limit_bytes=63 << 20
+        ),
         name="backward",
-    )(dy, xb, seg, whole, vec, joint, ctx, logsum, n1, r1, g, gp, n2, r2)
+    )(cot, seg, vec, tokens, x_saved, whole, j_s, c_s, l_s, n1_s, r1_s, g_s, gp_s, n2_s, r2_s)
 
 
 def local_kernels(
@@ -1178,36 +1582,25 @@
         tokens[0], segments, vecs, joint_weight, output_weight, expand_weight, shrink_weight
     )
     activations = final[None]
-    grad = cotangent[0]
-    blocks, sums_list = [], []
-    for number in (1, 0):
-        saved = (j_s[number], c_s[number], l_s[number], n1_s[number], r1_s[number], g_s[number], gp_s[number], n2_s[number], r2_s[number])
-        grad, ga, ge, gs, sums = backward_call(
-            grad, tokens[0] if number == 0 else x_saved, segments, whole[3 * number : 3 * number + 3], number, vec[number], saved
-        )
-        blocks.append((
-            lax.psum(lax.psum_scatter(ga, "fsdp", scatter_dimension=1, tiled=True), "dp"),
-            lax.psum(lax.psum_scatter(ge, "fsdp", scatter_dimension=1, tiled=True), "dp"),
-            lax.psum(lax.psum_scatter(gs.reshape(3072, 768), "fsdp", scatter_dimension=0, tiled=True), "dp"),
-        ))
-        sums_list.append(sums)
-    sums = lax.psum(jnp.stack(sums_list[::-1]), ("dp", "fsdp"))
+    blocks, sums, grad = backward_call(
+        cotangent[0], segments, vec, tokens[0], x_saved, whole, j_s, c_s, l_s, n1_s, r1_s, g_s, gp_s, n2_s, r2_s
+    )
     f = lax.axis_index("fsdp")
     mine = lax.dynamic_slice_in_dim(sums[:, :8], f * 96, 96, axis=2)
     hidden_mine = lax.dynamic_slice_in_dim(sums[:, 8:12].reshape(2, 3072), f * 384, 384, axis=1)
     collected = []
     for number in range(2):
-        ga, ge, gs = blocks[1 - number]
+        gs, ge, ga = blocks[3 * (1 - number)], blocks[3 * (1 - number) + 1], blocks[3 * (1 - number) + 2]
         collected.append((
             ga[:3].transpose(1, 0, 2).reshape(96, 2304).astype(jnp.float32),
             ga[3].astype(jnp.float32),
             ge.transpose(1, 0, 2).reshape(96, 3072).astype(jnp.float32),
-            gs.astype(jnp.float32),
+            gs.reshape(384, 768).astype(jnp.float32),
             mine[number, :2],
             mine[number, 2:8],
             hidden_mine[number],
         ))
-    input_gradient = grad.astype(jnp.bfloat16)[None]
+    input_gradient = grad[None]
     fsdp_count = lax.axis_size("fsdp")
     token_total = row_count * slot_count * lax.axis_size("dp") * fsdp_count
     root_scale = 1.0 / math.sqrt(token_total)

time: 886 us -> 483 us (0.55)
  waiting for transfers between devices: 414 us -> 0 us
  Pallas kernels: 281 us -> 360 us
  local copies, waits for them, and re-layouts: 65.6 us -> 22.2 us
  between operations: 16.4 us -> 1.49 us
    reduce_scatter x6 -> x0, waiting for transfers between devices: 328 us -> none  [the longest x2 111 us: local_kernels(): lax.psum_scatter(ga, 'fsdp', scatter_dimension=1, tiled=True)]
    psum x2 -> x0, waiting for transfers between devices: 82.5 us -> none  [the longest x1 82.5 us: local_kernels(): lax.psum(lax.psum_scatter(ga, 'fsdp', scatter_dimension=1, tiled=True), '...]
    pallas_call x2 -> x1, Pallas kernels: 132 us -> 211 us  [backward_call(): pl.pallas_call(backward_kernel, out_shape=[sd((6, 4, 96, 768), BF), sd((2...]
    slice x3 -> x1, local copies, waits for them, and re-layouts: 23 us -> 1 us  [local_kernels(): blocks[3 * (1 - number)]]
    squeeze x10 -> x0, local copies, waits for them, and re-layouts: 16.2 us -> none  [the longest x1 3.61 us: local_kernels(): gp_s[number]]
  transfers between devices with their start and end apart: 8 -> 0, of which waited for: 7 -> 0; matrix products, arithmetic and copies ran while one was open for 2% -> 0% of each run, Pallas kernels for 0% -> 0%
where the time goes in v2:
time: 483 us; the launch traced here: 480 us
  Pallas kernels  360 us (75%)
  blocking collectives  54.9 us (11%)
  other arithmetic  40.6 us (8%)
  local copies, waits for them, and re-layouts  22.2 us (5%)
    pallas_call x1, Pallas kernels, backward_call(): pl.pallas_call(backward_kernel, out_shape=[sd((6, 4, 96, 768), BF), sd((2...  211 us
    pallas_call x1, Pallas kernels, forward_call(): pl.pallas_call(forward_kernel, out_shape=saved, in_specs=[vm, vm, vm] + [...  149 us
    psum x1, blocking collectives, local_kernels(): lax.psum((partial_list[0][1], partial_list[1][1], partial_list[2][1], par...  27.8 us
    psum x1, blocking collectives, local_kernels(): norms = lax.psum((matrix_squares, vector_updates), 'fsdp')  27.2 us

profile of v2, /device:TPU:0, one launch (start us, length us, event | category | flops | bytes accessed | tf_op | source)
XLA Modules:
  0.0 479.5 jit_solution(12140521572360312931)
XLA Ops:
  0.7 0.7 slice_bitcast_fusion.9
  1.4 0.7 copy.117
  2.1 0.8 slice_reduce_fusion
  3.1 0.6 pad.4.vecs
  3.7 149.0 %forward.1 = (bf16[6,4,768,768]{3,2,1,0:T(8,128)(2,1)}, f32[2,16,768]{2,1,0:T(8,128)}, bf16[512,768]{1,0:T(8,128)(2,1)}, bf16[2,3,512,768]{3,2,1,0:T(8,128)(2,1)...) custom-call(bf16[512,768]{1,0:T(8,128)(2,1)} %bitcast.79, ...), custom_call_target="tpu_custom_call" | custom-call | tf_op jit(solution)/shard_map/forward/pallas_call | solution.py:1083
  152.7 211.3 %backward.1 = (bf16[6,4,96,768]{3,2,1,0:T(8,128)(2,1)}, f32[2,16,768]{2,1,0:T(8,128)}, bf16[512,768]{1,0:T(8,128)(2,1)}) custom-call(bf16[512,768]{1,0:T(8,128)(2,1)} %bitcast.85, s32[1,512]{1,0:T(1,128)} %seg.3, f32[2,16,768]{2,1,0:T(8,128)} %get-tuple-element.48.vec, bf16[512,768]{1,0:T(8,128)(2,1)} %bitcast.80, ...), custom_call_target="tpu_custom_call" | custom-call | tf_op jit(solution)/shard_map/backward/pallas_call | solution.py:1511
  364.0 1.2 slice_bitcast_fusion.3
  367.1 2.2 fusion.4
  369.3 1.0 slice_bitcast_fusion.5
  370.3 0.8 fusion.6
  371.1 1.0 fusion.37
  372.5 1.2 convert_element_type.139
  374.2 1.2 convert_element_type.136
  375.5 2.8 fusion
  378.3 2.8 fusion.2
  381.1 1.2 multiply_reduce_fusion.12
  382.3 0.7 fusion.8
  383.6 0.8 slice_bitcast_fusion.6
  384.4 1.9 multiply_reduce_fusion.10
  386.3 0.8 fusion.36
  387.2 0.8 fusion.35
  388.0 0.9 fusion.33
  388.9 27.8 %all-reduce.2 = (f32[2,4]{0,1:T(4,128)S(1)}, f32[2,768]{1,0:T(2,128)S(1)}, f32[2,3072]{1,0:T(2,128)S(1)}, f32[2,768]{1,0:T(2,128)S(1)}, f32[2,2304]{1,0:T(2,128)S(1)}) all-reduce(f32[2,4]{0,1:T(4,128)S(1)} %pad_maximum_fusion.3, f32[2,768]{1,0:T(2,128)} %get-tuple-element.220, ...), channel_id=1, replica_groups=mesh['dp'=4,'fsdp'=8] {'fsdp'}, use_global_device_ids=true, to_apply=%region_15.16 | all-reduce | flops 13832 | bytes 110656 | tf_op jit(solution)/shard_map/psum | solution.py:1626
  416.7 0.7 multiply_add_fusion.6
  417.5 2.5 multiply_reduce_fusion
  420.1 0.7 multiply_reduce_fusion.1
  421.2 0.7 multiply_reduce_fusion.4
  425.1 0.6 multiply_reduce_fusion.11
  425.8 0.7 multiply_reduce_fusion.9
  426.4 0.6 multiply_reduce_fusion.13
  427.1 1.3 copy.123
  428.4 1.3 multiply_reduce_fusion.8
  429.8 1.4 copy.127
  431.1 1.3 copy.126
  432.4 1.4 pad_maximum_fusion
  433.8 27.2 %all-reduce.1 = (f32[2,4]{0,1:T(4,128)}, f32[2,4]{0,1:T(4,128)}, f32[2,9]{0,1:T(8,128)}, f32[2,9]{0,1:T(8,128)}) all-reduce(f32[2,4]{0,1:T(4,128)} %pad_maximum_fusion.4, f32[2,4]{0,1:T(4,128)} %pad_maximum_fusion.2, f32[2,9]{0,1:T(8,128)} %get-tuple-element.292, ...), channel_id=1, replica_groups=mesh['dp'=4,'fsdp'=8] {'fsdp'}, use_global_device_ids=true, to_apply=%region_26.27 | all-reduce | flops 52 | bytes 416 | tf_op jit(solution)/shard_map/psum | solution.py:1655
  461.0 0.8 maximum_bitcast_fusion
  461.8 0.8 multiply_bitcast_fusion
  462.7 4.2 fusion.32
  466.9 1.2 fusion.31
  468.3 2.5 fusion.30
  470.8 1.1 copy-done.5
  472.0 2.5 fusion.29
  474.7 0.7 multiply_subtract_fusion.6
  475.7 0.6 copy.133
  476.3 0.7 multiply_subtract_fusion.5
  477.6 0.9 copy.146
  478.5 0.9 copy.147
  (145 shorter events, 8.5 us)
Async XLA Ops:
  367.0 4.0 copy-start.10
  371.1 95.9 %copy-start.9 = (f32[2,96,768]{2,1,0:T(8,128)}, f32[2,96,768]{2,1,0:T(8,128)S(1)}, u32[]{:S(2)}) copy-start(f32[2,96,768]{2,1,0:T(8,128)S(1)} %get-tuple-element.327) | copy-start | bytes 1769476
  375.5 2.9 copy-start.11
  378.3 89.9 %copy-start = (f32[2,96,3072]{2,1,0:T(8,128)}, f32[2,96,3072]{2,1,0:T(8,128)S(1)}, u32[]{:S(2)}) copy-start(f32[2,96,3072]{2,1,0:T(8,128)S(1)} %get-tuple-element.328) | copy-start | bytes 7077892
  378.3 2.8 copy-start.18
  378.3 2.8 copy-start.53
  378.3 4.0 copy-start.21
  381.1 38.9 %copy-start.30 = (f32[2,3072]{1,0:T(2,128)S(1)}, f32[2,3072]{1,0:T(2,128)}, u32[]{:S(2)}) copy-start(f32[2,3072]{1,0:T(2,128)} %param.36) | copy-start | bytes 73732
  387.2 32.9 %copy-start.28 = (f32[2,384]{1,0:T(2,128)}, f32[2,384]{1,0:T(2,128)S(1)}, u32[]{:S(2)}) copy-start(f32[2,384]{1,0:T(2,128)S(1)} %get-tuple-element.350) | copy-start | bytes 9220
  388.0 32.8 %copy-start.36 = (f32[2,96]{1,0:T(2,128)}, f32[2,96]{1,0:T(2,128)S(1)}, u32[]{:S(2)}) copy-start(f32[2,96]{1,0:T(2,128)S(1)} %get-tuple-element.348) | copy-start | bytes 2308
  388.8 32.0 %copy-start.38 = (f32[2,96]{1,0:T(2,128)}, f32[2,96]{1,0:T(2,128)S(1)}, u32[]{:S(2)}) copy-start(f32[2,96]{1,0:T(2,128)S(1)} %get-tuple-element.346) | copy-start | bytes 2308
  388.9 32.4 %copy-start.40 = (f32[2,96]{1,0:T(2,128)}, f32[2,96]{1,0:T(2,128)S(1)}, u32[]{:S(2)}) copy-start(f32[2,96]{1,0:T(2,128)S(1)} %get-tuple-element.344) | copy-start | bytes 2308
  416.7 3.3 copy-start.47
  416.7 4.1 copy-start.49
  416.7 4.1 copy-start.44
  416.7 4.5 copy-start.46
  417.4 2.6 copy-start.23
  417.4 3.4 copy-start.43
  417.4 3.7 copy-start.31
  417.5 3.8 copy-start.7
  420.1 2.4 copy-start.4
  420.8 46.1 %copy-start.17 = (f32[2,768]{1,0:T(2,128)}, f32[2,768]{1,0:T(2,128)S(1)}, u32[]{:S(2)}) copy-start(f32[2,768]{1,0:T(2,128)S(1)} %multiply_add_fusion.7) | copy-start | bytes 18436
  422.9 2.8 copy-start.19
  422.9 3.5 copy-start.32
  462.7 4.3 copy-start.39
  462.7 4.3 copy-start.45
  462.7 5.5 %copy-start.3 = (f32[2,96,3072]{2,1,0:T(8,128)S(1)}, f32[2,96,3072]{2,1,0:T(8,128)}, u32[]{:S(2)}) copy-start(f32[2,96,3072]{2,1,0:T(8,128)} %expand_w.1) | copy-start | bytes 7077892
  462.7 5.5 %copy-start.15 = (f32[2,3072]{1,0:T(2,128)S(1)}, f32[2,3072]{1,0:T(2,128)}, u32[]{:S(2)}) copy-start(f32[2,3072]{1,0:T(2,128)} %copy-done.14) | copy-start | bytes 73732
  462.7 5.5 %copy-start.37 = (f32[2,96]{1,0:T(2,128)S(1)}, f32[2,96]{1,0:T(2,128)}, u32[]{:S(2)}) copy-start(f32[2,96]{1,0:T(2,128)} %copy-done.36) | copy-start | bytes 2308
  462.7 5.5 %copy-start.50 = (f32[2]{0:T(128)S(1)}, f32[2]{0:T(128)}, u32[]{:S(2)}) copy-start(f32[2]{0:T(128)} %copy-done.49) | copy-start | bytes 28
  468.2 2.6 copy-start.1
  468.2 3.6 copy-start.5
  468.2 3.6 copy-start.24
  468.2 3.6 copy-start.29
  468.3 3.6 copy-start.48
  471.9 2.6 copy-start.52
  471.9 2.7 copy-start.51
  471.9 2.8 copy-start.33
  471.9 2.8 copy-start.41
  471.9 2.8 copy-start.42
  471.9 3.7 copy-start.20
  471.9 3.6 copy-start.22
  471.9 4.4 copy-start.27
  472.0 4.3 copy-start.34
  472.0 4.3 copy-start.35
  472.0 5.0 %copy-start.25 = (f32[2,6,96]{2,1,0:T(8,128)S(1)}, f32[2,6,96]{2,1,0:T(8,128)}, u32[]{:S(2)}) copy-start(f32[2,6,96]{2,1,0:T(8,128)} %get-tuple-element.237) | copy-start | bytes 13828
  472.0 5.6 %copy-start.12 = (bf16[512,768]{1,0:T(8,128)(2,1)S(1)}, bf16[512,768]{1,0:T(8,128)(2,1)}, u32[]{:S(2)}) copy-start(bf16[512,768]{1,0:T(8,128)(2,1)} %get-tuple-element.47) | copy-start | bytes 2359300
  472.0 6.5 %copy-start.13 = (bf16[512,768]{1,0:T(8,128)(2,1)S(1)}, bf16[512,768]{1,0:T(8,128)(2,1)}, u32[]{:S(2)}) copy-start(bf16[512,768]{1,0:T(8,128)(2,1)} %get-tuple-element.60) | copy-start | bytes 2359300
  (6 other events, 9.7 us)

commit v3 on v2

--- a/solution.py
+++ b/solution.py
@@ -791,49 +791,36 @@
 ) + (("down", 3.0),)
 
 
+SPREAD = 0.85
+
+
 def forward_plan():
-    events = []
-    z_free = 5.0
-    xy_free = 0.0
-    ready = {}
-    jobs = []
-    for k, (g, first, count) in enumerate(PARTS):
-        share = count / 96.0
-        z_start = z_free
-        z_free = z_start + 12.6 * share
-        jobs.append([z_free + 1.5, k, "xy", 9.9 * share])
-        events.append((z_start if k else 0.0, 0, "z", k))
-    done = []
-    jobs.sort()
-    while jobs:
-        jobs.sort(key=lambda j: (max(j[0], xy_free), 0 if j[2] == "dg" else 1, j[1]))
-        at, k, kind, cost = jobs.pop(0)
-        start = max(at, xy_free)
-        xy_free = start + cost
-        share = PARTS[k][2] / 96.0
-        if kind == "xy":
-            events.append((at, 1, "xy", k))
-            jobs.append([xy_free + 1.5, k, "dg", 5.1 * share])
-        else:
-            events.append((at, 2, "dg", k))
-            events.append((xy_free + 1.5, 3, "last", k))
-            events.append((xy_free + 1.5 + 2.0, 4, "fin", k))
-            ready[PARTS[k][0]] = xy_free + 3.5 + 2.0
-    events.sort()
-    order, now, pos = [], 0.0, 0
-    for layer in range(2):
-        for name, cost in UNIT_TIMES:
-            need = {"joint": 0, "up0": 1, "down": 2}.get(name)
-            start = now
-            if need is not None:
-                start = max(now, ready[3 * layer + need])
-            while pos < len(events) and events[pos][0] <= start + 0.3:
-                order.append(events[pos][2:])
-                pos += 1
+    count = len(PARTS)
+    steps = []
+    for i in range(count + 3):
+        for lag, kind in enumerate(("xy", "dg", "last", "fin")):
+            if 0 <= i - lag < count:
+                steps.append((kind, i - lag))
+    units = [(layer, name, cost) for layer in range(2) for name, cost in UNIT_TIMES]
+    last = {PARTS[k][0]: k for k in range(count)}
+    need = {"joint": 0, "up0": 1, "down": 2}
+    order, finished, at, budget = [], set(), 0, 0.0
+    for step in steps:
+        order.append(step)
+        if step[0] == "fin":
+            finished.add(step[1])
+        budget += SPREAD
+        while at < len(units):
+            layer, name, cost = units[at]
+            if name in need and last[3 * layer + need[name]] not in finished:
+                budget = min(budget, 0.0)
+                break
+            if cost > budget + 0.5:
+                break
+            budget -= cost
             order.append(("run", layer, name))
-            now = start + cost
-    assert pos == len(events)
-    return order
+            at += 1
+    return order + [("run", layer, name) for layer, name, cost in units[at:]]
 
 
 def forward_kernel(
@@ -887,7 +874,7 @@
     greet([gather.x_side, gather.y_side, gather.sibling] + gather.planes)
     gather.z_send(0)
 
-    vg[z, c] = vecs[...]
+    vg[z, c] = vecs[...].reshape(32, 128)
 
     def vec_copy(zz, peer, slot):
         return pltpu.make_async_remote_copy(
@@ -902,13 +889,13 @@
     for k, peer in enumerate(gather.planes):
         vec_copy(z, peer, k).start()
     take(1)
+    gather.z_send(1)
     take(2)
     take(3)
     for k in range(3):
         vec_copy((z + 3 - k) % 4, gather.planes[0], k).wait_recv()
     for zz in range(4):
         vec_copy(zz, gather.sibling, 3 + zz).start()
-    gather.z_send(1)
     take(4)
     take(5)
     build_mask(seg, bias)
@@ -917,16 +904,17 @@
     lane = lax.broadcasted_iota(jnp.int32, (128, 768), 1)
     spot = lax.broadcasted_iota(jnp.int32, (128, 768), 0)
     for layer in range(2):
-        acc = jnp.zeros((16, 768), F32)
+        acc = jnp.zeros((8, 768), F32)
         for m in range(8):
             pick = jnp.where((lane == spot + 96 * m) & (spot < 96), 1.0, 0.0).astype(BF)
-            first = vg[m // 2, m % 2, 16 * layer : 16 * layer + 8, :]
-            rest = [vg[b, m // 4, 16 * layer + 8 + m % 4 : 16 * layer + 9 + m % 4, :] for b in range(4)]
-            left = jnp.concatenate([first] + rest + [jnp.zeros((4, 128), F32)], axis=0)
-            acc = acc + nn(left.astype(BF), pick)
-        vec[layer] = acc
-
-    state = {"sent": 2}
+            acc = acc + nn(vg[m // 2, m % 2, 16 * layer : 16 * layer + 8, :].astype(BF), pick)
+            for k in range(3):
+                row = vg[m // 2, m % 2, 16 * layer + 8 + k : 16 * layer + 9 + k, :].astype(BF).astype(F32)
+                start = 384 * (m % 2) + 128 * k
+                vec[layer, 8 + m // 2 : 9 + m // 2, start : start + 128] = row
+        vec[layer, 0:8, :] = acc
+        vec[layer, 12:16, :] = jnp.zeros((4, 768), F32)
+
     started = []
 
     def save(src, dst):
@@ -939,8 +927,6 @@
         return pltpu.make_async_copy(whole.at[grp], wv.at[grp % 3], wv_sems.at[grp % 3])
 
     def event(kind, k):
-        if kind == "z":
-            return
         if kind == "xy":
             gather.xy_send(k)
             if k + 2 < len(PARTS):
@@ -1093,16 +1079,19 @@
     )(tokens, seg, vecs, joint_w, output_w, expand_w, shrink_w)
 
 
-def pack_vectors(norm_gains, biases, hidden_bias):
-    parts = []
-    for layer in range(2):
-        parts.append(norm_gains[layer])
-        parts.append(biases[layer])
-        parts.append(hidden_bias[layer].reshape(4, 96))
-        parts.append(jnp.zeros((4, 96), F32))
-    rows = jnp.concatenate(parts, axis=0)
-    return jnp.pad(rows, ((0, 0), (0, 32)))
-
+def pack_vectors(gains, biases, hidden, fill=0.0):
+    rows = jnp.pad(jnp.concatenate([gains, biases], axis=1), ((0, 0), (0, 0), (0, 32)), constant_values=fill)
+    tail = jnp.concatenate([hidden.reshape(2, 3, 128), jnp.full((2, 5, 128), fill, F32)], axis=1)
+    return jnp.concatenate([rows, tail], axis=1)
+
+
+def pack_rows(joint, output, expand, shrink):
+    wide = jnp.pad(jnp.stack([joint, output, expand], axis=1), ((0, 0), (0, 0), (0, 32)), constant_values=1.0)
+    rows = jnp.concatenate([wide, shrink.reshape(2, 3, 128)], axis=1).reshape(12, 128)
+    return jnp.pad(rows, ((0, 4), (0, 0)), constant_values=1.0)
+
+
+ROOT_SCALE = 1.0 / math.sqrt(32 * T)
 
 BACK_UNITS = (
     (("ln2", 3.5),)
@@ -1142,6 +1131,12 @@
         elif name == "ag":
             xy_free = max(xy_free, now) + 1.6
             pending.append((xy_free + 1.5, "fin", t, 0))
+        elif name == "fin":
+            pending.append((now, "stat", t, 0))
+        elif name == "stat":
+            now += 1.0
+        elif name == "vec" and zz < 4:
+            pending.append((now + 2.5, "vec", t, zz + 1))
 
     def step(limit):
         pending.sort()
@@ -1163,6 +1158,7 @@
             for zz in PARTS_OF.get(name, ()):
                 core_free = max(core_free, now) + 1.0
                 pending.append((core_free + 1.5, "xy1", 3 * (1 - layer) + GROUP_OF[name[0]], zz))
+    pending.append((now, "vec", 0, 0))
     while step(1e9):
         pass
     return order
@@ -1289,10 +1285,12 @@
 
 
 def backward_kernel(
-    cot, seg, vec, tokens, x_saved, whole, j_saved, c_saved, l_saved, n1_saved, r1_saved, g_saved, gp_saved, n2_saved, r2_saved,
-    fin, total, grad_in,
+    cot, seg, vec, squares, rows_old, columns_old, vec_now, vec_old,
+    tokens, x_saved, whole, j_saved, c_saved, l_saved, n1_saved, r1_saved, g_saved, gp_saved, n2_saved, r2_saved,
+    fin, grad_in, rows_new, columns_new, column_scale, vec_grad, vec_scale,
     gb, rc, rx1, ry1, rx2, ry2, rz, wv, g, dz, dj, ctx, n1, n2, r1, r2, logsum, xb, dob, at, hb, bias, du, sums, vr, va,
-    sems, group_sems, credits, load_sems, vec_sems,
+    row_cols, pay, pay_in, pay_z, pay_sum,
+    sems, group_sems, credits, load_sems, vec_sems, pay_sems,
 ):
     red = Reduce(gb, rc, rx1, ry1, rx2, ry2, rz, fin, sems, group_sems, credits)
     q, z, c = red.q, red.z, red.c
@@ -1412,6 +1410,8 @@
                 red.core_send(base + 2, zz)
         elif name == "dx":
             input_back(dj, wv.at[(base + 2) % 2], du, du, sl)
+            if layer == 0:
+                grad_in[...] = du[...].astype(BF)
             release(layer, "dj")
             next_weights(base + 2)
 
@@ -1426,8 +1426,12 @@
             red.total(t)
         elif name == "ag":
             red.share(t)
+        elif name == "fin":
+            red.finish(t)
+        elif name == "stat":
+            statistics(t)
         else:
-            red.finish(t)
+            vec_event(zz)
 
     def vec_copy(src, dst, k, peer):
         return pltpu.make_async_remote_copy(
@@ -1435,11 +1439,178 @@
             device_id=peer, device_id_type=MESH,
         )
 
-    def vec_hop(k, src, peer, out):
-        cp = vec_copy(src, vr.at[k], k, peer)
+    hops = ((sums, red.sibling), (va.at[0], red.x_side), (va.at[1], red.y_side))
+
+    def vec_event(k):
+        if 1 <= k <= 3:
+            src, peer = hops[k - 1]
+            vec_copy(src, vr.at[k - 1], k - 1, peer).wait()
+            va[k - 1] = src[...] + vr[k - 1]
+        if k <= 2:
+            src, peer = hops[k]
+            vec_copy(src, vr.at[k], k, peer).start()
+        elif k == 3:
+            for j, peer in enumerate(red.planes):
+                vec_copy(va.at[2], vr.at[3 + j], 3 + j, peer).start()
+        else:
+            for j, peer in enumerate(red.planes):
+                vec_copy(va.at[2], vr.at[3 + j], 3 + j, peer).wait()
+            vec_grads(plane_sum(va[2], [vr[3], vr[4], vr[5]]))
+
+    def plane_sum(own, others):
+        acc = jnp.zeros(own.shape, F32)
+        for plane in range(4):
+            part = jnp.where(z == plane, own, 0.0)
+            for k in range(3):
+                part = jnp.where((z + 3 - k) % 4 == plane, others[k], part)
+            acc = acc + part
+        return acc
+
+    f = 2 * z + c
+
+    def vec_grads(total):
+        down = lax.broadcasted_iota(jnp.int32, (768, 128), 0)
+        across = lax.broadcasted_iota(jnp.int32, (768, 128), 1)
+        pick = jnp.where((down == across + 96 * f) & (across < 96), 1.0, 0.0).astype(F32)
+        for layer in range(2):
+            sums[layer] = total[layer] * ROOT_SCALE
+            mine = lax.dot_general(
+                sums[layer, 0:8, :], pick, (((1,), (0,)), ((), ())), precision=lax.Precision.HIGHEST, preferred_element_type=F32
+            )
+            vec_grad[layer] = jnp.zeros((16, 128), F32)
+            vec_grad[layer, 0:8, :] = mine
+            for k in range(3):
+                part = jnp.zeros((1, 128), F32)
+                for zz in range(4):
+                    for cc in range(2):
+                        here = sums[layer, 8 + zz : 9 + zz, 384 * cc + 128 * k : 384 * cc + 128 * k + 128]
+                        part = jnp.where(f == 2 * zz + cc, here, part)
+                vec_grad[layer, 8 + k : 9 + k, :] = part
+
+    def all_sum(v):
+        return jnp.sum(jnp.sum(v, axis=1, keepdims=True), axis=0, keepdims=True)
+
+    lane = lax.broadcasted_iota(jnp.int32, (1, 768), 1)
+    lane_c = lax.broadcasted_iota(jnp.int32, (128, 128), 1)
+
+    def row_column(layer, chunk):
+        return row_cols[:, 6 * layer + chunk : 6 * layer + chunk + 1]
+
+    def set_row_column(layer, chunk, value):
+        if value.shape[0] < 128:
+            value = jnp.concatenate([value, jnp.zeros((128 - value.shape[0], 1), F32)], axis=0)
+        row_cols[...] = jnp.where(lane_c == 6 * layer + chunk, value, row_cols[...])
+
+    def squared(t, b):
+        v = fin[t, b].astype(F32) * ROOT_SCALE
+        return v * v
+
+    def put_scalar(layer, index, value):
+        pay[layer, 18:19, :] = jnp.where(lane == index, value, pay[layer, 18:19, :])
+
+    def row_sums(sq):
+        return jnp.sum(sq + FLOOR_SQUARE, axis=1, keepdims=True)
+
+    def column_sums(sq):
+        return jnp.sum(sq + FLOOR_SQUARE, axis=0, keepdims=True)
+
+    def statistics(t):
+        layer, kind = 1 - t // 3, (2, 1, 0)[t % 3]
+        if kind == 2:
+            sums_of = jnp.concatenate([row_sums(squared(t, b)) for b in range(4)], axis=0)
+            old = jnp.concatenate([row_column(layer, 3 + k) for k in range(3)], axis=0)
+            new = DECAY_RATE * old + (1.0 - DECAY_RATE) * (sums_of / 768.0)
+            for k in range(3):
+                set_row_column(layer, 3 + k, new[128 * k : 128 * k + 128])
+            col, quo = jnp.zeros((1, 768), F32), jnp.zeros((1, 768), F32)
+            for b in range(4):
+                sq = squared(t, b)
+                col = col + column_sums(sq)
+                quo = quo + jnp.sum(sq / new[96 * b : 96 * b + 96], axis=0, keepdims=True)
+            pay[layer, 8:9, :] = col
+            pay[layer, 17:18, :] = quo
+            put_scalar(layer, 3, jnp.sum(new, axis=0, keepdims=True))
+            return
+        sets = (((0, 1, 2), 0, 0, 0), ((3,), 1, 3, 1)) if kind == 0 else (((0, 1, 2, 3), 2, 4, 2),)
+        for blocks, chunk, first, index in sets:
+            sums_of = jnp.zeros((96, 1), F32)
+            for b in blocks:
+                sums_of = sums_of + row_sums(squared(t, b))
+            old = row_column(layer, chunk)[0:96]
+            new = DECAY_RATE * old + (1.0 - DECAY_RATE) * (sums_of / (768.0 * len(blocks)))
+            set_row_column(layer, chunk, new)
+            for k, b in enumerate(blocks):
+                sq = squared(t, b)
+                pay[layer, first + k : first + k + 1, :] = column_sums(sq)
+                pay[layer, 9 + first + k : 10 + first + k, :] = jnp.sum(sq / new, axis=0, keepdims=True)
+            put_scalar(layer, index, jnp.sum(new, axis=0, keepdims=True))
+
+    def vec_moments(layer):
+        grad = vec_grad[layer]
+        return DECAY_RATE * vec_old[layer] + (1.0 - DECAY_RATE) * (grad * grad + FLOOR_SQUARE)
+
+    def exchange_statistics():
+        for layer in range(2):
+            for m in range(4):
+                put_scalar(layer, 4 + m, all_sum(squares[4 * layer + m : 4 * layer + m + 1, :]))
+            grad, now = vec_grad[layer], vec_now[layer]
+            step = grad * grad / vec_moments(layer)
+            for r in range(9):
+                rows = slice(r, r + 1) if r < 8 else slice(8, 11)
+                put_scalar(layer, 8 + r, all_sum(now[rows] * now[rows]))
+                put_scalar(layer, 17 + r, all_sum(step[rows]))
+
+        def copy(src, dst, k, peer):
+            return pltpu.make_async_remote_copy(
+                src_ref=src, dst_ref=dst, send_sem=pay_sems.at[2 * k], recv_sem=pay_sems.at[2 * k + 1],
+                device_id=peer, device_id_type=MESH,
+            )
+
+        cp = copy(pay, pay_in, 0, red.sibling)
         cp.start()
         cp.wait()
-        out[...] = src[...] + vr[k]
+        pay_z[3] = pay[c] + pay_in[c]
+        copies = [copy(pay_z.at[3], pay_z.at[k], 1 + k, peer) for k, peer in enumerate(red.planes)]
+        for cp in copies:
+            cp.start()
+        for cp in copies:
+            cp.wait()
+        pay_sum[c] = plane_sum(pay_z[3], [pay_z[0], pay_z[1], pay_z[2]])
+        cp = copy(pay_sum.at[c], pay_sum.at[c], 4, red.sibling)
+        cp.start()
+        cp.wait()
+
+    def finish_statistics():
+        rows_new[...] = row_cols[...].T[0:16]
+        for layer in range(2):
+            scalars = pay_sum[layer, 18:19, :]
+            pick = lambda index: scalars[:, index : index + 1]
+            for m, (first, count, rows) in enumerate(((0, 3, 768.0), (3, 1, 768.0), (4, 4, 768.0), (8, 1, 3072.0))):
+                new = DECAY_RATE * columns_old[layer, first : first + count, :] + (1.0 - DECAY_RATE) * (
+                    pay_sum[layer, first : first + count, :] / rows
+                )
+                columns_new[layer, first : first + count, :] = new
+                mean_rows = pick(m) / rows
+                entries = rows * 768.0 * count
+                energy = mean_rows * all_sum(pay_sum[layer, 9 + first : 9 + first + count, :] / new)
+                clip = jnp.sqrt(energy / entries) / CLIP_LIMIT
+                stride = STEP_RATE * jnp.maximum(FLOOR_SCALE, jnp.sqrt(pick(4 + m) / entries))
+                column_scale[layer, first : first + count, :] = lax.rsqrt(new) * (
+                    jnp.sqrt(mean_rows) * stride / jnp.maximum(clip, 1.0)
+                )
+            vec_scale[layer] = jnp.zeros((16, 128), F32)
+            for r in range(9):
+                entries = 768.0 if r < 8 else 3072.0
+                clip = jnp.sqrt(pick(17 + r) / entries) / CLIP_LIMIT
+                stride = STEP_RATE * jnp.maximum(FLOOR_SCALE, jnp.sqrt(pick(8 + r) / entries))
+                value = stride / jnp.maximum(clip, 1.0)
+                if r < 8:
+                    vec_scale[layer, r : r + 1, :] = jnp.broadcast_to(value, (1, 128))
+                else:
+                    vec_scale[layer, 8:11, :] = jnp.broadcast_to(value, (3, 128))
+
+    row_cols[...] = jnp.concatenate([rows_old[...], jnp.ones((112, 128), F32)], axis=0).T
+    pay[...] = jnp.zeros_like(pay)
 
     order = backward_plan()
     pos = 0
@@ -1481,28 +1652,15 @@
             event(*it)
         pos = look
 
-    grad_in[...] = du[...].astype(BF)
-    vec_hop(0, sums, red.sibling, va.at[0])
-    vec_hop(1, va.at[0], red.x_side, va.at[1])
-    vec_hop(2, va.at[1], red.y_side, va.at[2])
-    for k, peer in enumerate(red.planes):
-        vec_copy(va.at[2], vr.at[3 + k], 3 + k, peer).start()
-    for k, peer in enumerate(red.planes):
-        vec_copy(va.at[2], vr.at[3 + k], 3 + k, peer).wait()
-    acc = jnp.zeros((2, 16, 768), F32)
-    for plane in range(4):
-        part = jnp.where(z == plane, va[2], 0.0)
-        for k in range(3):
-            part = jnp.where((z + 3 - k) % 4 == plane, vr[3 + k], part)
-        acc = acc + part
-    total[...] = acc
+    exchange_statistics()
+    finish_statistics()
     for t in range(3, 6):
         red.drain(t)
     for t in range(6):
         red.drain_share(t)
 
 
-def backward_call(cot, seg, vec, tokens, x_saved, whole, j_s, c_s, l_s, n1_s, r1_s, g_s, gp_s, n2_s, r2_s):
+def backward_call(cot, seg, vec, squares, rows_old, columns_old, vec_now, vec_old, tokens, x_saved, whole, j_s, c_s, l_s, n1_s, r1_s, g_s, gp_s, n2_s, r2_s):
     sd = jax.ShapeDtypeStruct
     any_spec = pl.BlockSpec(memory_space=pl.ANY)
     vm = pl.BlockSpec(memory_space=pltpu.VMEM)
@@ -1510,9 +1668,12 @@
     dma = pltpu.SemaphoreType.DMA
     return pl.pallas_call(
         backward_kernel,
-        out_shape=[sd((6, 4, 96, 768), BF), sd((2, 16, 768), F32), sd((T, D), BF)],
-        in_specs=[vm, vm, vm] + [any_spec] * 12,
-        out_specs=[vm] * 3,
+        out_shape=[
+            sd((6, 4, 96, 768), BF), sd((T, D), BF), sd((16, 128), F32), sd((2, 9, 768), F32), sd((2, 9, 768), F32),
+            sd((2, 16, 128), F32), sd((2, 16, 128), F32),
+        ],
+        in_specs=[vm] * 8 + [any_spec] * 12,
+        out_specs=[vm] * 7,
         scratch_shapes=[
             V((3, 2, 2, 4, 2, 96, 768), BF),
             V((4, 2, 2, 96, 768), BF),
@@ -1540,17 +1701,141 @@
             V((2, 16, 768), F32),
             V((6, 2, 16, 768), F32),
             V((3, 2, 16, 768), F32),
+            V((128, 128), F32),
+            V((2, 24, 768), F32),
+            V((2, 24, 768), F32),
+            V((4, 24, 768), F32),
+            V((2, 24, 768), F32),
             dma((24, 10)),
             dma((6, 10)),
             pltpu.SemaphoreType.REGULAR((5, 4)),
             dma((12,)),
             dma((12,)),
+            dma((10,)),
         ],
         compiler_params=pltpu.CompilerParams(
             collective_id=1, has_side_effects=True, vmem_limit_bytes=63 << 20
         ),
         name="backward",
-    )(cot, seg, vec, tokens, x_saved, whole, j_s, c_s, l_s, n1_s, r1_s, g_s, gp_s, n2_s, r2_s)
+    )(cot, seg, vec, squares, rows_old, columns_old, vec_now, vec_old, tokens, x_saved, whole, j_s, c_s, l_s, n1_s, r1_s, g_s, gp_s, n2_s, r2_s)
+
+
+def update_kernel(
+    fin, rows_new, columns_new, column_scale, vec_grad, vec_scale, vec_now, vec_old, final, grad_in, joint_w, output_w, expand_w, shrink_w,
+    *refs,
+):
+    outs, scratch = refs[:31], refs[31:]
+    activations, input_gradient = outs[0], outs[1]
+    grads, small_grads = outs[2:6], outs[6:9]
+    nexts, small_nexts = outs[9:13], outs[13:16]
+    copies = outs[16:20]
+    row_outs, column_outs = outs[20:28:2], outs[21:28:2]
+    small_moments = outs[28:31]
+    masters = (joint_w, output_w, expand_w, shrink_w)
+    wbuf, gbuf, nbuf, cbuf, pbuf, in_sems, out_sems, pass_sems = scratch
+    inward = [
+        pltpu.make_async_copy(final, pbuf.at[0], pass_sems.at[0]),
+        pltpu.make_async_copy(grad_in, pbuf.at[1], pass_sems.at[1]),
+    ]
+    through = [
+        pltpu.make_async_copy(pbuf.at[0], activations, pass_sems.at[2]),
+        pltpu.make_async_copy(pbuf.at[1], input_gradient, pass_sems.at[3]),
+    ]
+    pieces = []
+    for layer in range(2):
+        for m, count in enumerate((3, 1, 4, 4)):
+            for b in range(count):
+                kind = (0, 0, 1, 2)[m]
+                t = 3 * (1 - layer) + (2, 1, 0)[kind]
+                pieces.append((layer, m, b, t, 3 if m == 1 else b))
+
+    def part(ref, layer, m, b):
+        if m == 1:
+            return ref.at[layer]
+        if m == 3:
+            return ref.at[layer, pl.ds(96 * b, 96), :]
+        return ref.at[layer, :, pl.ds(768 * b, 768)]
+
+    loads = [
+        pltpu.make_async_copy(part(masters[m], layer, m, b), wbuf.at[n], in_sems.at[n])
+        for n, (layer, m, b, t, block) in enumerate(pieces)
+    ]
+    for cp in loads + inward:
+        cp.start()
+    columns = jnp.concatenate([lax.rsqrt(rows_new[...]), jnp.zeros((112, 128), F32)], axis=0).T
+    stores = []
+    for n, (layer, m, b, t, block) in enumerate(pieces):
+        if n == 12:
+            for before, cp in zip(inward, through):
+                before.wait()
+                cp.start()
+        if m < 3:
+            left = columns[0:96, 6 * layer + m : 6 * layer + m + 1]
+        else:
+            left = jnp.concatenate([columns[:, 6 * layer + 3 + k : 6 * layer + 4 + k] for k in range(3)], axis=0)
+            left = left[96 * b : 96 * b + 96]
+        j = (0, 3, 4, 8)[m] + (b if m != 3 else 0)
+        grad = fin[t, block].astype(F32) * ROOT_SCALE
+        loads[n].wait()
+        new = wbuf[n] - grad * left * column_scale[layer, j : j + 1, :]
+        gbuf[n] = grad
+        nbuf[n] = new
+        cbuf[n] = new.astype(BF)
+        for k, (src, dst) in enumerate(((gbuf, grads[m]), (nbuf, nexts[m]), (cbuf, copies[m]))):
+            cp = pltpu.make_async_copy(src.at[n], part(dst, layer, m, b), out_sems.at[n, k])
+            cp.start()
+            stores.append(cp)
+    for layer in range(2):
+        grad, now = vec_grad[layer], vec_now[layer]
+        moments = DECAY_RATE * vec_old[layer] + (1.0 - DECAY_RATE) * (grad * grad + FLOOR_SQUARE)
+        new = now - vec_scale[layer] * (grad * lax.rsqrt(moments))
+        for out, value in zip((small_grads, small_nexts, small_moments), (grad, new, moments)):
+            out[0][layer] = value[0:2, 0:96]
+            out[1][layer] = value[2:8, 0:96]
+            for k in range(3):
+                out[2][layer : layer + 1, 128 * k : 128 * k + 128] = value[8 + k : 9 + k, :]
+        for m in range(3):
+            row_outs[m][layer : layer + 1, :] = rows_new[6 * layer + m : 6 * layer + m + 1, 0:96]
+        for k in range(3):
+            row_outs[3][layer : layer + 1, 128 * k : 128 * k + 128] = rows_new[6 * layer + 3 + k : 6 * layer + 4 + k, :]
+        for m, (first, count) in enumerate(((0, 3), (3, 1), (4, 4), (8, 1))):
+            for k in range(count):
+                column_outs[m][layer : layer + 1, 768 * k : 768 * k + 768] = columns_new[layer, first + k : first + k + 1, :]
+    for cp in stores + through:
+        cp.wait()
+
+
+def update_call(*args):
+    sd = jax.ShapeDtypeStruct
+    any_spec = pl.BlockSpec(memory_space=pl.ANY)
+    vm = pl.BlockSpec(memory_space=pltpu.VMEM)
+    V = pltpu.VMEM
+    mats = ((2, 96, 2304), (2, 96, 768), (2, 96, 3072), (2, 384, 768))
+    small = ((2, 2, 96), (2, 6, 96), (2, 384))
+    stats = ((2, 96), (2, 2304), (2, 96), (2, 768), (2, 96), (2, 3072), (2, 384), (2, 768))
+    shapes = (
+        [sd((T, D), BF)] * 2 + [sd(s, F32) for s in mats] + [sd(s, F32) for s in small] + [sd(s, F32) for s in mats]
+        + [sd(s, F32) for s in small] + [sd(s, BF) for s in mats] + [sd(s, F32) for s in stats] + [sd(s, F32) for s in small]
+    )
+    specs = [any_spec] * 6 + [vm] * 3 + [any_spec] * 4 + [vm] * 3 + [any_spec] * 4 + [vm] * 11
+    return pl.pallas_call(
+        update_kernel,
+        out_shape=shapes,
+        in_specs=[vm] * 8 + [any_spec] * 6,
+        out_specs=specs,
+        scratch_shapes=[
+            V((24, 96, 768), F32),
+            V((24, 96, 768), F32),
+            V((24, 96, 768), F32),
+            V((24, 96, 768), BF),
+            V((2, T, D), BF),
+            pltpu.SemaphoreType.DMA((24,)),
+            pltpu.SemaphoreType.DMA((24, 3)),
+            pltpu.SemaphoreType.DMA((4,)),
+        ],
+        compiler_params=pltpu.CompilerParams(vmem_limit_bytes=56 << 20),
+        name="update",
+    )(*args)
 
 
 def local_kernels(
@@ -1581,134 +1866,18 @@
     (whole, vec, x_saved, j_s, c_s, l_s, n1_s, r1_s, g_s, gp_s, n2_s, r2_s, final, squares) = forward_call(
         tokens[0], segments, vecs, joint_weight, output_weight, expand_weight, shrink_weight
     )
-    activations = final[None]
-    blocks, sums, grad = backward_call(
-        cotangent[0], segments, vec, tokens[0], x_saved, whole, j_s, c_s, l_s, n1_s, r1_s, g_s, gp_s, n2_s, r2_s
-    )
-    f = lax.axis_index("fsdp")
-    mine = lax.dynamic_slice_in_dim(sums[:, :8], f * 96, 96, axis=2)
-    hidden_mine = lax.dynamic_slice_in_dim(sums[:, 8:12].reshape(2, 3072), f * 384, 384, axis=1)
-    collected = []
-    for number in range(2):
-        gs, ge, ga = blocks[3 * (1 - number)], blocks[3 * (1 - number) + 1], blocks[3 * (1 - number) + 2]
-        collected.append((
-            ga[:3].transpose(1, 0, 2).reshape(96, 2304).astype(jnp.float32),
-            ga[3].astype(jnp.float32),
-            ge.transpose(1, 0, 2).reshape(96, 3072).astype(jnp.float32),
-            gs.reshape(384, 768).astype(jnp.float32),
-            mine[number, :2],
-            mine[number, 2:8],
-            hidden_mine[number],
-        ))
-    input_gradient = grad[None]
-    fsdp_count = lax.axis_size("fsdp")
-    token_total = row_count * slot_count * lax.axis_size("dp") * fsdp_count
-    root_scale = 1.0 / math.sqrt(token_total)
-    stacked_grads = [
-        jnp.stack([entry[index] for entry in collected]) * root_scale for index in range(7)
-    ]
-    matrices = (
-        (stacked_grads[0], joint_weight, joint_rows, joint_columns),
-        (stacked_grads[1], output_weight, output_rows, output_columns),
-        (stacked_grads[2], expand_weight, expand_rows, expand_columns),
-        (stacked_grads[3], shrink_weight, shrink_rows, shrink_columns),
-    )
-    partial_list = [factored_partials(item[0], item[1], item[2]) for item in matrices]
-    vectors = (
-        (stacked_grads[4], norm_gains, gain_moments),
-        (stacked_grads[5], biases, bias_moments),
-        (stacked_grads[6][:, None, :], hidden_bias[:, None, :], hidden_moments[:, None, :]),
-    )
-    vector_list = [vector_partials(item[0], item[2]) for item in vectors]
-    vector_squares = jnp.concatenate(
-        [jnp.sum(item[1] * item[1], axis=2) for item in vectors], axis=1
-    )
-    statistics = lax.psum(
-        (
-            partial_list[0][1],
-            partial_list[1][1],
-            partial_list[2][1],
-            partial_list[3][1],
-            jnp.stack([item[2] for item in partial_list], axis=1),
-            jnp.stack([item[3] for item in partial_list], axis=1),
-            vector_squares,
-        ),
-        "fsdp",
-    )
-    updates = []
-    columns_list = []
-    for index in range(4):
-        gradient = matrices[index][0]
-        total_rows = gradient.shape[1] * fsdp_count
-        rows_next = partial_list[index][0]
-        columns_next = DECAY_RATE * matrices[index][3] + (1.0 - DECAY_RATE) * (
-            statistics[index] / total_rows
-        )
-        row_average = statistics[4][:, index] / total_rows
-        estimate = rows_next[:, :, None] * columns_next[:, None, :] / row_average[:, None, None]
-        updates.append(gradient * lax.rsqrt(estimate))
-        columns_list.append(columns_next)
-    matrix_squares = jnp.stack([jnp.sum(item * item, axis=(1, 2)) for item in updates], axis=1)
-    vector_updates = jnp.concatenate(
-        [jnp.sum(item[1] * item[1], axis=2) for item in vector_list], axis=1
-    )
-    norms = lax.psum((matrix_squares, vector_updates), "fsdp")
-    matrix_next = []
-    for index in range(4):
-        gradient = matrices[index][0]
-        entry_count = gradient.shape[1] * fsdp_count * gradient.shape[2]
-        clip_ratio = jnp.sqrt(norms[0][:, index] / entry_count) / CLIP_LIMIT
-        update = updates[index] / jnp.maximum(clip_ratio, 1.0)[:, None, None]
-        stride = STEP_RATE * jnp.maximum(
-            FLOOR_SCALE, jnp.sqrt(statistics[5][:, index] / entry_count)
-        )
-        matrix_next.append(matrices[index][1] - stride[:, None, None] * update)
-    vector_next = []
-    offset = 0
-    for index in range(3):
-        gradient = vectors[index][0]
-        kinds = gradient.shape[1]
-        entry_count = gradient.shape[2] * fsdp_count
-        clip_ratio = jnp.sqrt(norms[1][:, offset : offset + kinds] / entry_count) / CLIP_LIMIT
-        update = vector_list[index][1] / jnp.maximum(clip_ratio, 1.0)[:, :, None]
-        stride = STEP_RATE * jnp.maximum(
-            FLOOR_SCALE, jnp.sqrt(statistics[6][:, offset : offset + kinds] / entry_count)
-        )
-        vector_next.append(vectors[index][1] - stride[:, :, None] * update)
-        offset = offset + kinds
-    return (
-        activations,
-        input_gradient,
-        stacked_grads[0],
-        stacked_grads[1],
-        stacked_grads[2],
-        stacked_grads[3],
-        stacked_grads[4],
-        stacked_grads[5],
-        stacked_grads[6],
-        matrix_next[0],
-        matrix_next[1],
-        matrix_next[2],
-        matrix_next[3],
-        vector_next[0],
-        vector_next[1],
-        vector_next[2][:, 0, :],
-        matrix_next[0].astype(jnp.bfloat16),
-        matrix_next[1].astype(jnp.bfloat16),
-        matrix_next[2].astype(jnp.bfloat16),
-        matrix_next[3].astype(jnp.bfloat16),
-        partial_list[0][0],
-        columns_list[0],
-        partial_list[1][0],
-        columns_list[1],
-        partial_list[2][0],
-        columns_list[2],
-        partial_list[3][0],
-        columns_list[3],
-        vector_list[0][0],
-        vector_list[1][0],
-        vector_list[2][0][:, 0, :],
-    )
+    old = pack_vectors(gain_moments, bias_moments, hidden_moments, 1.0)
+    rows_old = pack_rows(joint_rows, output_rows, expand_rows, shrink_rows)
+    columns_old = jnp.concatenate([joint_columns, output_columns, expand_columns, shrink_columns], axis=1).reshape(2, 9, 768)
+    blocks, grad_in, rows_new, columns_new, column_scale, vec_grad, vec_scale = backward_call(
+        cotangent[0], segments, vec, squares, rows_old, columns_old, vecs, old,
+        tokens[0], x_saved, whole, j_s, c_s, l_s, n1_s, r1_s, g_s, gp_s, n2_s, r2_s
+    )
+    outs = update_call(
+        blocks, rows_new, columns_new, column_scale, vec_grad, vec_scale, vecs, old, final, grad_in,
+        joint_weight, output_weight, expand_weight, shrink_weight
+    )
+    return (outs[0][None], outs[1][None]) + tuple(outs[2:])
 
 
 def solution(mesh):

time: 483 us -> 377 us (0.78)
  blocking collectives: 54.9 us -> 0 us
  other arithmetic: 40.6 us -> 3.59 us
  local copies, waits for them, and re-layouts: 22.2 us -> 8.81 us
    psum x2 -> x0, blocking collectives: 54.9 us -> none  [the longest x1 27.8 us: local_kernels(): lax.psum((partial_list[0][1], partial_list[1][1], partial_list[2][1], par...]
    reduce_sum x21 -> x0, other arithmetic: 23.1 us -> none  [the longest x4 8.6 us: factored_partials(): jnp.sum(squared, axis=1)]
    pallas_call x1, Pallas kernels: 149 us -> 131 us  [forward_call(): pl.pallas_call(forward_kernel, out_shape=saved, in_specs=[vm, vm, vm] + [...]
    pallas_call x1 -> x2, Pallas kernels: 211 us -> 228 us  [the longest x1 214 us: backward_call(): pl.pallas_call(backward_kernel, out_shape=[sd((6, 4, 96, 768), BF), sd((T...]
    convert_element_type x4 -> x0, other arithmetic: 10.4 us -> none  [the longest x1 4.19 us: local_kernels(): matrix_next[0].astype(jnp.bfloat16)]
    convert_element_type x10 -> x0, local copies, waits for them, and re-layouts: 7.38 us -> none  [the longest x4 3.39 us: local_kernels(): ge.transpose(1, 0, 2).reshape(96, 3072).astype(jnp.float32)]
where the time goes in v3:
time: 377 us; the launch traced here: 372 us
  Pallas kernels  358 us (95%)
  local copies, waits for them, and re-layouts  8.81 us (2%)
    pallas_call x1, Pallas kernels, backward_call(): pl.pallas_call(backward_kernel, out_shape=[sd((6, 4, 96, 768), BF), sd((T...  214 us
    pallas_call x1, Pallas kernels, forward_call(): pl.pallas_call(forward_kernel, out_shape=saved, in_specs=[vm, vm, vm] + [...  131 us
    pallas_call x1, Pallas kernels, update_call(): pl.pallas_call(update_kernel, out_shape=shapes, in_specs=[vm] * 8 + [any_...  13.9 us

profile of v3, /device:TPU:0, one launch (start us, length us, event | category | flops | bytes accessed | tf_op | source)
XLA Modules:
  0.0 371.8 jit_solution(960500801625712031)
XLA Ops:
  0.7 0.1 pad.35.clone
  0.8 0.1 pad.21.clone
  0.8 0.7 reshape.77
  1.5 0.7 select_maximum_fusion.2
  2.3 0.7 reshape.78
  3.0 0.6 pad.17.rows_old
  3.6 0.7 reshape.81
  4.3 0.7 copy.59
  5.0 0.7 select_maximum_fusion.1
  5.7 0.7 copy.60
  6.3 0.7 select_maximum_fusion
  7.0 0.7 maximum_maximum_fusion
  7.7 0.8 pad_maximum_fusion
  8.5 0.7 reshape.80.columns_old
  9.2 130.6 %forward.1 = (bf16[6,4,768,768]{3,2,1,0:T(8,128)(2,1)}, f32[2,16,768]{2,1,0:T(8,128)}, bf16[512,768]{1,0:T(8,128)(2,1)}, bf16[2,3,512,768]{3,2,1,0:T(8,128)(2,1)...) custom-call(bf16[512,768]{1,0:T(8,128)(2,1)} %bitcast.7, ...), custom_call_target="tpu_custom_call" | custom-call | tf_op jit(solution)/shard_map/forward/pallas_call | solution.py:1069
  139.8 213.7 %backward.1 = (bf16[6,4,96,768]{3,2,1,0:T(8,128)(2,1)}, bf16[512,768]{1,0:T(8,128)(2,1)}, f32[16,128]{1,0:T(8,128)}, f32[2,9,768]{2,1,0:T(8,128)}, f32[2,9,768]{...) custom-call(bf16[512,768]{1,0:T(8,128)(2,1)} %bitcast.9, s32[1,512]{1,0:T(1,128)} %seg.3, ...), custom_call_target="tpu_custom_call" | custom-call | tf_op jit(solution)/shard_map/backward/pallas_call | solution.py:1669
  353.5 13.9 %update.1 = (bf16[512,768]{1,0:T(8,128)(2,1)}, bf16[512,768]{1,0:T(8,128)(2,1)}, f32[2,96,2304]{2,1,0:T(8,128)}, f32[2,96,768]{2,1,0:T(8,128)}, f32[2,96,3072]{2...) custom-call(bf16[6,4,96,768]{3,2,1,0:T(8,128)(2,1)} %get-tuple-eleme, ...), custom_call_target="tpu_custom_call" | custom-call | tf_op jit(solution)/shard_map/update/pallas_call | solution.py:1821
  367.4 1.3 copy.61
  368.7 1.3 copy.62
  370.0 1.3 copy.63
  (4 shorter events, 0.0 us)

commit v4 on v3

--- a/solution.py
+++ b/solution.py
@@ -453,7 +453,7 @@
         ).astype(F32)
 
 
-def joint_forward(xb, wa, vec, joint, tile=256):
+def joint_forward(xb, wa, vec, joint, tile=T):
     for b in range(3):
         @pl.loop(0, T // tile)
         def _(i, b=b):
@@ -502,7 +502,7 @@
     return c * inv, inv
 
 
-def out_forward(ctx, x, wo, vec, n1, r1, h, hb, tile=128):
+def out_forward(ctx, x, wo, vec, n1, r1, h, hb, tile=T):
     @pl.loop(0, T // tile)
     def _(i):
         r = rows_at(i, tile)
@@ -527,7 +527,7 @@
     return z * cdf, cdf + z * (e * 0.3989422804014327)
 
 
-def ffn_up(hb, we, vec, g, gp, b, tile=128):
+def ffn_up(hb, we, vec, g, gp, b, tile=T):
     @pl.loop(0, T // tile)
     def _(i):
         r = rows_at(i, tile)
@@ -537,7 +537,7 @@
         gp[b, r, :] = der.astype(BF)
 
 
-def ffn_down(g, ws, vec, h, n2, r2, x_out, xb_out, tile=128):
+def ffn_down(g, ws, vec, h, n2, r2, x_out, xb_out, tile=T):
     @pl.loop(0, T // tile)
     def _(i):
         r = rows_at(i, tile)
@@ -557,7 +557,7 @@
     return jnp.sum(v.reshape(v.shape[0] // 8, 8, v.shape[1]), axis=0)
 
 
-def norm_backward(dy, n, r, gain_row, du, dub, sums, rows, tile=128):
+def norm_backward(dy, n, r, gain_row, du, dub, sums, rows, tile=256):
     def step(i, carry):
         s = rows_at(i, tile)
         g = dy[s, :].astype(F32)
@@ -595,7 +595,7 @@
         out[r, :] = nn(at[r, :], bmat[...]).astype(BF)
 
 
-def ffn_back_block(dob, ws, gp, dz, sums, b, tile=128):
+def ffn_back_block(dob, ws, gp, dz, sums, b, tile=T):
     def step(i, acc):
         r = rows_at(i, tile)
         v = (nt(dob[r, :], ws[b]) * gp[b, r, :].astype(F32)).astype(BF)
@@ -606,7 +606,7 @@
     sums[8 + b : 9 + b, :] = jnp.sum(acc, axis=0, keepdims=True)
 
 
-def ffn_back_input(dz, we, du, tile=128):
+def ffn_back_input(dz, we, du, tile=T):
     @pl.loop(0, T // tile)
     def _(i):
         r = rows_at(i, tile)
@@ -616,14 +616,14 @@
         du[r, :] = u
 
 
-def context_back(dab, wo, dc, tile=256):
+def context_back(dab, wo, dc, tile=T):
     @pl.loop(0, T // tile)
     def _(i):
         r = rows_at(i, tile)
         dc[r, :] = nt(dab[r, :], wo[...]).astype(BF)
 
 
-def attend_backward_pair(p, joint, bias, logsum, dc, dj):
+def attend_backward_pair(p, joint, bias, logsum, ctx, dc, dj):
     lanes = pl.ds(pl.multiple_of(p * 128, 128), 128)
     masks = head_masks()
     q2 = joint[0, :, lanes]
@@ -632,6 +632,11 @@
     d2 = dc[:, lanes]
     kt = k2.T
     ls = logsum[p]
+    both = d2.astype(F32) * ctx[:, lanes].astype(F32)
+    high = both.astype(BF)
+    low = (both - high.astype(F32)).astype(BF)
+    pick = jnp.concatenate(masks + [jnp.zeros((6, 128), F32)], axis=0).astype(BF)
+    delta = nt(pick, high) + nt(pick, low)
     dk = jnp.zeros((T, 128), F32)
     dv = jnp.zeros((T, 128), F32)
     dqt = []
@@ -639,9 +644,7 @@
         qm = q2 * (masks[h] * 0.125).astype(BF)
         dm = d2 * masks[h].astype(BF)
         prob = jnp.exp(nt(k2, qm) + bias[...] - ls[h : h + 1, :])
-        dp = nt(v2, dm)
-        delta = jnp.sum(prob * dp, axis=0, keepdims=True)
-        ds = (prob * (dp - delta)).astype(BF)
+        ds = (prob * (nt(v2, dm) - delta[h : h + 1, :])).astype(BF)
         dv = dv + nn(prob.astype(BF), dm)
         dk = dk + nn(ds, qm)
         dqt.append(nn(kt[64 * h : 64 * h + 64, :], ds))
@@ -650,7 +653,7 @@
     dj[2, :, lanes] = dv.astype(BF)
 
 
-def input_back(dj, wa, du, dx, sums, tile=128):
+def input_back(dj, wa, du, dx, sums, tile=T):
     def step(i, carry):
         r = rows_at(i, tile)
         u = du[r, :]
@@ -786,12 +789,22 @@
         self.total(k, 10, 16 * count)
 
 
-UNIT_TIMES = (("joint", 3.0),) + tuple((f"att{p}", 1.4) for p in range(6)) + (("out", 2.0),) + tuple(
-    (f"up{b}", 1.7) for b in range(4)
-) + (("down", 3.0),)
-
-
-SPREAD = 0.85
+UNIT_TIMES = (("joint", 2.1),) + tuple((f"att{p}", 1.3) for p in range(6)) + (("out", 1.0),) + tuple(
+    (f"up{b}", 1.0) for b in range(4)
+) + (("down", 2.8),)
+
+
+SPREAD = 0.7
+
+
+def pack_vectors(ref, gains, biases, hidden, fill):
+    ref[...] = jnp.full(ref.shape, fill, F32)
+    for layer in range(2):
+        ref[layer, 0:2, 0:96] = gains[layer]
+        for r in range(6):
+            ref[layer, 2 + r : 3 + r, 0:96] = biases[r, layer : layer + 1, :]
+        for k in range(3):
+            ref[layer, 8 + k : 9 + k, :] = hidden[layer : layer + 1, 128 * k : 128 * k + 128]
 
 
 def forward_plan():
@@ -824,9 +837,9 @@
 
 
 def forward_kernel(
-    tokens, seg, vecs, joint_w, output_w, expand_w, shrink_w,
+    tokens, seg, gains, biases, hidden, joint_w, output_w, expand_w, shrink_w,
     whole, vec_out, x_saved, j_saved, c_saved, l_saved, n1_saved, r1_saved, g_saved, gp_saved, n2_saved, r2_saved, final, squares,
-    stage, sbuf, wv, bias, x1, h, hb, xb, joint, ctx, logsum, n1, r1, g, gp, n2, r2, vg, vec,
+    stage, sbuf, wv, bias, x1, h, hb, xb, joint, ctx, logsum, n1, r1, g, gp, n2, r2, vg, vec, vec_now,
     sems, stage_sems, wv_sems, vec_sems, out_sems,
 ):
     masters = (joint_w, output_w, expand_w, shrink_w)
@@ -874,7 +887,8 @@
     greet([gather.x_side, gather.y_side, gather.sibling] + gather.planes)
     gather.z_send(0)
 
-    vg[z, c] = vecs[...].reshape(32, 128)
+    pack_vectors(vec_now, gains, biases, hidden, 0.0)
+    vg[z, c] = vec_now[...].reshape(32, 128)
 
     def vec_copy(zz, peer, slot):
         return pltpu.make_async_remote_copy(
@@ -1019,7 +1033,7 @@
         cp.wait()
 
 
-def forward_call(tokens, seg, vecs, joint_w, output_w, expand_w, shrink_w):
+def forward_call(tokens, seg, gains, biases, hidden, joint_w, output_w, expand_w, shrink_w):
     sd = jax.ShapeDtypeStruct
     any_spec = pl.BlockSpec(memory_space=pl.ANY)
     vm = pl.BlockSpec(memory_space=pltpu.VMEM)
@@ -1060,6 +1074,7 @@
         V((2, T, 128), F32),
         V((4, 2, 32, 128), F32),
         V((2, 16, 768), F32),
+        V((2, 16, 128), F32),
         pltpu.SemaphoreType.DMA((len(PARTS), 13)),
         pltpu.SemaphoreType.DMA((2, 4)),
         pltpu.SemaphoreType.DMA((3,)),
@@ -1069,37 +1084,25 @@
     return pl.pallas_call(
         forward_kernel,
         out_shape=saved,
-        in_specs=[vm, vm, vm] + [any_spec] * 4,
+        in_specs=[vm] * 5 + [any_spec] * 4,
         out_specs=[any_spec] * 13 + [vm],
         scratch_shapes=scratch,
         compiler_params=pltpu.CompilerParams(
             collective_id=0, has_side_effects=True, vmem_limit_bytes=62 << 20
         ),
         name="forward",
-    )(tokens, seg, vecs, joint_w, output_w, expand_w, shrink_w)
-
-
-def pack_vectors(gains, biases, hidden, fill=0.0):
-    rows = jnp.pad(jnp.concatenate([gains, biases], axis=1), ((0, 0), (0, 0), (0, 32)), constant_values=fill)
-    tail = jnp.concatenate([hidden.reshape(2, 3, 128), jnp.full((2, 5, 128), fill, F32)], axis=1)
-    return jnp.concatenate([rows, tail], axis=1)
-
-
-def pack_rows(joint, output, expand, shrink):
-    wide = jnp.pad(jnp.stack([joint, output, expand], axis=1), ((0, 0), (0, 0), (0, 32)), constant_values=1.0)
-    rows = jnp.concatenate([wide, shrink.reshape(2, 3, 128)], axis=1).reshape(12, 128)
-    return jnp.pad(rows, ((0, 4), (0, 0)), constant_values=1.0)
+    )(tokens, seg, gains, biases, hidden, joint_w, output_w, expand_w, shrink_w)
 
 
 ROOT_SCALE = 1.0 / math.sqrt(32 * T)
 
 BACK_UNITS = (
-    (("ln2", 3.5),)
-    + tuple((f"s{i}", 2.0) for i in range(4))
-    + tuple((f"dz{i}", 2.0) for i in range(4))
-    + (("ht", 1.2), ("e0", 3.5), ("e1", 3.5), ("dh", 4.5), ("ln1", 3.5), ("o", 3.5))
-    + tuple((f"att{p}", 2.6) for p in range(6))
-    + (("xt", 0.8), ("q0", 2.8), ("q1", 2.8), ("dx", 3.5))
+    (("ln2", 1.2),)
+    + tuple((f"s{i}", 1.3) for i in range(4))
+    + tuple((f"dz{i}", 1.0) for i in range(4))
+    + (("ht", 0.9), ("e0", 1.5), ("e1", 1.5), ("dh", 2.8), ("ln1", 1.2), ("o", 2.4))
+    + tuple((f"att{p}", 1.75) for p in range(6))
+    + (("xt", 0.5), ("q0", 1.5), ("q1", 1.5), ("dx", 2.4))
 )
 GROUP_OF = {"s": 0, "e": 1, "o": 2, "q": 2}
 PARTS_OF = {"s0": (0,), "s1": (1,), "s2": (2,), "s3": (3,), "e0": (0, 1), "e1": (2, 3), "q0": (0, 1), "q1": (2, 3)}
@@ -1138,10 +1141,31 @@
         elif name == "vec" and zz < 4:
             pending.append((now + 2.5, "vec", t, zz + 1))
 
+    emitted = set()
+
+    def force(name, t, zz):
+        if t < 0 or (name, t, zz) in emitted:
+            return
+        for entry in list(pending):
+            if entry[1:] == (name, t, zz):
+                pending.remove(entry)
+                settle(entry)
+                return
+        force({"xy2": "xy1", "z": "xy2"}[name], t, zz)
+        force(name, t, zz)
+
+    def settle(entry):
+        name, t, zz = entry[1:]
+        emitted.add((name, t, zz))
+        after = {"xy1": "xy2", "xy2": "z"}.get(name)
+        if after:
+            force(after, t - 1, zz)
+        emit(entry)
+
     def step(limit):
         pending.sort()
         if pending and pending[0][0] <= limit:
-            emit(pending.pop(0))
+            settle(pending.pop(0))
             return True
         return False
 
@@ -1153,6 +1177,8 @@
                 t = 3 * (1 - layer) + GROUP_OF[name[0]]
                 while t >= 3 and t - 3 not in summed:
                     step(1e9)
+            for zz in PARTS_OF.get(name, ()):
+                force("xy1", t - 1, zz)
             order.append(("run", layer, name))
             now += cost
             for zz in PARTS_OF.get(name, ()):
@@ -1285,11 +1311,12 @@
 
 
 def backward_kernel(
-    cot, seg, vec, squares, rows_old, columns_old, vec_now, vec_old,
+    cot, seg, vec, squares, joint_rows, output_rows, expand_rows, shrink_rows,
+    joint_columns, output_columns, expand_columns, shrink_columns, gains, biases, hidden, gain_old, bias_old, hidden_old,
     tokens, x_saved, whole, j_saved, c_saved, l_saved, n1_saved, r1_saved, g_saved, gp_saved, n2_saved, r2_saved,
     fin, grad_in, rows_new, columns_new, column_scale, vec_grad, vec_scale,
     gb, rc, rx1, ry1, rx2, ry2, rz, wv, g, dz, dj, ctx, n1, n2, r1, r2, logsum, xb, dob, at, hb, bias, du, sums, vr, va,
-    row_cols, pay, pay_in, pay_z, pay_sum,
+    row_cols, pay, pay_in, pay_z, pay_sum, columns_old, vec_now, vec_old,
     sems, group_sems, credits, load_sems, vec_sems, pay_sems,
 ):
     red = Reduce(gb, rc, rx1, ry1, rx2, ry2, rz, fin, sems, group_sems, credits)
@@ -1397,11 +1424,10 @@
             for pair in range(2):
                 blocks_pair((base + 2) % 3, 3, pair, dob[...])
             context_back(dob, wv.at[(base + 2) % 2, 3], hb)
-            release(layer, "ctx")
         elif name == "xt":
             need(layer, "xb")
             transpose_into(xb, at)
-            release(layer, "xb", "logsum")
+            release(layer, "xb", "logsum", "ctx")
         elif name[0] == "q":
             pair = int(name[1])
             for b in range(3):
@@ -1609,7 +1635,20 @@
                 else:
                     vec_scale[layer, 8:11, :] = jnp.broadcast_to(value, (3, 128))
 
-    row_cols[...] = jnp.concatenate([rows_old[...], jnp.ones((112, 128), F32)], axis=0).T
+    row_cols[...] = jnp.ones((128, 128), F32)
+    for layer in range(2):
+        for m, ref in enumerate((joint_rows, output_rows, expand_rows)):
+            row_cols[6 * layer + m : 6 * layer + m + 1, 0:96] = ref[layer : layer + 1, :]
+        for k in range(3):
+            row_cols[6 * layer + 3 + k : 6 * layer + 4 + k, :] = shrink_rows[layer : layer + 1, 128 * k : 128 * k + 128]
+        at_row = 0
+        for ref, count in ((joint_columns, 3), (output_columns, 1), (expand_columns, 4), (shrink_columns, 1)):
+            for k in range(count):
+                columns_old[layer, at_row : at_row + 1, :] = ref[layer : layer + 1, 768 * k : 768 * k + 768]
+                at_row += 1
+    row_cols[...] = row_cols[...].T
+    pack_vectors(vec_now, gains, biases, hidden, 0.0)
+    pack_vectors(vec_old, gain_old, bias_old, hidden_old, 1.0)
     pay[...] = jnp.zeros_like(pay)
 
     order = backward_plan()
@@ -1646,7 +1685,7 @@
                 def _():
                     for it in items:
                         event(*it)
-            attend_backward_pair(p, dj, bias, logsum, hb, dj)
+            attend_backward_pair(p, dj, bias, logsum, ctx, hb, dj)
 
         for it in tail:
             event(*it)
@@ -1660,7 +1699,7 @@
         red.drain_share(t)
 
 
-def backward_call(cot, seg, vec, squares, rows_old, columns_old, vec_now, vec_old, tokens, x_saved, whole, j_s, c_s, l_s, n1_s, r1_s, g_s, gp_s, n2_s, r2_s):
+def backward_call(*args):
     sd = jax.ShapeDtypeStruct
     any_spec = pl.BlockSpec(memory_space=pl.ANY)
     vm = pl.BlockSpec(memory_space=pltpu.VMEM)
@@ -1672,7 +1711,7 @@
             sd((6, 4, 96, 768), BF), sd((T, D), BF), sd((16, 128), F32), sd((2, 9, 768), F32), sd((2, 9, 768), F32),
             sd((2, 16, 128), F32), sd((2, 16, 128), F32),
         ],
-        in_specs=[vm] * 8 + [any_spec] * 12,
+        in_specs=[vm] * 18 + [any_spec] * 12,
         out_specs=[vm] * 7,
         scratch_shapes=[
             V((3, 2, 2, 4, 2, 96, 768), BF),
@@ -1706,6 +1745,9 @@
             V((2, 24, 768), F32),
             V((4, 24, 768), F32),
             V((2, 24, 768), F32),
+            V((2, 9, 768), F32),
+            V((2, 16, 128), F32),
+            V((2, 16, 128), F32),
             dma((24, 10)),
             dma((6, 10)),
             pltpu.SemaphoreType.REGULAR((5, 4)),
@@ -1717,11 +1759,11 @@
             collective_id=1, has_side_effects=True, vmem_limit_bytes=63 << 20
         ),
         name="backward",
-    )(cot, seg, vec, squares, rows_old, columns_old, vec_now, vec_old, tokens, x_saved, whole, j_s, c_s, l_s, n1_s, r1_s, g_s, gp_s, n2_s, r2_s)
+    )(*args)
 
 
 def update_kernel(
-    fin, rows_new, columns_new, column_scale, vec_grad, vec_scale, vec_now, vec_old, final, grad_in, joint_w, output_w, expand_w, shrink_w,
+    fin, rows_new, columns_new, column_scale, vec_grad, vec_scale, gains, biases, hidden, gain_old, bias_old, hidden_old, final, grad_in, joint_w, output_w, expand_w, shrink_w,
     *refs,
 ):
     outs, scratch = refs[:31], refs[31:]
@@ -1732,7 +1774,7 @@
     row_outs, column_outs = outs[20:28:2], outs[21:28:2]
     small_moments = outs[28:31]
     masters = (joint_w, output_w, expand_w, shrink_w)
-    wbuf, gbuf, nbuf, cbuf, pbuf, in_sems, out_sems, pass_sems = scratch
+    wbuf, gbuf, nbuf, cbuf, pbuf, vec_now, vec_old, in_sems, out_sems, pass_sems = scratch
     inward = [
         pltpu.make_async_copy(final, pbuf.at[0], pass_sems.at[0]),
         pltpu.make_async_copy(grad_in, pbuf.at[1], pass_sems.at[1]),
@@ -1762,6 +1804,8 @@
     ]
     for cp in loads + inward:
         cp.start()
+    pack_vectors(vec_now, gains, biases, hidden, 0.0)
+    pack_vectors(vec_old, gain_old, bias_old, hidden_old, 1.0)
     columns = jnp.concatenate([lax.rsqrt(rows_new[...]), jnp.zeros((112, 128), F32)], axis=0).T
     stores = []
     for n, (layer, m, b, t, block) in enumerate(pieces):
@@ -1791,7 +1835,8 @@
         new = now - vec_scale[layer] * (grad * lax.rsqrt(moments))
         for out, value in zip((small_grads, small_nexts, small_moments), (grad, new, moments)):
             out[0][layer] = value[0:2, 0:96]
-            out[1][layer] = value[2:8, 0:96]
+            for r in range(6):
+                out[1][r, layer : layer + 1, :] = value[2 + r : 3 + r, 0:96]
             for k in range(3):
                 out[2][layer : layer + 1, 128 * k : 128 * k + 128] = value[8 + k : 9 + k, :]
         for m in range(3):
@@ -1811,7 +1856,7 @@
     vm = pl.BlockSpec(memory_space=pltpu.VMEM)
     V = pltpu.VMEM
     mats = ((2, 96, 2304), (2, 96, 768), (2, 96, 3072), (2, 384, 768))
-    small = ((2, 2, 96), (2, 6, 96), (2, 384))
+    small = ((2, 2, 96), (6, 2, 96), (2, 384))
     stats = ((2, 96), (2, 2304), (2, 96), (2, 768), (2, 96), (2, 3072), (2, 384), (2, 768))
     shapes = (
         [sd((T, D), BF)] * 2 + [sd(s, F32) for s in mats] + [sd(s, F32) for s in small] + [sd(s, F32) for s in mats]
@@ -1821,7 +1866,7 @@
     return pl.pallas_call(
         update_kernel,
         out_shape=shapes,
-        in_specs=[vm] * 8 + [any_spec] * 6,
+        in_specs=[vm] * 12 + [any_spec] * 6,
         out_specs=specs,
         scratch_shapes=[
             V((24, 96, 768), F32),
@@ -1829,6 +1874,8 @@
             V((24, 96, 768), F32),
             V((24, 96, 768), BF),
             V((2, T, D), BF),
+            V((2, 16, 128), F32),
+            V((2, 16, 128), F32),
             pltpu.SemaphoreType.DMA((24,)),
             pltpu.SemaphoreType.DMA((24, 3)),
             pltpu.SemaphoreType.DMA((4,)),
@@ -1861,22 +1908,23 @@
     bias_moments,
     hidden_moments,
 ):
-    row_count, slot_count, features = tokens.shape
-    vecs = pack_vectors(norm_gains, biases, hidden_bias)
+    turned = biases.transpose(1, 0, 2)
+    turned_old = bias_moments.transpose(1, 0, 2)
     (whole, vec, x_saved, j_s, c_s, l_s, n1_s, r1_s, g_s, gp_s, n2_s, r2_s, final, squares) = forward_call(
-        tokens[0], segments, vecs, joint_weight, output_weight, expand_weight, shrink_weight
-    )
-    old = pack_vectors(gain_moments, bias_moments, hidden_moments, 1.0)
-    rows_old = pack_rows(joint_rows, output_rows, expand_rows, shrink_rows)
-    columns_old = jnp.concatenate([joint_columns, output_columns, expand_columns, shrink_columns], axis=1).reshape(2, 9, 768)
+        tokens[0], segments, norm_gains, turned, hidden_bias, joint_weight, output_weight, expand_weight, shrink_weight
+    )
+    vectors = (norm_gains, turned, hidden_bias, gain_moments, turned_old, hidden_moments)
     blocks, grad_in, rows_new, columns_new, column_scale, vec_grad, vec_scale = backward_call(
-        cotangent[0], segments, vec, squares, rows_old, columns_old, vecs, old,
+        cotangent[0], segments, vec, squares, joint_rows, output_rows, expand_rows, shrink_rows,
+        joint_columns, output_columns, expand_columns, shrink_columns, *vectors,
         tokens[0], x_saved, whole, j_s, c_s, l_s, n1_s, r1_s, g_s, gp_s, n2_s, r2_s
     )
-    outs = update_call(
-        blocks, rows_new, columns_new, column_scale, vec_grad, vec_scale, vecs, old, final, grad_in,
+    outs = list(update_call(
+        blocks, rows_new, columns_new, column_scale, vec_grad, vec_scale, *vectors, final, grad_in,
         joint_weight, output_weight, expand_weight, shrink_weight
-    )
+    ))
+    for n in (7, 14, 29):
+        outs[n] = outs[n].transpose(1, 0, 2)
     return (outs[0][None], outs[1][None]) + tuple(outs[2:])
 
 

time: 377 us -> 334 us (0.89)
  Pallas kernels: 358 us -> 328 us
  local copies, waits for them, and re-layouts: 8.81 us -> 0 us
    pallas_call x1, Pallas kernels: 214 us -> 187 us  [backward_call(): pl.pallas_call(backward_kernel, out_shape=[sd((6, 4, 96, 768), BF), sd((T...]
    unnamed x5 -> x0, local copies, waits for them, and re-layouts: 5.26 us -> none
    pallas_call x2, Pallas kernels: 144 us -> 141 us  [the longest x1 127 us: forward_call(): pl.pallas_call(forward_kernel, out_shape=saved, in_specs=[vm] * 5 + [any_...]
where the time goes in v4:
time: 334 us; the launch traced here: 329 us
  Pallas kernels  328 us (98%)
    pallas_call x1, Pallas kernels, backward_call(): pl.pallas_call(backward_kernel, out_shape=[sd((6, 4, 96, 768), BF), sd((T...  187 us
    pallas_call x1, Pallas kernels, forward_call(): pl.pallas_call(forward_kernel, out_shape=saved, in_specs=[vm] * 5 + [any_...  127 us
    pallas_call x1, Pallas kernels, update_call(): pl.pallas_call(update_kernel, out_shape=shapes, in_specs=[vm] * 12 + [any...  14 us

profile of v4, /device:TPU:0, one launch (start us, length us, event | category | flops | bytes accessed | tf_op | source)
XLA Modules:
  0.0 328.5 jit_solution(1805037008980684072)
XLA Ops:
  0.7 126.6 %forward.1 = (bf16[6,4,768,768]{3,2,1,0:T(8,128)(2,1)}, f32[2,16,768]{2,1,0:T(8,128)}, bf16[512,768]{1,0:T(8,128)(2,1)}, bf16[2,3,512,768]{3,2,1,0:T(8,128)(2,1)...) custom-call(bf16[512,768]{1,0:T(8,128)(2,1)} %bitcast.9, ...), custom_call_target="tpu_custom_call" | custom-call | tf_op jit(solution)/shard_map/forward/pallas_call | solution.py:1084
  127.3 187.1 %backward.1 = (bf16[6,4,96,768]{3,2,1,0:T(8,128)(2,1)}, bf16[512,768]{1,0:T(8,128)(2,1)}, f32[16,128]{1,0:T(8,128)}, f32[2,9,768]{2,1,0:T(8,128)}, f32[2,9,768]{...) custom-call(bf16[512,768]{1,0:T(8,128)(2,1)} %bitcast.11, s32[1,512]{1,0:T(1,128)} %seg.3, ...), custom_call_target="tpu_custom_call" | custom-call | tf_op jit(solution)/shard_map/backward/pallas_call | solution.py:1708
  314.3 14.0 %update.1 = (bf16[512,768]{1,0:T(8,128)(2,1)}, bf16[512,768]{1,0:T(8,128)(2,1)}, f32[2,96,2304]{2,1,0:T(8,128)}, f32[2,96,768]{2,1,0:T(8,128)}, f32[2,96,3072]{2...) custom-call(bf16[6,4,96,768]{3,2,1,0:T(8,128)(2,1)} %get-tuple-eleme, ...), custom_call_target="tpu_custom_call" | custom-call | tf_op jit(solution)/shard_map/update/pallas_call | solution.py:1866

commit v5 on v4

--- a/solution.py
+++ b/solution.py
@@ -794,7 +794,7 @@
 ) + (("down", 2.8),)
 
 
-SPREAD = 0.7
+SPREAD = 0.95
 
 
 def pack_vectors(ref, gains, biases, hidden, fill):
@@ -812,7 +812,7 @@
     steps = []
     for i in range(count + 3):
         for lag, kind in enumerate(("xy", "dg", "last", "fin")):
-            if 0 <= i - lag < count:
+            if 0 <= i - lag < count and (kind != "fin" or sum(PARTS[i - lag][1:]) == 96):
                 steps.append((kind, i - lag))
     units = [(layer, name, cost) for layer in range(2) for name, cost in UNIT_TIMES]
     last = {PARTS[k][0]: k for k in range(count)}
@@ -950,10 +950,11 @@
         elif kind == "last":
             gather.last_send(k)
         elif kind == "fin":
-            gather.finish(k)
-            grp, first, count = PARTS[k]
-            if first + count == 96:
-                load(grp).start()
+            grp = PARTS[k][0]
+            for part in range(len(PARTS)):
+                if PARTS[part][0] == grp:
+                    gather.finish(part)
+            load(grp).start()
 
     order = forward_plan()
     pos = 0
@@ -1108,6 +1109,9 @@
 PARTS_OF = {"s0": (0,), "s1": (1,), "s2": (2,), "s3": (3,), "e0": (0, 1), "e1": (2, 3), "q0": (0, 1), "q1": (2, 3)}
 
 
+LINK, LATENCY, STEP, COMPUTE = 3.2, 1.5, 0.4, 1.0
+
+
 def backward_plan():
     now, xy_free, z_free, core_free = 0.0, 0.0, 0.0, 0.0
     pending, order, summed = [], [], set()
@@ -1115,25 +1119,25 @@
     def emit(entry):
         nonlocal now, xy_free, z_free
         ready, name, t, zz = entry
-        now = max(now, ready) + 0.4
+        now = max(now, ready) + STEP
         order.append((name, t, zz))
         if name == "xy1":
-            xy_free = max(xy_free, now) + 3.2
-            pending.append((xy_free + 1.5, "xy2", t, zz))
+            xy_free = max(xy_free, now) + LINK
+            pending.append((xy_free + LATENCY, "xy2", t, zz))
         elif name == "xy2":
-            xy_free = max(xy_free, now) + 1.6
-            pending.append((xy_free + 1.5, "z", t, zz))
+            xy_free = max(xy_free, now) + LINK / 2
+            pending.append((xy_free + LATENCY, "z", t, zz))
         elif name == "z":
-            z_free = max(z_free, now) + 3.2
+            z_free = max(z_free, now) + LINK
             if sum(1 for o in order if o[0] == "z" and o[1] == t) == 4:
-                pending.append((z_free + 1.5, "sum", t, 0))
+                pending.append((z_free + LATENCY, "sum", t, 0))
         elif name == "sum":
             summed.add(t)
-            xy_free = max(xy_free, now) + 3.2
-            pending.append((xy_free + 1.5, "ag", t, 0))
+            xy_free = max(xy_free, now) + LINK
+            pending.append((xy_free + LATENCY, "ag", t, 0))
         elif name == "ag":
-            xy_free = max(xy_free, now) + 1.6
-            pending.append((xy_free + 1.5, "fin", t, 0))
+            xy_free = max(xy_free, now) + LINK / 2
+            pending.append((xy_free + LATENCY, "fin", t, 0))
         elif name == "fin":
             pending.append((now, "stat", t, 0))
         elif name == "stat":
@@ -1180,10 +1184,10 @@
             for zz in PARTS_OF.get(name, ()):
                 force("xy1", t - 1, zz)
             order.append(("run", layer, name))
-            now += cost
+            now += cost * COMPUTE
             for zz in PARTS_OF.get(name, ()):
                 core_free = max(core_free, now) + 1.0
-                pending.append((core_free + 1.5, "xy1", 3 * (1 - layer) + GROUP_OF[name[0]], zz))
+                pending.append((core_free + LATENCY, "xy1", 3 * (1 - layer) + GROUP_OF[name[0]], zz))
     pending.append((now, "vec", 0, 0))
     while step(1e9):
         pass
@@ -1774,7 +1778,7 @@
     row_outs, column_outs = outs[20:28:2], outs[21:28:2]
     small_moments = outs[28:31]
     masters = (joint_w, output_w, expand_w, shrink_w)
-    wbuf, gbuf, nbuf, cbuf, pbuf, vec_now, vec_old, in_sems, out_sems, pass_sems = scratch
+    wbuf, gbuf, nbuf, cbuf, pbuf, fbuf, vec_now, vec_old, in_sems, out_sems, pass_sems = scratch
     inward = [
         pltpu.make_async_copy(final, pbuf.at[0], pass_sems.at[0]),
         pltpu.make_async_copy(grad_in, pbuf.at[1], pass_sems.at[1]),
@@ -1802,7 +1806,14 @@
         pltpu.make_async_copy(part(masters[m], layer, m, b), wbuf.at[n], in_sems.at[n])
         for n, (layer, m, b, t, block) in enumerate(pieces)
     ]
-    for cp in loads + inward:
+    blocks = [
+        pltpu.make_async_copy(fin.at[t, block], fbuf.at[n], in_sems.at[24 + n])
+        for n, (layer, m, b, t, block) in enumerate(pieces)
+    ]
+    for one, two in zip(blocks, loads):
+        one.start()
+        two.start()
+    for cp in inward:
         cp.start()
     pack_vectors(vec_now, gains, biases, hidden, 0.0)
     pack_vectors(vec_old, gain_old, bias_old, hidden_old, 1.0)
@@ -1819,8 +1830,9 @@
             left = jnp.concatenate([columns[:, 6 * layer + 3 + k : 6 * layer + 4 + k] for k in range(3)], axis=0)
             left = left[96 * b : 96 * b + 96]
         j = (0, 3, 4, 8)[m] + (b if m != 3 else 0)
-        grad = fin[t, block].astype(F32) * ROOT_SCALE
+        blocks[n].wait()
         loads[n].wait()
+        grad = fbuf[n].astype(F32) * ROOT_SCALE
         new = wbuf[n] - grad * left * column_scale[layer, j : j + 1, :]
         gbuf[n] = grad
         nbuf[n] = new
@@ -1866,7 +1878,7 @@
     return pl.pallas_call(
         update_kernel,
         out_shape=shapes,
-        in_specs=[vm] * 12 + [any_spec] * 6,
+        in_specs=[any_spec] + [vm] * 11 + [any_spec] * 6,
         out_specs=specs,
         scratch_shapes=[
             V((24, 96, 768), F32),
@@ -1874,9 +1886,10 @@
             V((24, 96, 768), F32),
             V((24, 96, 768), BF),
             V((2, T, D), BF),
+            V((24, 96, 768), BF),
             V((2, 16, 128), F32),
             V((2, 16, 128), F32),
-            pltpu.SemaphoreType.DMA((24,)),
+            pltpu.SemaphoreType.DMA((48,)),
             pltpu.SemaphoreType.DMA((24, 3)),
             pltpu.SemaphoreType.DMA((4,)),
         ],

time: 334 us -> 330 us (0.988)
  Pallas kernels: 328 us -> 324 us
    pallas_call x1, Pallas kernels: 127 us -> 123 us  [forward_call(): pl.pallas_call(forward_kernel, out_shape=saved, in_specs=[vm] * 5 + [any_...]
where the time goes in v5:
time: 330 us; the launch traced here: 325 us
  Pallas kernels  324 us (98%)
    pallas_call x1, Pallas kernels, backward_call(): pl.pallas_call(backward_kernel, out_shape=[sd((6, 4, 96, 768), BF), sd((T...  187 us
    pallas_call x1, Pallas kernels, forward_call(): pl.pallas_call(forward_kernel, out_shape=saved, in_specs=[vm] * 5 + [any_...  123 us
    pallas_call x1, Pallas kernels, update_call(): pl.pallas_call(update_kernel, out_shape=shapes, in_specs=[any_spec] + [vm...  14.1 us

profile of v5, /device:TPU:0, one launch (start us, length us, event | category | flops | bytes accessed | tf_op | source)
XLA Modules:
  0.0 324.6 jit_solution(15818496084074866012)
XLA Ops:
  0.7 122.9 %forward.1 = (bf16[6,4,768,768]{3,2,1,0:T(8,128)(2,1)}, f32[2,16,768]{2,1,0:T(8,128)}, bf16[512,768]{1,0:T(8,128)(2,1)}, bf16[2,3,512,768]{3,2,1,0:T(8,128)(2,1)...) custom-call(bf16[512,768]{1,0:T(8,128)(2,1)} %bitcast.9, ...), custom_call_target="tpu_custom_call" | custom-call | tf_op jit(solution)/shard_map/forward/pallas_call | solution.py:1085
  123.6 186.7 %backward.1 = (bf16[6,4,96,768]{3,2,1,0:T(8,128)(2,1)}, bf16[512,768]{1,0:T(8,128)(2,1)}, f32[16,128]{1,0:T(8,128)}, f32[2,9,768]{2,1,0:T(8,128)}, f32[2,9,768]{...) custom-call(bf16[512,768]{1,0:T(8,128)(2,1)} %bitcast.11, s32[1,512]{1,0:T(1,128)} %seg.3, ...), custom_call_target="tpu_custom_call" | custom-call | tf_op jit(solution)/shard_map/backward/pallas_call | solution.py:1712
  310.3 14.1 %update.1 = (bf16[512,768]{1,0:T(8,128)(2,1)}, bf16[512,768]{1,0:T(8,128)(2,1)}, f32[2,96,2304]{2,1,0:T(8,128)}, f32[2,96,768]{2,1,0:T(8,128)}, f32[2,96,3072]{2...) custom-call(bf16[6,4,96,768]{3,2,1,0:T(8,128)(2,1)} %get-tuple-eleme, ...), custom_call_target="tpu_custom_call" | custom-call | tf_op jit(solution)/shard_map/update/pallas_call | solution.py:1878
